TPU v7x, 32 devices: a whole 2x2x4 slice. The times are simulated.
32 devices in a mesh: mod: 2 (over x), dp: 16 (over z, y, core).
Axes of the slice: x: 2, y: 2, z: 4, core: 2. Of those that a mesh axis runs over, the one named last changes fastest.
Arguments:
- stream_in: float32 [2, 16, 577, 768], P('mod', 'dp'), may hold values from -6 to 6
- cotangent: float32 [2, 16, 577, 768], P('mod', 'dp'), may hold values from -6 to 6
- patch_count: int32 [16], P('dp'), may hold values from 197 to 577, as said below
- pos_index: int32 [16, 577], P('dp'), may hold values from 0 to 576, as said below
- attn_blocks: float32 [256, 96, 96], P(('mod', 'dp'))
- attn_left: float32 [256, 96, 96], P(('mod', 'dp')), as said below
- attn_right: float32 [256, 96, 96], P(('mod', 'dp')), as said below
- ffn_blocks: float32 [2, 512, 96, 96], P('mod', 'dp')
- ffn_left: float32 [2, 512, 96, 96], P('mod', 'dp'), as said below
- ffn_right: float32 [2, 512, 96, 96], P('mod', 'dp'), as said below
- vectors: float32 [13, 768], replicated
- vectors_mom: float32 [13, 768], replicated, may hold values from -28 to 28
- ffn_bias: float32 [2, 3072], replicated, may hold values from -4 to 4
- ffn_bias_mom: float32 [2, 3072], replicated, may hold values from -16 to 16
- pos_table: float32 [577, 768], replicated, may hold values from -6 to 6
- pos_mom: float32 [577, 768], replicated, may hold values from -4 to 4
Outputs:
- stream_out: float32 [2, 16, 577, 768], P('mod', 'dp')
- stream_grad: float32 [2, 16, 577, 768], P('mod', 'dp')
- attn_grad: float32 [256, 96, 96], P(('mod', 'dp'))
- attn_left_new: float32 [256, 96, 96], P(('mod', 'dp'))
- attn_right_new: float32 [256, 96, 96], P(('mod', 'dp'))
- attn_new: float32 [256, 96, 96], P(('mod', 'dp'))
- ffn_grad: float32 [2, 512, 96, 96], P('mod', 'dp')
- ffn_left_new: float32 [2, 512, 96, 96], P('mod', 'dp')
- ffn_right_new: float32 [2, 512, 96, 96], P('mod', 'dp')
- ffn_new: float32 [2, 512, 96, 96], P('mod', 'dp')
- vectors_mom_new: float32 [13, 768], replicated
- vectors_new: float32 [13, 768], replicated
- ffn_bias_mom_new: float32 [2, 3072], replicated
- ffn_bias_new: float32 [2, 3072], replicated
- pos_mom_new: float32 [577, 768], replicated
- pos_new: float32 [577, 768], replicated
Inputs may be any that keep to these rules, and one draw needn't show every extreme that they name: `patch_count`: each item holds 197 or 577 image patches; both numbers occur in every draw. `pos_index`: an item of 577 patches has slot s at row s; for an item of 197 patches slot 0 is at row 0 and the patch in row i, column j of its 14 x 14 grid at row 1 + 24 * a + b, with a = (i * 23 + 13 // 2) // 13 and b likewise of j; unused slots hold 0. `attn_left`: every block is symmetric positive definite. `attn_right`: every block is symmetric positive definite. `ffn_left`: every block is symmetric positive definite. `ffn_right`: every block is symmetric positive definite.
All inputs are finite; a program needn't handle non-finite values.
Results may differ from a plain program's by a relative error of at most 0.011.
The roundings to bfloat16 on the way count: a program that leaves them out, or rounds other values in their place, can miss the bound.
Values may be sent and summed in bfloat16 or wider, within the bound.
No kernel may reach another device: no remote copies, remote signals or barrier semaphores. Data moves between devices by JAX's collectives and lax.ppermute only.
A program may use at most 256 MiB of HBM per device.

v0:
```python
import math

import jax
import jax.numpy as jnp
from jax import lax
from jax.sharding import PartitionSpec as P

HEADS = 12
TEXT = 64
NEWTON = 6


HIGHEST = lax.Precision.HIGHEST
norm_eps = 1e-05
stat_decay = 0.5
matrix_rate = 0.25
moment_keep = 0.9


def from_root(shard, axis, root):
    mine = lax.axis_index(axis) == root
    return lax.psum(jnp.where(mine, shard, jnp.zeros_like(shard)), axis)


def gelu_exact(values):
    return jax.nn.gelu(values, approximate=False)


def row_contract(left_rows, right_rows):
    return lax.dot_general(
        left_rows, right_rows, (((0,), (0,)), ((), ())), preferred_element_type=jnp.float32
    )


def times_transposed(rows, weight):
    return lax.dot_general(
        rows, weight, (((1,), (1,)), ((), ())), preferred_element_type=jnp.float32
    )


def blocks_to_matrix(blocks, row_blocks, col_blocks):
    block_size = blocks.shape[-1]
    leading = blocks.shape[:-3]
    shaped = blocks.reshape(leading + (row_blocks, col_blocks, block_size, block_size))
    moved = jnp.swapaxes(shaped, -3, -2)
    return moved.reshape(leading + (row_blocks * block_size, col_blocks * block_size))


def matrix_to_blocks(matrix, block_size):
    leading = matrix.shape[:-2]
    row_blocks = matrix.shape[-2] // block_size
    col_blocks = matrix.shape[-1] // block_size
    shaped = matrix.reshape(leading + (row_blocks, block_size, col_blocks, block_size))
    moved = jnp.swapaxes(shaped, -3, -2)
    return moved.reshape(leading + (row_blocks * col_blocks, block_size, block_size))


def norm_forward(values, norm_gain, norm_bias):
    row_mean = jnp.mean(values, axis=-1, keepdims=True)
    centred = values - row_mean
    spread = jnp.mean(centred * centred, axis=-1, keepdims=True)
    inv_std = lax.rsqrt(spread + norm_eps)
    normal_rows = centred * inv_std
    return (normal_rows * norm_gain + norm_bias, normal_rows, inv_std)


def norm_backward(grad_out, normal_rows, inv_std, norm_gain):
    grad_norm = grad_out * norm_gain
    mean_grad = jnp.mean(grad_norm, axis=-1, keepdims=True)
    mean_proj = jnp.mean(grad_norm * normal_rows, axis=-1, keepdims=True)
    grad_in = inv_std * (grad_norm - mean_grad - normal_rows * mean_proj)
    grad_gain = jnp.sum(grad_out * normal_rows, axis=(0, 1))
    grad_shift = jnp.sum(grad_out, axis=(0, 1))
    return (grad_in, grad_gain, grad_shift)


def attend_forward(query_heads, key_heads, value_heads, key_mask, score_scale):
    scores = (
        jnp.einsum("qhd,khd->hqk", query_heads, key_heads, preferred_element_type=jnp.float32)
        * score_scale
    )
    scores = jnp.where(key_mask[None, None, :], scores, -jnp.inf)
    top_score = jnp.max(scores, axis=-1, keepdims=True)
    log_total = top_score + jnp.log(jnp.sum(jnp.exp(scores - top_score), axis=-1, keepdims=True))
    attn_probs = jnp.exp(scores - log_total).astype(jnp.bfloat16)
    context = jnp.einsum(
        "hqk,khd->qhd", attn_probs, value_heads, preferred_element_type=jnp.float32
    )
    return (context, log_total)


def attend_backward(
    query_heads, key_heads, value_heads, key_mask, score_scale, log_total, grad_heads
):
    scores = (
        jnp.einsum("qhd,khd->hqk", query_heads, key_heads, preferred_element_type=jnp.float32)
        * score_scale
    )
    scores = jnp.where(key_mask[None, None, :], scores, -jnp.inf)
    attn_probs = jnp.exp(scores - log_total)
    grad_probs = jnp.einsum(
        "qhd,khd->hqk", grad_heads, value_heads, preferred_element_type=jnp.float32
    )
    row_dot = jnp.sum(attn_probs * grad_probs, axis=-1, keepdims=True)
    grad_scores = (attn_probs * (grad_probs - row_dot)).astype(jnp.bfloat16)
    grad_query = (
        jnp.einsum("hqk,khd->qhd", grad_scores, key_heads, preferred_element_type=jnp.float32)
        * score_scale
    )
    grad_key = (
        jnp.einsum("hqk,qhd->khd", grad_scores, query_heads, preferred_element_type=jnp.float32)
        * score_scale
    )
    grad_value = jnp.einsum(
        "hqk,qhd->khd",
        attn_probs.astype(jnp.bfloat16),
        grad_heads,
        preferred_element_type=jnp.float32,
    )
    return (grad_query, grad_key, grad_value)


def inverse_root(stats):
    identity = jnp.eye(stats.shape[-1], dtype=stats.dtype)
    norm_value = jnp.sqrt(jnp.sum(stats * stats, axis=(-2, -1), keepdims=True))
    matrix = stats / norm_value
    factor = identity * norm_value ** (-0.25)
    for iteration in range(NEWTON):
        step_mat = (5.0 * identity - matrix) * 0.25
        square = jnp.einsum("bij,bjk->bik", step_mat, step_mat, precision=HIGHEST)
        factor = jnp.einsum("bij,bjk->bik", factor, step_mat, precision=HIGHEST)
        fourth = jnp.einsum("bij,bjk->bik", square, square, precision=HIGHEST)
        matrix = jnp.einsum("bij,bjk->bik", fourth, matrix, precision=HIGHEST)
    return factor


def shampoo_update(grads, lefts, rights, weights):
    left_new = stat_decay * lefts + (1.0 - stat_decay) * jnp.einsum(
        "bij,bkj->bik", grads, grads, precision=HIGHEST
    )
    right_new = stat_decay * rights + (1.0 - stat_decay) * jnp.einsum(
        "bji,bjk->bik", grads, grads, precision=HIGHEST
    )
    left_root = inverse_root(left_new)
    right_root = inverse_root(right_new)
    update = jnp.einsum(
        "bij,bjk->bik",
        jnp.einsum("bij,bjk->bik", left_root, grads, precision=HIGHEST),
        right_root,
        precision=HIGHEST,
    )
    return (left_new, right_new, weights - matrix_rate * update)


def local(
    stream_in,
    cotangent,
    patch_count,
    pos_index,
    attn_blocks,
    attn_left,
    attn_right,
    ffn_blocks,
    ffn_left,
    ffn_right,
    vectors,
    vectors_mom,
    ffn_bias,
    ffn_bias_mom,
    pos_table,
    pos_mom,
):
    block_size = attn_blocks.shape[-1]
    model_width = vectors.shape[1]
    hidden_units = ffn_bias.shape[1]
    item_count = stream_in.shape[1]
    slot_count = stream_in.shape[2]
    text_len = TEXT
    head_count = HEADS
    head_dim = model_width // head_count
    row_total = item_count * slot_count
    row_blocks = model_width // block_size
    col_blocks = hidden_units // block_size
    split_at = row_blocks * col_blocks
    score_scale = head_dim ** (-0.5)
    attn_all = lax.all_gather(attn_blocks.astype(jnp.bfloat16), ("mod", "dp"), axis=0, tiled=True)
    attn_mats = blocks_to_matrix(
        attn_all.reshape(4, row_blocks * row_blocks, block_size, block_size), row_blocks, row_blocks
    )
    ffn_all = lax.all_gather(ffn_blocks.astype(jnp.bfloat16), "dp", axis=1, tiled=True)[0]
    up_mat = blocks_to_matrix(ffn_all[:split_at], row_blocks, col_blocks)
    down_mat = blocks_to_matrix(ffn_all[split_at:], col_blocks, row_blocks)
    w_qkv = jnp.concatenate([attn_mats[0], attn_mats[1], attn_mats[2]], axis=1)
    w_out = attn_mats[3]
    modality = lax.axis_index("mod")
    is_text = modality == 1
    image_flag = (1 - modality).astype(jnp.float32)
    own_vec = lax.dynamic_slice_in_dim(vectors, 3 + 5 * modality, 5, 0)
    own_up_bias = lax.dynamic_index_in_dim(ffn_bias, modality, 0, keepdims=False)
    inputs = stream_in[0]
    image_valid = jnp.arange(slot_count)[None, :] < patch_count[:, None]
    keep_rows = jnp.logical_or(is_text, image_valid).astype(jnp.float32)[:, :, None]
    hidden = inputs + image_flag * jnp.take(pos_table, pos_index, axis=0)
    first_normed, first_rows, first_scale = norm_forward(hidden, own_vec[0], own_vec[1])
    first_b = first_normed.reshape(row_total, model_width).astype(jnp.bfloat16)
    qkv_bias = jnp.concatenate([vectors[0], jnp.zeros_like(vectors[0]), vectors[1]])
    projected = (jnp.dot(first_b, w_qkv, preferred_element_type=jnp.float32) + qkv_bias).astype(
        jnp.bfloat16
    )
    projected = projected.reshape(item_count, slot_count, 3 * model_width)
    queries_b = projected[:, :, :model_width]
    own_kv = projected[:, :, model_width:]
    mono_mask = jnp.ones((slot_count - text_len,), jnp.bool_)

    def item_setup(own_pairs, image_pairs, text_pairs, item_valid):
        joint_pairs = jnp.concatenate([image_pairs, text_pairs], axis=0)
        joint_mask = jnp.concatenate([item_valid, jnp.ones((text_len,), jnp.bool_)])
        joint_keys = joint_pairs[:, :model_width].reshape(-1, head_count, head_dim)
        joint_values = joint_pairs[:, model_width:].reshape(-1, head_count, head_dim)
        mono_keys = own_pairs[text_len:, :model_width].reshape(-1, head_count, head_dim)
        mono_values = own_pairs[text_len:, model_width:].reshape(-1, head_count, head_dim)
        return (joint_keys, joint_values, joint_mask, mono_keys, mono_values)

    image_kv = from_root(own_kv, "mod", 0)
    pair_kv = from_root(own_kv[:, :text_len], "mod", 1)

    def item_attention(item):
        own_query, own_pairs, image_pairs, text_pairs, item_valid = item
        joint_keys, joint_values, joint_mask, mono_keys, mono_values = item_setup(
            own_pairs, image_pairs, text_pairs, item_valid
        )
        query_heads = own_query.reshape(slot_count, head_count, head_dim)

        def image_side(unused):
            return attend_forward(query_heads, joint_keys, joint_values, joint_mask, score_scale)

        def text_side(unused):
            pair_context, pair_total = attend_forward(
                query_heads[:text_len], joint_keys, joint_values, joint_mask, score_scale
            )
            mono_context, mono_total = attend_forward(
                query_heads[text_len:], mono_keys, mono_values, mono_mask, score_scale
            )
            return (
                jnp.concatenate([pair_context, mono_context], axis=0),
                jnp.concatenate([pair_total, mono_total], axis=1),
            )

        return lax.cond(is_text, text_side, image_side, 0)

    context, log_totals = lax.map(
        item_attention, (queries_b, own_kv, image_kv, pair_kv, image_valid)
    )
    context_b = context.reshape(row_total, model_width).astype(jnp.bfloat16)
    attn_out = jnp.dot(context_b, w_out, preferred_element_type=jnp.float32) + vectors[2]
    middle = hidden + attn_out.reshape(hidden.shape)
    second_normed, second_rows, second_scale = norm_forward(middle, own_vec[2], own_vec[3])
    second_b = second_normed.reshape(row_total, model_width).astype(jnp.bfloat16)
    pre_act = jnp.dot(second_b, up_mat, preferred_element_type=jnp.float32) + own_up_bias
    activated, gelu_pull = jax.vjp(gelu_exact, pre_act)
    activated_b = activated.astype(jnp.bfloat16)
    branch = jnp.dot(activated_b, down_mat, preferred_element_type=jnp.float32) + own_vec[4]
    stream_out = keep_rows * (middle + branch.reshape(middle.shape))
    grad_res = keep_rows * cotangent[0]
    grad_branch = grad_res.reshape(row_total, model_width).astype(jnp.bfloat16)
    grad_down_bias = jnp.sum(grad_branch.astype(jnp.float32), axis=0)
    grad_down = row_contract(activated_b, grad_branch)
    grad_pre = gelu_pull(times_transposed(grad_branch, down_mat))[0].astype(jnp.bfloat16)
    grad_up_bias = jnp.sum(grad_pre.astype(jnp.float32), axis=0)
    grad_up = row_contract(second_b, grad_pre)
    grad_second = times_transposed(grad_pre, up_mat).reshape(middle.shape)
    grad_mid_norm, grad_late_gain, grad_late_shift = norm_backward(
        grad_second, second_rows, second_scale, own_vec[2]
    )
    grad_middle = grad_res + grad_mid_norm
    grad_attn_out = grad_middle.reshape(row_total, model_width).astype(jnp.bfloat16)
    grad_out_bias = jnp.sum(grad_attn_out.astype(jnp.float32), axis=0)
    grad_wout = row_contract(context_b, grad_attn_out)
    grad_context = (
        times_transposed(grad_attn_out, w_out)
        .astype(jnp.bfloat16)
        .reshape(item_count, slot_count, model_width)
    )

    def item_attention_grad(item):
        own_query, own_pairs, image_pairs, text_pairs, item_valid, item_total, item_grad = item
        joint_keys, joint_values, joint_mask, mono_keys, mono_values = item_setup(
            own_pairs, image_pairs, text_pairs, item_valid
        )
        query_heads = own_query.reshape(slot_count, head_count, head_dim)
        grad_heads = item_grad.reshape(slot_count, head_count, head_dim)

        def split_joint(grad_keys, grad_values):
            flat_keys = grad_keys.reshape(-1, model_width)
            flat_values = grad_values.reshape(-1, model_width)
            image_part = jnp.concatenate([flat_keys[:slot_count], flat_values[:slot_count]], axis=1)
            text_part = jnp.concatenate([flat_keys[slot_count:], flat_values[slot_count:]], axis=1)
            return (image_part, text_part)

        def image_side(unused):
            grad_q, grad_k, grad_v = attend_backward(
                query_heads,
                joint_keys,
                joint_values,
                joint_mask,
                score_scale,
                item_total,
                grad_heads,
            )
            image_part, text_part = split_joint(grad_k, grad_v)
            padded = jnp.pad(text_part, ((0, slot_count - text_len), (0, 0)))
            return (grad_q.reshape(slot_count, model_width), image_part, padded)

        def text_side(unused):
            pair_q, pair_k, pair_v = attend_backward(
                query_heads[:text_len],
                joint_keys,
                joint_values,
                joint_mask,
                score_scale,
                item_total[:, :text_len],
                grad_heads[:text_len],
            )
            mono_q, mono_k, mono_v = attend_backward(
                query_heads[text_len:],
                mono_keys,
                mono_values,
                mono_mask,
                score_scale,
                item_total[:, text_len:],
                grad_heads[text_len:],
            )
            image_part, text_part = split_joint(pair_k, pair_v)
            mono_part = jnp.concatenate(
                [mono_k.reshape(-1, model_width), mono_v.reshape(-1, model_width)], axis=1
            )
            grad_q = jnp.concatenate([pair_q, mono_q], axis=0).reshape(slot_count, model_width)
            return (grad_q, image_part, jnp.concatenate([text_part, mono_part], axis=0))

        return lax.cond(is_text, text_side, image_side, 0)

    grad_query, grad_image_kv, grad_text_kv = lax.map(
        item_attention_grad,
        (queries_b, own_kv, image_kv, pair_kv, image_valid, log_totals, grad_context),
    )
    own_share = jnp.where(is_text, grad_text_kv, grad_image_kv)
    from_text = from_root(grad_image_kv, "mod", 1)
    from_image = from_root(grad_text_kv[:, :text_len], "mod", 0)
    padded_image = jnp.pad(from_image, ((0, 0), (0, slot_count - text_len), (0, 0)))
    own_kv_grad = own_share + jnp.where(is_text, padded_image, from_text)
    grad_full = jnp.concatenate([grad_query, own_kv_grad], axis=2)
    grad_qkv = grad_full.reshape(row_total, 3 * model_width).astype(jnp.bfloat16)
    grad_bias_q = jnp.sum(grad_qkv[:, :model_width].astype(jnp.float32), axis=0)
    grad_bias_v = jnp.sum(grad_qkv[:, 2 * model_width :].astype(jnp.float32), axis=0)
    grad_wqkv = row_contract(first_b, grad_qkv)
    grad_first = times_transposed(grad_qkv, w_qkv).reshape(hidden.shape)
    grad_hidden_norm, grad_early_gain, grad_early_shift = norm_backward(
        grad_first, first_rows, first_scale, own_vec[0]
    )
    grad_hidden = grad_middle + grad_hidden_norm
    grad_pos = jax.ops.segment_sum(
        (image_flag * grad_hidden).reshape(row_total, model_width),
        pos_index.reshape(row_total),
        num_segments=slot_count,
    )
    attn_stack = jnp.stack(
        [
            grad_wqkv[:, :model_width],
            grad_wqkv[:, model_width : 2 * model_width],
            grad_wqkv[:, 2 * model_width :],
            grad_wout,
        ]
    )
    attn_full = matrix_to_blocks(attn_stack, block_size).reshape(-1, block_size, block_size)
    attn_grad = lax.psum_scatter(attn_full, ("mod", "dp"), scatter_dimension=0, tiled=True)
    ffn_full = jnp.concatenate(
        [matrix_to_blocks(grad_up, block_size), matrix_to_blocks(grad_down, block_size)], axis=0
    )[None]
    ffn_grad = lax.psum_scatter(ffn_full, "dp", scatter_dimension=1, tiled=True)
    selector = (jnp.arange(2) == modality).astype(jnp.float32)
    own_rows = jnp.stack(
        [grad_early_gain, grad_early_shift, grad_late_gain, grad_late_shift, grad_down_bias]
    )
    shared_rows = jnp.stack([grad_bias_q, grad_bias_v, grad_out_bias])
    vector_grad = jnp.concatenate(
        [shared_rows, (selector[:, None, None] * own_rows[None]).reshape(10, model_width)], axis=0
    )
    up_bias_grad = selector[:, None] * grad_up_bias[None]
    vector_sum, up_bias_sum, pos_sum = lax.psum(
        (vector_grad, up_bias_grad, grad_pos), ("mod", "dp")
    )
    items_total = item_count * lax.axis_size("dp")
    vector_rate = 0.3 / math.sqrt(items_total * slot_count)
    pos_rate = 0.5 / math.sqrt(items_total)
    vectors_mom_new = moment_keep * vectors_mom + vector_sum
    vectors_new = vectors - vector_rate * vectors_mom_new
    ffn_bias_mom_new = moment_keep * ffn_bias_mom + up_bias_sum
    ffn_bias_new = ffn_bias - vector_rate * ffn_bias_mom_new
    pos_mom_new = moment_keep * pos_mom + pos_sum
    pos_new = pos_table - pos_rate * pos_mom_new
    attn_left_new, attn_right_new, attn_new = shampoo_update(
        attn_grad, attn_left, attn_right, attn_blocks
    )
    flat_shape = (-1, block_size, block_size)
    ffn_left_flat, ffn_right_flat, ffn_new_flat = shampoo_update(
        ffn_grad.reshape(flat_shape),
        ffn_left.reshape(flat_shape),
        ffn_right.reshape(flat_shape),
        ffn_blocks.reshape(flat_shape),
    )
    return (
        stream_out[None],
        grad_hidden[None],
        attn_grad,
        attn_left_new,
        attn_right_new,
        attn_new,
        ffn_grad,
        ffn_left_flat.reshape(ffn_blocks.shape),
        ffn_right_flat.reshape(ffn_blocks.shape),
        ffn_new_flat.reshape(ffn_blocks.shape),
        vectors_mom_new,
        vectors_new,
        ffn_bias_mom_new,
        ffn_bias_new,
        pos_mom_new,
        pos_new,
    )


def solution(mesh):
    return jax.shard_map(
        local,
        mesh=mesh,
        in_specs=(
            P("mod", "dp", None, None),
            P("mod", "dp", None, None),
            P("dp"),
            P("dp", None),
            P(("mod", "dp"), None, None),
            P(("mod", "dp"), None, None),
            P(("mod", "dp"), None, None),
            P("mod", "dp", None, None),
            P("mod", "dp", None, None),
            P("mod", "dp", None, None),
            P(),
            P(),
            P(),
            P(),
            P(),
            P(),
        ),
        out_specs=(
            P("mod", "dp", None, None),
            P("mod", "dp", None, None),
            P(("mod", "dp"), None, None),
            P(("mod", "dp"), None, None),
            P(("mod", "dp"), None, None),
            P(("mod", "dp"), None, None),
            P("mod", "dp", None, None),
            P("mod", "dp", None, None),
            P("mod", "dp", None, None),
            P("mod", "dp", None, None),
            P(),
            P(),
            P(),
            P(),
            P(),
            P(),
        ),
        check_vma=False,
    )
```

profile of v0, /device:TPU:0, one launch (start us, length us, event | category | flops | bytes accessed | tf_op | source)
XLA Modules:
  0.0 1174.9 jit_solution(12668709446242699518)
XLA Ops:
  21.0 63.6 %all-gather.3.cloned.1.call-done = bf16[256,96,96]{2,1,0:T(8,128)(2,1)} async-done(((bf16[8,96,96]{2,1,0:T(8,128)(2,1)}), bf16[256,96,96]{2,1,0:T(8,128)(2,1)}) %all-gather.3.cloned.1.call-update) | async-done | bytes 4718608 | tf_op jit(solution)/shard_map/all_gather | solution.py:186
  124.2 46.2 %all-reduce.14.cloned.1.call-done = (bf16[577,1536]{1,0:T(8,128)(2,1)}, bf16[64,1536]{1,0:T(8,128)(2,1)}) async-done(((bf16[577,1536]{1,0:T(8,128)(2,1)}, bf16[64,1536]{1,0:T(8,128)(2,1)}), (bf16[577,1536]{1,0:T(8,128)(2,1)}, bf16[64,1536]{1,0:T(8,128)(2,1)})) %all-reduce.14.cloned.1.call-update) | async-done | bytes 1969168 | tf_op jit(solution)/shard_map/psum | solution.py:22
  176.0 37.8 %conditional.2 = (f32[12,577,1]{1,0,2:T(8,128)S(1)}, bf16[577,768]{0,1:T(8,128)(2,1)S(1)}) conditional(s32[]{:T(128)} %convert_element_type.173, (pred[641]{0:T(1024)(128)(4,1)S(1)}, bf16[577,12,64]{0,2,1:T(8,128)(2,1)S(1)}, bf16[641,12,64]{0,2,1:T(8,128)(2,1)S(1)}, bf16[641,12,64]{0,2,1:T(8,128)(2,1)}) %tuple.138, (pred[641]{0:T(1024)(128)(4,1)S(1)}, ...), branch_computations={%region_4.7_spmd, %region_7.12_spmd} | conditional | flops 1185458048 | bytes 57249260 | solution.py:249
  176.0 9.1 fusion
  185.1 10.9 exponential_reduce_fusion
  196.0 9.5 fusion.3
  218.7 9.1 fusion.322
  233.0 12.1 %reshape.701 = bf16[768,3072]{1,0:T(8,128)(2,1)} reshape(bf16[8,96,32,96]{3,2,1,0:T(8,128)(2,1)} %bitcast.470) | data formatting | bytes 9437184 | tf_op jit(solution)/shard_map/reshape | solution.py:46
  253.5 10.8 reshape.703
  270.2 22.6 %convert_reduce_fusion = (f32[3072]{0:T(1024)}, bf16[577,3072]{1,0:T(8,128)(2,1)S(1)}, f32[577,3072]{1,0:T(8,128)}, f32[577,3072]{1,0:T(8,128)}) fusion(f32[577,3072]{1,0:T(8,128)S(1)} %fusion.315, f32[3072]{0:T(1024)S(1)} %bitcast.513, bf16[3072,768]{1,0:T(8,128)(2,1)S(1)} %copy-done.35, bf16[1,577,1,1,1,1,768]{6,0,5,4,3,2,1:T(2,128)(2,1)S(1)} %copy-done.40), kind=kOutput, calls=%fused_computation.111 | convolution fusion | flops 2855565312 | bytes 30445056 | tf_op jit(solution)/shard_map/dot_general | solution.py:36
  306.0 84.6 %conditional.3 = (f32[577,1536]{0,1:T(8,128)}, f32[577,1536]{0,1:T(8,128)}, f32[1,64,1536]{1,2,0:T(8,128)S(1)}, bf16[1,577,768]{1,2,0:T(8,128)(2,1)}, bf16[577,768]{0,1:T(8,128)(2,1)S(1)}) conditional(s32[]{:T(128)} %convert_element_type.173, (pred[641]{0:T(1024)(128)(4,1)S(1)}, bf16[577,12,64]{0,2,1:T(8,128)(2,1)S(1)}, ...), branch_computations={%region_16.18_spmd, %region_18.21_spmd} | conditional | flops 2912879104 | bytes 272373088 | solution.py:340
  306.0 8.5 fusion.331
  314.5 9.1 fusion.29
  325.8 14.1 %multiply_reduce_fusion.1 = (f32[12,577]{1,0:T(8,128)S(1)}, f32[12,577,641]{1,2,0:T(8,128)}) fusion(f32[12,577,641]{1,2,0:T(8,128)} %fusion.331, f32[12,577]{1,0:T(8,128)S(1)} %bitcast.510, pred[641]{0:T(1024)(128)(4,1)S(1)} %get-tuple-element.112, bf16[577,12,64]{0,2,1:T(8,128)(2,1)S(1)} %copy-done.3, bf16[641,12,64]{0,2,1:T(8,128)(2,1)S(1)} %copy-done.15), kind=kOutput, calls=%fused_computation.42 | convolution fusion | flops 590284864 | bytes 37433152 | tf_op jit(solution)/shard_map/while/body/eval_jaxpr/cond/branch_0_fun/qhd,khd->hqk/dot_general | solution.py:101
  339.9 18.4 %multiply_convert_fusion = bf16[12,577,641]{1,2,0:T(8,128)(2,1)} fusion(f32[12,577,641]{1,2,0:T(8,128)} %get-tuple-element.314, f32[12,577,641]{1,2,0:T(8,128)} %fusion.331, f32[12,577]{1,0:T(8,128)S(1)} %get-tuple-element.313, f32[12,577]{1,0:T(8,128)S(1)} %bitcast.511, pred[641]{0:T(1024)(128)(4,1)S(1)} %get-tuple-element.112), kind=kLoop, calls=%fused_computation.41 | loop fusion | flops 26629704 | bytes 44438872 | tf_op jit(solution)/shard_map/while/body/eval_jaxpr/cond/branch_0_fun/convert_element_type | solution.py:105
  393.9 120.3 %all-reduce.12.cloned.1.call-done = (f32[1,577,1536]{1,2,0:T(8,128)}, f32[1,64,1536]{1,2,0:T(8,128)}) async-done(((f32[1,577,1536]{1,2,0:T(8,128)}, f32[1,64,1536]{1,2,0:T(8,128)}), (f32[1,577,1536]{1,2,0:T(8,128)}, f32[1,64,1536]{1,2,0:T(8,128)})) %all-reduce.12.cloned.1.call-update) | async-done | bytes 3938320 | tf_op jit(solution)/shard_map/psum | solution.py:22
  524.4 8.8 scatter_custom_fusion
  574.6 19.9 %fusion.61 = (bf16[3072,577]{0,1:T(8,128)(2,1)}, f32[3072,577]{0,1:T(8,128)}) fusion(f32[577,3072]{1,0:T(8,128)} %get-tuple-element.355, f32[577,3072]{1,0:T(8,128)} %copy-done.2, f32[3072]{0:T(1024)S(1)} %bitcast.514), kind=kLoop, calls=%fused_computation.107 | loop fusion | flops 129395712 | bytes 24827904 | tf_op jit(solution)/shard_map/convert_element_type | solution.py:268
  600.7 8.7 fusion.63
  628.1 9.5 maximum_bitcast_fusion
  639.1 9.1 multiply_bitcast_fusion.3
  656.6 40.6 %all-reduce.3 = (f32[13,768]{1,0:T(8,128)S(1)}, f32[2,3072]{1,0:T(2,128)S(1)}) all-reduce(f32[13,768]{1,0:T(8,128)S(1)} %pad_maximum_fusion.6, f32[2,3072]{1,0:T(2,128)S(1)} %broadcast_multiply_fusion.1), channel_id=1, replica_groups=mesh['mod'=2,'dp'=16] {'mod','dp'}, use_global_device_ids=true, to_apply=%region_39.40 | all-reduce | flops 16128 | bytes 129024 | tf_op jit(solution)/shard_map/psum | solution.py:389
  703.0 125.4 %reduce-scatter.3.cloned.1.call-done = f32[8,96,96]{2,1,0:T(8,128)} async-done(((f32[256,96,96]{2,1,0:T(8,128)}), f32[8,96,96]{2,1,0:T(8,128)}) %reduce-scatter.3.cloned.1.call-update) | async-done | bytes 294928 | tf_op jit(solution)/shard_map/reduce_scatter | solution.py:375
  857.0 219.0 %reduce-scatter.5.cloned.1.call-done = f32[1,32,96,96]{3,2,1,0:T(8,128)} async-done(((f32[1,512,96,96]{3,2,1,0:T(8,128)}), f32[1,32,96,96]{3,2,1,0:T(8,128)}) %reduce-scatter.5.cloned.1.call-update) | async-done | bytes 1179664 | tf_op jit(solution)/shard_map/reduce_scatter | solution.py:379
  (380 shorter events, 332.4 us)
Async XLA Ops:
  8.0 76.6 %all-gather.3.cloned.1.call-start = ((), (), s32[]{:S(2)}) async-start(), calls=%async_computation.2 | async-start | bytes 6488064 | tf_op jit(solution)/shard_map/all_gather | solution.py:186
  9.8 160.6 %all-reduce.14.cloned.1.call-start = ((), (), s32[]{:S(2)}) async-start(), calls=%async_computation.8 | async-start | bytes 3981312 | tf_op jit(solution)/shard_map/psum | solution.py:22
  16.8 87.5 %copy-start.74 = (f32[768]{0:T(1024)}, f32[768]{0:T(1024)S(1)}, u32[]{:S(2)}) copy-start(f32[768]{0:T(1024)S(1)} %get-tuple-element.282) | copy-start | bytes 9220
  16.8 87.5 %copy-start.79 = (f32[768]{0:T(1024)}, f32[768]{0:T(1024)S(1)}, u32[]{:S(2)}) copy-start(f32[768]{0:T(1024)S(1)} %get-tuple-element.281) | copy-start | bytes 9220
  18.9 85.4 %copy-start.65 = (f32[577]{0:T(1024)}, f32[577]{0:T(1024)S(1)}, u32[]{:S(2)}) copy-start(f32[577]{0:T(1024)S(1)} %broadcast_multiply_fusion.7) | copy-start | bytes 6928
  19.5 84.8 %copy-start.72 = (f32[577]{0:T(1024)}, f32[577]{0:T(1024)S(1)}, u32[]{:S(2)}) copy-start(f32[577]{0:T(1024)S(1)} %add_rsqrt_fusion.1) | copy-start | bytes 6928
  111.0 107.7 %all-gather.5.cloned.1.call-start = ((), (), s32[]{:S(2)}) async-start(), calls=%async_computation.3 | async-start | bytes 13369344 | tf_op jit(solution)/shard_map/all_gather | solution.py:190
  113.7 400.5 %all-reduce.12.cloned.1.call-start = ((), (), s32[]{:S(2)}) async-start(), calls=%async_computation.7 | async-start | bytes 9437184 | tf_op jit(solution)/shard_map/psum | solution.py:22
  114.6 183.6 %copy-start.63 = (f32[577]{0:T(1024)}, f32[577]{0:T(1024)S(1)}, u32[]{:S(2)}) copy-start(f32[577]{0:T(1024)S(1)} %or_convert_fusion) | copy-start | bytes 6928
  114.7 155.5 %copy-start.58 = (f32[1,3072]{1,0:T(1,128)}, f32[1,3072]{1,0:T(1,128)S(1)}, u32[]{:S(2)}) copy-start(f32[1,3072]{1,0:T(1,128)S(1)} %constant_dynamic-slice_fusion) | copy-start | bytes 36868
  264.3 28.5 %slice-start.8 = ((s8[4718592]{0:T(1024)(128)(4,1)}), s8[4194304]{0:T(1024)(128)(4,1)S(1)}, s32[]{:S(2)}) async-start(s8[4718592]{0:T(1024)(128)(4,1)} %bitcast.493), calls=%async_computation.17 | async-start | bytes 8388608
  270.2 22.7 %copy-start.2 = (f32[577,3072]{1,0:T(8,128)}, f32[577,3072]{1,0:T(8,128)S(1)}, u32[]{:S(2)}) copy-start(f32[577,3072]{1,0:T(8,128)S(1)} %fusion.315) | copy-start | bytes 21270532
  270.2 22.7 %slice-start.9 = ((s8[4718592]{0:T(1024)(128)(4,1)}), s8[524288]{0:T(1024)(128)(4,1)S(1)}, s32[]{:S(2)}) async-start(s8[4718592]{0:T(1024)(128)(4,1)} %bitcast.493), calls=%async_computation.18 | async-start | bytes 1048576
  393.8 304.8 %all-reduce.10.cloned.1.call-start = ((), (), s32[]{:S(2)}) async-start(), calls=%async_computation.6 | async-start | bytes 3588096 | tf_op jit(solution)/shard_map/psum | solution.py:389
  533.2 295.2 %reduce-scatter.3.cloned.1.call-start = ((), (), s32[]{:S(2)}) async-start(), calls=%async_computation.4 | async-start | bytes 12976128 | tf_op jit(solution)/shard_map/reduce_scatter | solution.py:375
  572.1 503.8 %reduce-scatter.5.cloned.1.call-start = ((), (), s32[]{:S(2)}) async-start(), calls=%async_computation.5 | async-start | bytes 26738688 | tf_op jit(solution)/shard_map/reduce_scatter | solution.py:379
  656.1 41.2 %copy-start.57 = (f32[13,768]{1,0:T(8,128)S(1)}, f32[13,768]{1,0:T(8,128)}, u32[]{:S(2)}) copy-start(f32[13,768]{1,0:T(8,128)} %param.30) | copy-start | bytes 119812
  656.1 41.2 %copy-start.62 = (f32[13,768]{1,0:T(8,128)S(1)}, f32[13,768]{1,0:T(8,128)}, u32[]{:S(2)}) copy-start(f32[13,768]{1,0:T(8,128)} %param.31) | copy-start | bytes 119812
  656.1 41.8 %copy-start.61 = (f32[2,3072]{1,0:T(2,128)S(1)}, f32[2,3072]{1,0:T(2,128)}, u32[]{:S(2)}) copy-start(f32[2,3072]{1,0:T(2,128)} %param.32) | copy-start | bytes 73732
  656.1 41.8 %copy-start.67 = (f32[2,3072]{1,0:T(2,128)S(1)}, f32[2,3072]{1,0:T(2,128)}, u32[]{:S(2)}) copy-start(f32[2,3072]{1,0:T(2,128)} %param.33) | copy-start | bytes 73732
  656.2 42.4 %copy-start = (f32[577,768]{1,0:T(8,128)S(1)}, f32[577,768]{1,0:T(8,128)}, u32[]{:S(2)}) copy-start(f32[577,768]{1,0:T(8,128)} %param.34) | copy-start | bytes 5317636
  698.6 129.9 %copy-start.52 = (f32[8,96,96]{2,1,0:T(8,128)S(1)}, f32[8,96,96]{2,1,0:T(8,128)}, u32[]{:S(2)}) copy-start(f32[8,96,96]{2,1,0:T(8,128)} %param.26) | copy-start | bytes 884740
  703.0 127.5 %copy-start.53 = (f32[8,96,96]{2,1,0:T(8,128)S(1)}, f32[8,96,96]{2,1,0:T(8,128)}, u32[]{:S(2)}) copy-start(f32[8,96,96]{2,1,0:T(8,128)} %param.25) | copy-start | bytes 884740
  854.6 221.3 %copy-start.41 = (f32[1,32,96,96]{3,2,1,0:T(8,128)S(1)}, f32[1,32,96,96]{3,2,1,0:T(8,128)}, u32[]{:S(2)}) copy-start(f32[1,32,96,96]{3,2,1,0:T(8,128)} %param.29) | copy-start | bytes 3538948
  (62 other events, 224.6 us)
Sparse Core Ops, SparseCore 0:
  12.3 72.2 all-gather.2
  111.1 59.2 all-reduce.13
  393.9 120.1 all-reduce.11
  533.4 132.7 all-reduce.9
  673.7 154.7 reduce-scatter.2
  833.0 242.9 reduce-scatter.4
Sparse Core Ops, SparseCore 1:
  113.8 98.9 all-gather.4
where the time goes:
time: 1190 us; the launch traced here: 1170 us
  waiting for transfers between devices  575 us (48%)
  matrix products  254 us (21%)
  local copies, waits for them, and re-layouts  143 us (12%)
  other arithmetic  124 us (10%)
  blocking collectives  40.6 us (3%)
  loops' own time  19 us (2%)
  between operations  18.3 us (2%)
    reduce_scatter x1, waiting for transfers between devices, local(): ffn_grad = lax.psum_scatter(ffn_full, 'dp', scatter_dimension=1, tiled=True)  219 us
    psum x2, waiting for transfers between devices, from_root(): return lax.psum(jnp.where(mine, shard, jnp.zeros_like(shard)), axis)  166 us
    reduce_scatter x1, waiting for transfers between devices, local(): lax.psum_scatter(attn_full, ('mod', 'dp'), scatter_dimension=0, tiled=True)  125 us
    all_gather x1, waiting for transfers between devices, local(): lax.all_gather(attn_blocks.astype(jnp.bfloat16), ('mod', 'dp'), axis=0, t...  63.6 us
    psum x1, blocking collectives, local(): lax.psum((vector_grad, up_bias_grad, grad_pos), ('mod', 'dp'))  40.6 us
    dot_general x4, matrix products, times_transposed(): lax.dot_general(rows, weight, (((1,), (1,)), ((), ())), preferred_element...  32 us
    dot_general x24, matrix products, inverse_root(): factor = jnp.einsum('bij,bjk->bik', factor, step_mat, precision=HIGHEST)  29.4 us
    dot_general x20, matrix products, inverse_root(): square = jnp.einsum('bij,bjk->bik', step_mat, step_mat, precision=HIGHEST)  24.4 us
  transfers between devices with their start and end apart: 7, of which 5 were waited for; matrix products, arithmetic and copies ran while one was open for 18% of the time, Pallas kernels for 0%

commit v1 on v0

v1 whole, which is shorter than its diff:
```python
import functools
import math

import jax
import jax.numpy as jnp
from jax import lax
from jax.experimental import pallas as pl
from jax.experimental.pallas import tpu as pltpu
from jax.sharding import PartitionSpec as P

HEADS = 12
TEXT = 64
NEWTON = 6
PAIR_LANES = 128
QUERY_TILE = 256
VMEM_LIMIT = 56 << 20

f32 = jnp.float32
bf16 = jnp.bfloat16
norm_eps = 1e-05
stat_decay = 0.5
matrix_rate = 0.25
moment_keep = 0.9
masked_score = -1e30


def dot_nn(left, right):
    return lax.dot_general(left, right, (((1,), (0,)), ((), ())), preferred_element_type=f32)


def dot_nt(left, right):
    return lax.dot_general(left, right, (((1,), (1,)), ((), ())), preferred_element_type=f32)


def dot_tn(left, right):
    return lax.dot_general(left, right, (((0,), (0,)), ((), ())), preferred_element_type=f32)


def params(**kwargs):
    return pltpu.CompilerParams(vmem_limit_bytes=VMEM_LIMIT, **kwargs)


def round_up(value, step):
    return (value + step - 1) // step * step


def whole(shape):
    return pl.BlockSpec(shape, lambda *ids: (0,) * len(shape))


SMEM_SPEC = pl.BlockSpec(memory_space=pltpu.SMEM)


def pack_kernel(blocks_ref, out_ref):
    count = blocks_ref.shape[0]
    pieces = [blocks_ref[i] for i in range(count)]
    out_ref[0] = jnp.concatenate(pieces, axis=1).astype(bf16)


def pack_rows(blocks, per_row):
    count, size, _ = blocks.shape
    return pl.pallas_call(
        pack_kernel,
        grid=(count // per_row,),
        in_specs=[pl.BlockSpec((per_row, size, size), lambda i: (i, 0, 0))],
        out_specs=pl.BlockSpec((1, size, per_row * size), lambda i: (i, 0, 0)),
        out_shape=jax.ShapeDtypeStruct((count // per_row, size, per_row * size), bf16),
        compiler_params=params(),
        name="pack_rows",
    )(blocks)


def norm_rows(values):
    centred = values - jnp.mean(values, axis=-1, keepdims=True)
    spread = jnp.mean(centred * centred, axis=-1, keepdims=True)
    inv_std = lax.rsqrt(spread + norm_eps)
    return centred * inv_std, inv_std


def norm_input_grad(grad_out, normal, inv_std, gain):
    grad_norm = grad_out * gain
    mean_grad = jnp.mean(grad_norm, axis=-1, keepdims=True)
    mean_proj = jnp.mean(grad_norm * normal, axis=-1, keepdims=True)
    return inv_std * (grad_norm - mean_grad - normal * mean_proj)


def project_kernel(row_ref, hidden_ref, vec_ref, w_ref, qkv_ref, first_ref):
    step = pl.program_id(0)

    @pl.when(step == 0)
    def _():
        normal, _ = norm_rows(hidden_ref[...])
        first_ref[...] = (normal * vec_ref[0:1, :] + vec_ref[1:2, :]).astype(bf16)

    rows = hidden_ref.shape[0]
    bias = jnp.where(step == 0, vec_ref[5:6, :], jnp.where(step == 2, vec_ref[6:7, :], 0.0))
    out = (dot_nn(first_ref[...], w_ref[0]) + bias).astype(bf16)
    qkv_ref[...] = jnp.zeros(qkv_ref.shape, bf16)
    qkv_ref[pl.ds(pl.multiple_of(row_ref[0], 16), rows), :] = out


def project(rows_info, hidden, vec, attn_mats, seq):
    rows, width = hidden.shape
    return pl.pallas_call(
        project_kernel,
        grid=(3,),
        in_specs=[
            SMEM_SPEC,
            whole((rows, width)),
            whole(vec.shape),
            pl.BlockSpec((1, width, width), lambda i: (i, 0, 0)),
        ],
        out_specs=[pl.BlockSpec((seq, width), lambda i: (0, i)), whole((rows, width))],
        out_shape=[
            jax.ShapeDtypeStruct((seq, 3 * width), bf16),
            jax.ShapeDtypeStruct((rows, width), bf16),
        ],
        compiler_params=params(),
        name="project",
    )(rows_info, hidden, vec, attn_mats)


def key_bias(row_ref, seq):
    rows = lax.broadcasted_iota(jnp.int32, (seq, 1), 0)
    counts = jnp.logical_and(rows >= row_ref[1], rows < row_ref[2])
    return jnp.where(counts, 0.0, masked_score).astype(f32)


def transposed(values):
    return jnp.transpose(values.astype(f32), (1, 0)).astype(bf16)


def attend_kernel(row_ref, q_ref, k_ref, v_ref, ctx_ref, lse_ref):
    seq = q_ref.shape[0]
    half = PAIR_LANES // 2
    scale = half ** (-0.5)
    bias = key_bias(row_ref, seq)
    keys = k_ref[...]
    values_t = transposed(v_ref[...])
    for start in range(0, seq, QUERY_TILE):
        size = min(QUERY_TILE, seq - start)
        tile = slice(start, start + size)
        queries = q_ref[tile, :]
        lane = lax.broadcasted_iota(jnp.int32, (size, PAIR_LANES), 1)
        parts = []
        for head in range(2):
            own = (lane < half) == (head == 0)
            scores = dot_nt(keys, jnp.where(own, queries, jnp.zeros_like(queries))) * scale + bias
            top = jnp.max(scores, axis=0, keepdims=True)
            raised = jnp.exp(scores - top)
            total = jnp.sum(raised, axis=0, keepdims=True)
            probs = (raised * (1.0 / total)).astype(bf16)
            parts.append(dot_nn(values_t[half * head : half * (head + 1), :], probs))
            lse_ref[0, head : head + 1, tile] = top + jnp.log(total)
        ctx_ref[tile, :] = jnp.transpose(jnp.concatenate(parts, axis=0), (1, 0)).astype(bf16)


def attend(rows_info, qkv):
    seq = qkv.shape[0]
    width = qkv.shape[1] // 3
    pairs = width // PAIR_LANES

    def column(base):
        return pl.BlockSpec((seq, PAIR_LANES), lambda i, base=base: (0, base + i))

    return pl.pallas_call(
        attend_kernel,
        grid=(pairs,),
        in_specs=[SMEM_SPEC, column(0), column(pairs), column(2 * pairs)],
        out_specs=[column(0), pl.BlockSpec((1, 8, seq), lambda i: (i, 0, 0))],
        out_shape=[
            jax.ShapeDtypeStruct((seq, width), bf16),
            jax.ShapeDtypeStruct((pairs, 8, seq), f32),
        ],
        compiler_params=params(),
        name="attend",
    )(rows_info, qkv, qkv, qkv)


def attend_grad_kernel(row_ref, q_ref, k_ref, v_ref, g_ref, lse_ref, out_ref, dk_ref, dv_ref):
    seq = q_ref.shape[0]
    half = PAIR_LANES // 2
    scale = half ** (-0.5)
    bias = key_bias(row_ref, seq)
    keys = k_ref[...]
    values = v_ref[...]
    keys_t = transposed(keys)
    for start in range(0, seq, QUERY_TILE):
        size = min(QUERY_TILE, seq - start)
        tile = slice(start, start + size)
        queries = q_ref[tile, :]
        row = lax.broadcasted_iota(jnp.int32, (size, 1), 0) + start
        counts = jnp.logical_and(row >= row_ref[1], row < row_ref[2])
        grads = jnp.where(counts, g_ref[tile, :], jnp.zeros((size, PAIR_LANES), bf16))
        lane = lax.broadcasted_iota(jnp.int32, (size, PAIR_LANES), 1)
        parts = []
        for head in range(2):
            own = (lane < half) == (head == 0)
            own_q = jnp.where(own, queries, jnp.zeros_like(queries))
            own_g = jnp.where(own, grads, jnp.zeros_like(grads))
            scores = dot_nt(keys, own_q) * scale + bias
            probs = jnp.exp(scores - lse_ref[0, head : head + 1, tile])
            grad_probs = dot_nt(values, own_g)
            row_dot = jnp.sum(probs * grad_probs, axis=0, keepdims=True)
            grad_scores = (probs * (grad_probs - row_dot)).astype(bf16)
            grad_v = dot_nn(probs.astype(bf16), own_g)
            grad_k = dot_nn(grad_scores, own_q)
            if start == 0 and head == 0:
                dv_ref[...] = grad_v
                dk_ref[...] = grad_k
            else:
                dv_ref[...] += grad_v
                dk_ref[...] += grad_k
            parts.append(dot_nn(keys_t[half * head : half * (head + 1), :], grad_scores))
        grad_q = jnp.transpose(jnp.concatenate(parts, axis=0) * scale, (1, 0))
        out_ref[0, tile, :] = grad_q.astype(bf16)
    out_ref[1] = (dk_ref[...] * scale).astype(bf16)
    out_ref[2] = dv_ref[...].astype(bf16)


def attend_grad(rows_info, qkv, grad_ctx, lse):
    seq = qkv.shape[0]
    width = qkv.shape[1] // 3
    pairs = width // PAIR_LANES

    def column(base):
        return pl.BlockSpec((seq, PAIR_LANES), lambda i, base=base: (0, base + i))

    return pl.pallas_call(
        attend_grad_kernel,
        grid=(pairs,),
        in_specs=[
            SMEM_SPEC,
            column(0),
            column(pairs),
            column(2 * pairs),
            column(0),
            pl.BlockSpec((1, 8, seq), lambda i: (i, 0, 0)),
        ],
        out_specs=pl.BlockSpec((3, seq, PAIR_LANES), lambda i: (0, 0, i)),
        out_shape=jax.ShapeDtypeStruct((3, seq, width), bf16),
        scratch_shapes=[pltpu.VMEM((seq, PAIR_LANES), f32)] * 2,
        compiler_params=params(),
        name="attend_grad",
    )(rows_info, qkv, qkv, qkv, grad_ctx, lse)


def gelu_pair(values):
    size = jnp.abs(values)
    tail = 1.0 / (1.0 + (0.3275911 * 0.5**0.5) * size)
    poly = tail * (
        0.254829592
        + tail * (-0.284496736 + tail * (1.421413741 + tail * (-1.453152027 + tail * 1.061405429)))
    )
    bell = jnp.exp(-0.5 * values * values)
    upper = 0.5 * poly * bell
    share = jnp.where(values >= 0.0, 1.0 - upper, upper)
    return values * share, share + values * bell * ((2.0 * math.pi) ** -0.5)


def expert_kernel(
    row_ref,
    ctx_ref,
    pair_ref,
    hidden_ref,
    cot_ref,
    vec_ref,
    upb_ref,
    wo_ref,
    up_ref,
    down_ref,
    out_ref,
    gmid_ref,
    gctx_ref,
    dwo_ref,
    dup_ref,
    ddown_ref,
    dvec_ref,
    dupb_ref,
    own_ctx,
    middle,
    second,
    gres,
    gbranch,
    pre,
    gact,
    act,
    gpre,
    branch,
    gsecond,
):
    step = pl.program_id(0)
    last = pl.num_programs(0) - 1
    rows = hidden_ref.shape[0]
    width = hidden_ref.shape[1]
    out_rows = out_ref.shape[0]
    offset = pl.multiple_of(row_ref[0], 16)
    tile = 16
    tiles = rows // tile

    def tile_slice(i):
        return pl.ds(pl.multiple_of(i * tile, tile), tile)

    @pl.when(step == 0)
    def _():
        own_ctx[...] = ctx_ref[pl.ds(offset, rows), :]

        @pl.when(row_ref[3] == 1)
        def _():
            own_ctx[0 : pair_ref.shape[0], :] = pair_ref[...]

        middle[...] = dot_nn(own_ctx[...], wo_ref[...])

        def body(i, total):
            at = tile_slice(i)
            mid = hidden_ref[at, :] + (middle[at, :] + vec_ref[7:8, :])
            middle[at, :] = mid
            normal, _ = norm_rows(mid)
            second[at, :] = (normal * vec_ref[2:3, :] + vec_ref[3:4, :]).astype(bf16)
            row = lax.broadcasted_iota(jnp.int32, (tile, 1), 0) + i * tile
            kept = jnp.where(row < row_ref[4], cot_ref[at, :], 0.0)
            rounded = kept.astype(bf16)
            gbranch[at, :] = rounded
            return total + rounded.astype(f32)

        total = lax.fori_loop(0, tiles, body, jnp.zeros((tile, width), f32))
        dvec_ref[2:3, :] = jnp.sum(total, axis=0, keepdims=True)

    up = up_ref[...].reshape(width, up_ref.shape[3])
    down = down_ref[...]
    pre[...] = dot_nn(second[...], up)
    gact[...] = dot_nt(gbranch[...], down)

    def gelu_body(i, total):
        at = tile_slice(i)
        value, slope = gelu_pair(pre[at, :] + upb_ref[...])
        act[at, :] = value.astype(bf16)
        rounded = (gact[at, :] * slope).astype(bf16)
        gpre[at, :] = rounded
        return total + rounded.astype(f32)

    total = lax.fori_loop(0, tiles, gelu_body, jnp.zeros((tile, act.shape[1]), f32))
    dupb_ref[...] = jnp.sum(total, axis=0, keepdims=True)
    ddown_ref[...] = dot_tn(act[...], gbranch[...]).astype(bf16)
    dup_ref[...] = dot_tn(second[...], gpre[...]).astype(bf16).reshape(dup_ref.shape)
    own_branch = dot_nn(act[...], down)
    own_gsecond = dot_nt(gpre[...], up)

    @pl.when(step == 0)
    def _():
        branch[...] = own_branch
        gsecond[...] = own_gsecond

    @pl.when(step > 0)
    def _():
        branch[...] += own_branch
        gsecond[...] += own_gsecond

    @pl.when(step == last)
    def _():
        def body(i, totals):
            at = tile_slice(i)
            mid = middle[at, :]
            normal, inv_std = norm_rows(mid)
            grad_out = gsecond[at, :]
            row = lax.broadcasted_iota(jnp.int32, (tile, 1), 0) + i * tile
            kept = row < row_ref[4]
            branch[at, :] = jnp.where(kept, mid + (branch[at, :] + vec_ref[4:5, :]), 0.0)
            grad_in = norm_input_grad(grad_out, normal, inv_std, vec_ref[2:3, :])
            grad_mid = jnp.where(kept, cot_ref[at, :], 0.0) + grad_in
            gmid_ref[at, :] = grad_mid
            rounded = grad_mid.astype(bf16)
            gbranch[at, :] = rounded
            return (
                totals[0] + grad_out * normal,
                totals[1] + grad_out,
                totals[2] + rounded.astype(f32),
            )

        zero = jnp.zeros((tile, width), f32)
        gains, shifts, biases = lax.fori_loop(0, tiles, body, (zero, zero, zero))
        dvec_ref[0:1, :] = jnp.sum(gains, axis=0, keepdims=True)
        dvec_ref[1:2, :] = jnp.sum(shifts, axis=0, keepdims=True)
        dvec_ref[3:4, :] = jnp.sum(biases, axis=0, keepdims=True)
        dvec_ref[4:8, :] = jnp.zeros((4, width), f32)
        out_ref[...] = branch[0:out_rows, :]
        dwo_ref[...] = dot_tn(own_ctx[...], gbranch[...]).astype(bf16)
        gctx_ref[...] = jnp.zeros(gctx_ref.shape, bf16)
        gctx_ref[pl.ds(offset, rows), :] = dot_nt(gbranch[...], wo_ref[...]).astype(bf16)


def expert(rows_info, ctx, pair_ctx, hidden, cot, vec, up_bias, w_out, up_parts, down_mat, out_rows):
    rows, width = hidden.shape
    seq = ctx.shape[0]
    row_blocks, chunks, size, chunk = up_parts.shape
    return pl.pallas_call(
        expert_kernel,
        grid=(chunks,),
        in_specs=[
            SMEM_SPEC,
            whole(ctx.shape),
            whole(pair_ctx.shape),
            whole(hidden.shape),
            whole(cot.shape),
            whole(vec.shape),
            pl.BlockSpec((1, chunk), lambda i: (0, i)),
            whole(w_out.shape),
            pl.BlockSpec((row_blocks, 1, size, chunk), lambda i: (0, i, 0, 0)),
            pl.BlockSpec((chunk, width), lambda i: (i, 0)),
        ],
        out_specs=[
            whole((out_rows, width)),
            whole((rows, width)),
            whole((seq, width)),
            whole((width, width)),
            pl.BlockSpec((row_blocks, 1, size, chunk), lambda i: (0, i, 0, 0)),
            pl.BlockSpec((chunk, width), lambda i: (i, 0)),
            whole((8, width)),
            pl.BlockSpec((1, chunk), lambda i: (0, i)),
        ],
        out_shape=[
            jax.ShapeDtypeStruct((out_rows, width), f32),
            jax.ShapeDtypeStruct((rows, width), f32),
            jax.ShapeDtypeStruct((seq, width), bf16),
            jax.ShapeDtypeStruct((width, width), bf16),
            jax.ShapeDtypeStruct(up_parts.shape, bf16),
            jax.ShapeDtypeStruct(down_mat.shape, bf16),
            jax.ShapeDtypeStruct((8, width), f32),
            jax.ShapeDtypeStruct(up_bias.shape, f32),
        ],
        scratch_shapes=[
            pltpu.VMEM((rows, width), bf16),
            pltpu.VMEM((rows, width), f32),
            pltpu.VMEM((rows, width), bf16),
            pltpu.VMEM((8, 128), f32),
            pltpu.VMEM((rows, width), bf16),
            pltpu.VMEM((rows, chunk), f32),
            pltpu.VMEM((rows, chunk), f32),
            pltpu.VMEM((rows, chunk), bf16),
            pltpu.VMEM((rows, chunk), bf16),
            pltpu.VMEM((rows, width), f32),
            pltpu.VMEM((rows, width), f32),
        ],
        compiler_params=params(),
        name="expert",
    )(rows_info, ctx, pair_ctx, hidden, cot, vec, up_bias, w_out, up_parts, down_mat)


def project_grad_kernel(
    row_ref, dqkv_ref, first_ref, hidden_ref, gmid_ref, vec_ref, w_ref, out_ref, dw_ref, dvec_ref, gfirst, own
):
    step = pl.program_id(0)
    rows, width = hidden_ref.shape
    out_rows = out_ref.shape[0]
    tile = 16
    tiles = rows // tile
    own[...] = dqkv_ref[0, pl.ds(pl.multiple_of(row_ref[0], 16), rows), :]
    dw_ref[0] = dot_tn(first_ref[...], own[...]).astype(bf16)
    share = dot_nt(own[...], w_ref[0])

    @pl.when(step == 0)
    def _():
        gfirst[...] = share
        dvec_ref[4:8, :] = jnp.zeros((4, width), f32)
        dvec_ref[2:3, :] = jnp.sum(own[...].astype(f32), axis=0, keepdims=True)

    @pl.when(step > 0)
    def _():
        gfirst[...] += share

    @pl.when(step == 2)
    def _():
        dvec_ref[3:4, :] = jnp.sum(own[...].astype(f32), axis=0, keepdims=True)

        def body(i, totals):
            at = pl.ds(pl.multiple_of(i * tile, tile), tile)
            normal, inv_std = norm_rows(hidden_ref[at, :])
            grad_out = gfirst[at, :]
            grad_in = norm_input_grad(grad_out, normal, inv_std, vec_ref[0:1, :])
            gfirst[at, :] = gmid_ref[at, :] + grad_in
            return totals[0] + grad_out * normal, totals[1] + grad_out

        zero = jnp.zeros((tile, width), f32)
        gains, shifts = lax.fori_loop(0, tiles, body, (zero, zero))
        dvec_ref[0:1, :] = jnp.sum(gains, axis=0, keepdims=True)
        dvec_ref[1:2, :] = jnp.sum(shifts, axis=0, keepdims=True)
        out_ref[...] = gfirst[0:out_rows, :]


def project_grad(rows_info, dqkv, first, hidden, grad_middle, vec, attn_mats, out_rows):
    rows, width = hidden.shape
    seq = dqkv.shape[1]
    square = pl.BlockSpec((1, width, width), lambda i: (i, 0, 0))
    return pl.pallas_call(
        project_grad_kernel,
        grid=(3,),
        in_specs=[
            SMEM_SPEC,
            pl.BlockSpec((1, seq, width), lambda i: (i, 0, 0)),
            whole((rows, width)),
            whole((rows, width)),
            whole((rows, width)),
            whole(vec.shape),
            square,
        ],
        out_specs=[whole((out_rows, width)), square, whole((8, width))],
        out_shape=[
            jax.ShapeDtypeStruct((out_rows, width), f32),
            jax.ShapeDtypeStruct((3, width, width), bf16),
            jax.ShapeDtypeStruct((8, width), f32),
        ],
        scratch_shapes=[pltpu.VMEM((rows, width), f32), pltpu.VMEM((rows, width), bf16)],
        compiler_params=params(),
        name="project_grad",
    )(rows_info, dqkv, first, hidden, grad_middle, vec, attn_mats)


def widen(values):
    rows, cols = values.shape
    return jnp.concatenate([values, jnp.zeros((rows, PAIR_LANES - cols), f32)], axis=1)


def split_parts(values):
    high = values.astype(bf16)
    return high, (values - high.astype(f32)).astype(bf16)


def left_parts(values):
    return jnp.concatenate(split_parts(values), axis=1)


def right_parts(values):
    high, low = split_parts(values)
    rows, cols = high.shape
    gap = jnp.zeros((cols - rows, cols), bf16)
    near = jnp.concatenate([high, gap, high, gap], axis=0)
    far = jnp.concatenate([low, gap, jnp.zeros((cols, cols), bf16)], axis=0)
    return jnp.concatenate([near, far], axis=1)


def times(left, right):
    both = dot_nn(left, right)
    return both[:, :PAIR_LANES] + both[:, PAIR_LANES:]


def inverse_roots(stats, identity):
    size = stats[0].shape[0]
    mats, factors = [], []
    for stat in stats:
        norm = jnp.sqrt(jnp.sum(stat * stat, keepdims=True))
        mats.append(stat * (1.0 / norm))
        factors.append(lax.rsqrt(jnp.sqrt(norm)))
    for iteration in range(NEWTON):
        steps = [1.25 * identity - 0.25 * mat for mat in mats]
        if iteration == 0:
            factors = [step * factor for step, factor in zip(steps, factors)]
            squares = [times(left_parts(step), right_parts(step)) for step in steps]
        elif iteration < NEWTON - 1:
            both = [
                times(
                    jnp.concatenate([left_parts(step), left_parts(factor)], axis=0),
                    right_parts(step),
                )
                for step, factor in zip(steps, factors)
            ]
            squares = [pair[:size] for pair in both]
            factors = [pair[size:] for pair in both]
        else:
            return [
                times(left_parts(factor), right_parts(step)) for step, factor in zip(steps, factors)
            ]
        fourths = [times(left_parts(square), right_parts(square)) for square in squares]
        mats = [times(left_parts(fourth), right_parts(mat)) for fourth, mat in zip(fourths, mats)]


def shampoo_kernel(group, grads_ref, left_ref, right_ref, w_ref, g_out, left_out, right_out, w_out):
    count, size, _ = left_ref.shape
    row = lax.broadcasted_iota(jnp.int32, (size, PAIR_LANES), 0)
    col = lax.broadcasted_iota(jnp.int32, (size, PAIR_LANES), 1)
    identity = (row == col).astype(f32)
    for base in range(0, count, group):
        stats, grads = [], []
        for i in range(base, base + group):
            grad = grads_ref[0, :, i * size : (i + 1) * size]
            g_out[i] = grad
            grad = widen(grad)
            grad_t = widen(jnp.transpose(grad, (1, 0))[:size])
            grads.append(grad)
            outer = times(left_parts(grad), right_parts(grad_t))
            inner = times(left_parts(grad_t), right_parts(grad))
            left_new = stat_decay * left_ref[i] + (1.0 - stat_decay) * outer[:, :size]
            right_new = stat_decay * right_ref[i] + (1.0 - stat_decay) * inner[:, :size]
            left_out[i] = left_new
            right_out[i] = right_new
            stats += [widen(left_new), widen(right_new)]
        roots = inverse_roots(stats, identity)
        for at in range(group):
            half_way = times(left_parts(roots[2 * at]), right_parts(grads[at]))
            update = times(left_parts(half_way), right_parts(roots[2 * at + 1]))
            w_out[base + at] = w_ref[base + at] - matrix_rate * update[:, :size]


def shampoo(grad_rows, lefts, rights, weights):
    parts, size, span = grad_rows.shape
    count = span // size
    group = math.gcd(count, 4)
    blocks = pl.BlockSpec((count, size, size), lambda i: (i, 0, 0))
    shape = jax.ShapeDtypeStruct(lefts.shape, f32)
    return pl.pallas_call(
        functools.partial(shampoo_kernel, group),
        grid=(parts,),
        in_specs=[pl.BlockSpec((1, size, span), lambda i: (i, 0, 0)), blocks, blocks, blocks],
        out_specs=[blocks] * 4,
        out_shape=[shape] * 4,
        compiler_params=params(),
        name="shampoo",
    )(grad_rows, lefts, rights, weights)


def blocks_to_matrix(blocks, row_blocks, col_blocks):
    block_size = blocks.shape[-1]
    leading = blocks.shape[:-3]
    shaped = blocks.reshape(leading + (row_blocks, col_blocks, block_size, block_size))
    moved = jnp.swapaxes(shaped, -3, -2)
    return moved.reshape(leading + (row_blocks * block_size, col_blocks * block_size))


def local(
    stream_in,
    cotangent,
    patch_count,
    pos_index,
    attn_blocks,
    attn_left,
    attn_right,
    ffn_blocks,
    ffn_left,
    ffn_right,
    vectors,
    vectors_mom,
    ffn_bias,
    ffn_bias_mom,
    pos_table,
    pos_mom,
):
    size = attn_blocks.shape[-1]
    width = vectors.shape[1]
    hidden_units = ffn_bias.shape[1]
    slots = stream_in.shape[2]
    row_blocks = width // size
    chunks = hidden_units // width
    rows = round_up(slots, 16)
    seq = round_up(slots + TEXT, 32)
    own_attn = attn_blocks.shape[0]
    ffn_flat = ffn_blocks.shape[1]
    modality = lax.axis_index("mod")
    is_text = modality == 1
    image_flag = (1 - modality).astype(f32)

    attn_span = math.gcd(own_attn, row_blocks)
    ffn_span = math.gcd(ffn_flat, row_blocks)
    attn_rows = pack_rows(attn_blocks, attn_span)
    ffn_rows = pack_rows(ffn_blocks[0], ffn_span)
    attn_all = lax.all_gather(attn_rows, ("mod", "dp"), axis=0, tiled=True)
    ffn_all = lax.all_gather(ffn_rows, "dp", axis=0, tiled=True)

    def join(parts):
        lead, _, span = parts.shape
        if span == width:
            return parts
        shaped = parts.reshape(-1, width // span, size, span)
        return jnp.swapaxes(shaped, 1, 2).reshape(-1, size, width)

    attn_mats = join(attn_all).reshape(4, width, width)
    ffn_parts = join(ffn_all).reshape(2, -1, size, width)
    up_parts = ffn_parts[0].reshape(row_blocks, chunks, size, width)
    down_mat = ffn_parts[1].reshape(hidden_units, width)

    own_vec = lax.dynamic_slice_in_dim(vectors, 3 + 5 * modality, 5, 0)
    vec = jnp.concatenate([own_vec, vectors[0:3][jnp.array([0, 1, 2])]], axis=0)
    up_bias = lax.dynamic_slice_in_dim(ffn_bias, modality, 1, 0)
    count = patch_count[0]
    offset = TEXT * (1 - modality)
    first_key = jnp.where(is_text, TEXT, 0)
    end_key = jnp.where(is_text, slots, TEXT + count)
    kept_rows = jnp.where(is_text, slots, count)
    rows_info = jnp.stack([offset, first_key, end_key, modality, kept_rows]).astype(jnp.int32)
    pad = ((0, rows - slots), (0, 0))
    hidden = stream_in[0, 0] + image_flag * jnp.take(pos_table, pos_index[0], axis=0)
    hidden = jnp.pad(hidden, pad)
    cot = jnp.pad(cotangent[0, 0], pad)

    to_image = [(1, 0)]
    to_text = [(0, 1)]
    qkv, first = project(rows_info, hidden, vec, attn_mats, seq)
    pair_qkv = lax.ppermute(qkv[:TEXT], "mod", to_image)
    qkv = lax.dynamic_update_slice(qkv, jnp.where(is_text, qkv[:TEXT], pair_qkv), (0, 0))
    ctx, lse = attend(rows_info, qkv)
    pair_ctx = lax.ppermute(ctx[:TEXT], "mod", to_text)
    stream_out, grad_middle, grad_ctx, grad_wo, grad_up, grad_down, late_vec, grad_up_bias = expert(
        rows_info, ctx, pair_ctx, hidden, cot, vec, up_bias, attn_mats[3], up_parts, down_mat, slots
    )
    pair_grad = lax.ppermute(grad_ctx[:TEXT], "mod", to_image)
    grad_ctx = lax.dynamic_update_slice(
        grad_ctx, jnp.where(is_text, grad_ctx[:TEXT], pair_grad), (0, 0)
    )
    grad_qkv = attend_grad(rows_info, qkv, grad_ctx, lse)
    pair_dqkv = lax.ppermute(grad_qkv[:, :TEXT], "mod", to_text)
    grad_qkv = lax.dynamic_update_slice(
        grad_qkv, jnp.where(is_text, pair_dqkv, grad_qkv[:, :TEXT]), (0, 0, 0)
    )
    stream_grad, grad_wqkv, early_vec = project_grad(
        rows_info, grad_qkv, first, hidden, grad_middle, vec, attn_mats, slots
    )

    def spread(parts, span):
        if span == width:
            return parts
        shaped = parts.reshape(-1, size, width // span, span)
        return jnp.swapaxes(shaped, 1, 2).reshape(-1, size, span)

    ffn_full = jnp.concatenate(
        [grad_up.reshape(-1, size, width), grad_down.reshape(-1, size, width)], axis=0
    )
    ffn_sum = lax.psum_scatter(
        spread(ffn_full, ffn_span * size), "dp", scatter_dimension=0, tiled=True
    )
    attn_full = jnp.concatenate([grad_wqkv, grad_wo[None]], axis=0).reshape(-1, size, width)
    attn_sum = lax.psum_scatter(
        spread(attn_full, attn_span * size), ("mod", "dp"), scatter_dimension=0, tiled=True
    )
    grad_pos = jax.ops.segment_sum(image_flag * stream_grad, pos_index[0], num_segments=slots)
    selector = (jnp.arange(2) == modality).astype(f32)
    own_rows = jnp.stack([early_vec[0], early_vec[1], late_vec[0], late_vec[1], late_vec[2]])
    shared_rows = jnp.stack([early_vec[2], early_vec[3], late_vec[3]])
    vector_grad = jnp.concatenate(
        [shared_rows, (selector[:, None, None] * own_rows[None]).reshape(10, width)], axis=0
    )
    up_bias_grad = selector[:, None] * grad_up_bias
    vector_sum, up_bias_sum, pos_sum = lax.psum((vector_grad, up_bias_grad, grad_pos), ("mod", "dp"))

    items_total = lax.axis_size("dp")
    vector_rate = 0.3 / math.sqrt(items_total * slots)
    pos_rate = 0.5 / math.sqrt(items_total)
    vectors_mom_new = moment_keep * vectors_mom + vector_sum
    vectors_new = vectors - vector_rate * vectors_mom_new
    ffn_bias_mom_new = moment_keep * ffn_bias_mom + up_bias_sum
    ffn_bias_new = ffn_bias - vector_rate * ffn_bias_mom_new
    pos_mom_new = moment_keep * pos_mom + pos_sum
    pos_new = pos_table - pos_rate * pos_mom_new
    ffn_out = shampoo(ffn_sum.astype(f32), ffn_left[0], ffn_right[0], ffn_blocks[0])
    attn_out = shampoo(attn_sum.astype(f32), attn_left, attn_right, attn_blocks)
    return (
        stream_out[None, None],
        stream_grad[None, None],
        *attn_out,
        *(part[None] for part in ffn_out),
        vectors_mom_new,
        vectors_new,
        ffn_bias_mom_new,
        ffn_bias_new,
        pos_mom_new,
        pos_new,
    )


def solution(mesh):
    items = P("mod", "dp", None, None)
    owned = P(("mod", "dp"), None, None)
    return jax.shard_map(
        local,
        mesh=mesh,
        in_specs=(items, items, P("dp"), P("dp", None), owned, owned, owned, items, items, items)
        + (P(),) * 6,
        out_specs=(items, items, owned, owned, owned, owned, items, items, items, items)
        + (P(),) * 6,
        check_vma=False,
    )
```

time: 1190 us -> 707 us (0.59)
  matrix products: 254 us -> 0 us
  waiting for transfers between devices: 575 us -> 384 us
  Pallas kernels: 0 us -> 178 us
  local copies, waits for them, and re-layouts: 143 us -> 37.4 us
  other arithmetic: 124 us -> 39.3 us
  loops' own time: 19 us -> 0 us
    dot_general x111 -> x0, matrix products: 254 us -> none  [the longest x4 32 us: times_transposed(): lax.dot_general(rows, weight, (((1,), (1,)), ((), ())), preferred_element...]
    pallas_call x0 -> x9, Pallas kernels: none -> 178 us  [the longest x1 57.2 us: expert(): pl.pallas_call(expert_kernel, grid=(chunks,), in_specs=[SMEM_SPEC, whole(...]
    psum x2 -> x0, waiting for transfers between devices: 166 us -> none  [from_root(): return lax.psum(jnp.where(mine, shard, jnp.zeros_like(shard)), axis)]
    reduce_scatter x2, waiting for transfers between devices: 344 us -> 211 us  [the longest x1 107 us: local(): lax.psum_scatter(spread(attn_full, attn_span * size), ('mod', 'dp'), scat...]
    psum x1, waiting for transfers between devices: 0.01 us -> 66.2 us  [local(): lax.psum((vector_grad, up_bias_grad, grad_pos), ('mod', 'dp'))]
    convert_element_type x10 -> x3, other arithmetic: 55.4 us -> 3.83 us  [the longest x1 2.19 us: local(): ffn_sum.astype(f32)]
    reshape x4 -> x0, local copies, waits for them, and re-layouts: 36.5 us -> none  [the longest x2 22.9 us: blocks_to_matrix(): moved.reshape(leading + (row_blocks * block_size, col_blocks * block_size))]
    another operation x16 -> x2, local copies, waits for them, and re-layouts: 26.3 us -> 0.61 us  [the longest x1 0.6 us: local(): jnp.stack([offset, first_key, end_key, modality, kept_rows])]
  transfers between devices with their start and end apart: 7 -> 9, of which waited for: 5 -> 8; matrix products, arithmetic and copies ran while one was open for 18% -> 8% of each run, Pallas kernels for 0% -> 6%
where the time goes in v1:
time: 707 us; the launch traced here: 700 us
  waiting for transfers between devices  384 us (54%)
  Pallas kernels  178 us (25%)
  blocking collectives  41 us (6%)
  other arithmetic  39.3 us (6%)
  local copies, waits for them, and re-layouts  37.4 us (5%)
  between operations  14.9 us (2%)
    reduce_scatter x1, waiting for transfers between devices, local(): lax.psum_scatter(spread(attn_full, attn_span * size), ('mod', 'dp'), scat...  107 us
    reduce_scatter x1, waiting for transfers between devices, local(): lax.psum_scatter(spread(ffn_full, ffn_span * size), 'dp', scatter_dimensi...  104 us
    psum x1, waiting for transfers between devices, local(): lax.psum((vector_grad, up_bias_grad, grad_pos), ('mod', 'dp'))  66.2 us
    pallas_call x1, Pallas kernels, expert(): pl.pallas_call(expert_kernel, grid=(chunks,), in_specs=[SMEM_SPEC, whole(...  57.2 us
    all_gather x1, waiting for transfers between devices, local(): attn_all = lax.all_gather(attn_rows, ('mod', 'dp'), axis=0, tiled=True)  50.4 us
    psum x1, blocking collectives, local(): lax.psum((vector_grad, up_bias_grad, grad_pos), ('mod', 'dp'))  41 us
    pallas_call x2, Pallas kernels, shampoo(): pl.pallas_call(functools.partial(shampoo_kernel, group), grid=(parts,), i...  40.6 us
    all_gather x1, waiting for transfers between devices, local(): ffn_all = lax.all_gather(ffn_rows, 'dp', axis=0, tiled=True)  37.7 us
  transfers between devices with their start and end apart: 9, of which 8 were waited for; matrix products, arithmetic and copies ran while one was open for 8% of the time, Pallas kernels for 6%

profile of v1, /device:TPU:0, one launch (start us, length us, event | category | flops | bytes accessed | tf_op | source)
XLA Modules:
  0.0 700.4 jit_solution(5150540904502449836)
XLA Ops:
  9.1 3.6 pack_rows.3
  27.3 50.4 %all-gather.3.cloned.1.call-done = bf16[32,96,768]{2,1,0:T(8,128)(2,1)} async-done(((bf16[1,96,768]{2,1,0:T(8,128)(2,1)}), bf16[32,96,768]{2,1,0:T(8,128)(2,1)}) %all-gather.3.cloned.1.call-update) | async-done | bytes 4718608 | tf_op jit(solution)/shard_map/all_gather | solution.py:664
  77.7 6.9 project.1
  89.9 6.8 collective-permute-done
  98.4 22.3 %attend.1 = (bf16[672,768]{1,0:T(8,128)(2,1)}, f32[6,8,672]{2,1,0:T(8,128)}) custom-call(s32[5]{0:T(128)} %stack.27.row_ref, bf16[672,2304]{1,0:T(8,128)(2,1)} %select_dynamic-update-slice_fusion.1.q_ref.k_ref.v_ref, bf16[672,2304]{1,0:T(8,128)(2,1)} %select_dynamic-update-slice_fusion.1.q_ref.k_ref.v_ref, ...), custom_call_target="tpu_custom_call" | custom-call | tf_op jit(solution)/shard_map/attend/pallas_call | solution.py:166
  123.2 37.7 %all-gather.5.cloned.1.call-done = bf16[64,96,768]{2,1,0:T(8,128)(2,1)} async-done(((bf16[4,96,768]{2,1,0:T(8,128)(2,1)}), bf16[64,96,768]{2,1,0:T(8,128)(2,1)}) %all-gather.5.cloned.1.call-update) | async-done | bytes 9437200 | tf_op jit(solution)/shard_map/all_gather | solution.py:665
  160.9 8.0 %fusion.5 = (bf16[32,96,768]{2,1,0:T(8,128)(2,1)}, bf16[32,96,768]{2,1,0:T(8,128)(2,1)}) fusion(bf16[64,96,768]{2,1,0:T(8,128)(2,1)} %all-gather.5.cloned.1.call-done), kind=kLoop, calls=%fused_computation.34 | loop fusion | bytes 18874368 | tf_op jit(solution)/shard_map/slice | solution.py:677
  169.5 57.2 %expert.1 = (f32[577,768]{1,0:T(8,128)}, f32[592,768]{1,0:T(8,128)}, bf16[672,768]{1,0:T(8,128)(2,1)}, bf16[768,768]{1,0:T(8,128)(2,1)}, bf16[8,4,96,768]{3,2,1,...) custom-call(s32[5]{0:T(128)} %stack.27.row_ref, ...), custom_call_target="tpu_custom_call" | custom-call | tf_op jit(solution)/shard_map/expert/pallas_call | solution.py:396
  229.0 5.6 collective-permute-done.2
  236.1 24.8 %attend_grad.1 = bf16[3,672,768]{2,1,0:T(8,128)(2,1)} custom-call(s32[5]{0:T(128)} %stack.27.row_ref, bf16[672,2304]{1,0:T(8,128)(2,1)} %select_dynamic-update-slice_fusion.1.q_ref.k_ref.v_ref, bf16[672,2304]{1,0:T(8,128)(2,1)} %select_dynamic-update-slice_fusion.1.q_ref.k_ref.v_ref, bf16[672,2304]{1,0:T(8,128)(2,1)} %select_dynamic-update-slice_fusion.1.q_ref.k_ref.v_ref, ...), custom_call_target="tpu_custom_call" | custom-call | tf_op jit(solution)/shard_map/attend_grad/pallas_call | solution.py:229
  263.6 5.7 collective-permute-done.3
  271.1 21.0 %project_grad.1 = (f32[577,768]{1,0:T(8,128)}, bf16[3,768,768]{2,1,0:T(8,128)(2,1)}, f32[8,768]{1,0:T(8,128)}) custom-call(s32[5]{0:T(128)} %stack.27.row_ref, bf16[3,672,768]{2,1,0:T(8,128)(2,1)} %select_dynamic-update-slice_fusion.dqkv_ref, bf16[592,768]{1,0:T(8,128)(2,1)} %get-tuple-element.44.first_ref, f32[592,768]{1,0:T(8,128)} %pad.7.hidden_ref, ...), custom_call_target="tpu_custom_call" | custom-call | tf_op jit(solution)/shard_map/project_grad/pallas_call | solution.py:494
  292.1 9.4 %scatter_custom_fusion = f32[577,768]{1,0:T(8,128)} fusion(s32[577]{0:T(1024)S(1)} %reduce, f32[577,768]{1,0:T(8,128)} %get-tuple-element.46, f32[]{:T(128)} %constant.24.clone.1, f32[]{:T(128)S(6)} %convert_element_type.23), kind=kCustom, calls=%fused_computation.8 | custom fusion | flops 886272 | bytes 3545096 | tf_op jit(solution)/shard_map/scatter-add | solution.py:732
  302.8 4.5 pad_maximum_fusion.1
  307.4 7.8 %pad_maximum_fusion = bf16[64,96,768]{2,1,0:T(8,128)(2,1)} fusion(bf16[32,96,768]{2,1,0:T(8,128)(2,1)} %bitcast.44, bf16[32,96,768]{2,1,0:T(8,128)(2,1)} %bitcast.43), kind=kLoop, calls=%fused_computation.3 | loop fusion | flops 4718592 | bytes 18874368 | tf_op jit(solution)/shard_map/concatenate | solution.py:722
  316.0 4.5 copy.37
  320.7 4.5 copy.38
  325.3 41.0 %all-reduce.2 = (f32[13,768]{1,0:T(8,128)S(1)}, f32[2,3072]{1,0:T(2,128)S(1)}) all-reduce(f32[13,768]{1,0:T(8,128)S(1)} %pad_maximum_fusion.2, f32[2,3072]{1,0:T(2,128)S(1)} %broadcast_multiply_fusion.1), channel_id=1, replica_groups=mesh['mod'=2,'dp'=16] {'mod','dp'}, use_global_device_ids=true, to_apply=%region_2.3 | all-reduce | flops 16128 | bytes 129024 | tf_op jit(solution)/shard_map/psum | solution.py:740
  367.6 66.2 %all-reduce.5.cloned.1.call-done = f32[577,768]{1,0:T(8,128)} async-done(((f32[577,768]{1,0:T(8,128)}), f32[577,768]{1,0:T(8,128)}) %all-reduce.5.cloned.1.call-update) | async-done | bytes 1772560 | tf_op jit(solution)/shard_map/psum | solution.py:740
  433.8 4.2 multiply_subtract_fusion
  438.0 107.3 %reduce-scatter.3.cloned.1.call-done = bf16[1,96,768]{2,1,0:T(8,128)(2,1)} async-done(((bf16[32,96,768]{2,1,0:T(8,128)(2,1)}), bf16[1,96,768]{2,1,0:T(8,128)(2,1)}) %reduce-scatter.3.cloned.1.call-update) | async-done | bytes 147472 | tf_op jit(solution)/shard_map/reduce_scatter | solution.py:729
  546.9 9.3 %shampoo.2 = (f32[8,96,96]{2,1,0:T(8,128)}, f32[8,96,96]{2,1,0:T(8,128)}, f32[8,96,96]{2,1,0:T(8,128)}, f32[8,96,96]{2,1,0:T(8,128)}) custom-call(f32[1,96,768]{2,1,0:T(8,128)} %convert_element_type.24.grads_ref, f32[8,96,96]{2,1,0:T(8,128)} %left_ref.1, f32[8,96,96]{2,1,0:T(8,128)} %right_ref.1, f32[8,96,96]{2,1,0:T(8,128)} %w_ref.1), custom_call_target="tpu_custom_call" | custom-call | tf_op jit(solution)/shard_map/shampoo/pallas_call | solution.py:609
  556.3 104.0 %reduce-scatter.5.cloned.1.call-done = bf16[4,96,768]{2,1,0:T(8,128)(2,1)} async-done(((bf16[64,96,768]{2,1,0:T(8,128)(2,1)}), bf16[4,96,768]{2,1,0:T(8,128)(2,1)}) %reduce-scatter.5.cloned.1.call-update) | async-done | bytes 589840 | tf_op jit(solution)/shard_map/reduce_scatter | solution.py:725
  662.5 31.2 %shampoo.3 = (f32[32,96,96]{2,1,0:T(8,128)}, f32[32,96,96]{2,1,0:T(8,128)}, f32[32,96,96]{2,1,0:T(8,128)}, f32[32,96,96]{2,1,0:T(8,128)}) custom-call(f32[4,96,768]{2,1,0:T(8,128)} %convert_element_type.25.grads_ref, f32[32,96,96]{2,1,0:T(8,128)} %bitcast.46, f32[32,96,96]{2,1,0:T(8,128)} %bitcast.47, f32[32,96,96]{2,1,0:T(8,128)} %bitcast.41), custom_call_target="tpu_custom_call" | custom-call | tf_op jit(solution)/shard_map/shampoo/pallas_call | solution.py:609
  (82 shorter events, 41.6 us)
Async XLA Ops:
  7.2 6.2 copy-start.9
  7.2 70.6 %all-gather.3.cloned.1.call-start = ((), (), s32[]{:S(2)}) async-start(), calls=%async_computation.2 | async-start | bytes 4866048 | tf_op jit(solution)/shard_map/all_gather | solution.py:664
  9.0 151.9 %all-gather.5.cloned.1.call-start = ((), (), s32[]{:S(2)}) async-start(), calls=%async_computation.3 | async-start | bytes 10027008 | tf_op jit(solution)/shard_map/all_gather | solution.py:665
  12.7 421.2 %all-reduce.5.cloned.1.call-start = ((), (), s32[]{:S(2)}) async-start(), calls=%async_computation.6 | async-start | bytes 3588096 | tf_op jit(solution)/shard_map/psum | solution.py:740
  13.4 3.0 copy-start
  22.0 2.2 copy-start.1
  24.2 1.4 slice-start
  24.2 2.5 copy-start.3
  77.7 9.2 %copy-start.5 = (f32[2,3072]{1,0:T(2,128)S(1)}, f32[2,3072]{1,0:T(2,128)}, u32[]{:S(2)}) copy-start(f32[2,3072]{1,0:T(2,128)} %param.29) | copy-start | bytes 73732
  85.6 11.1 %collective-permute-start = (bf16[64,2304]{1,0:T(8,128)(2,1)S(1)}, bf16[64,2304]{1,0:T(8,128)(2,1)S(1)}, u32[]{:S(2)}, u32[]{:S(2)}) collective-permute-start(bf16[64,2304]{1,0:T(8,128)(2,1)S(1)} %slice.50), channel_id=1, source_target_pairs={{16,0},{17,1},{18,2},{19,3},{20,4},{21,5},{22,6},{23,7},{24,8},{25... | collective-permute-start | bytes 884744 | tf_op jit(solution)/shard_map/ppermute | solution.py:696
  121.6 47.3 %collective-permute-start.1 = (bf16[64,768]{1,0:T(8,128)(2,1)S(1)}, bf16[64,768]{1,0:T(8,128)(2,1)S(1)}, u32[]{:S(2)}, u32[]{:S(2)}) collective-permute-start(bf16[64,768]{1,0:T(8,128)(2,1)S(1)} %slice.51), channel_id=1, source_target_pairs={{0,16},{1,17},{2,18},{3,19},{4,20},{5,21},{6,22},{7,23},{8,24},{9,... | collective-permute-start | bytes 294920 | tf_op jit(solution)/shard_map/ppermute | solution.py:699
  168.9 0.6 copy-start.4
  227.7 6.8 collective-permute-start.2
  261.9 7.4 %collective-permute-start.3 = (bf16[3,64,768]{2,1,0:T(8,128)(2,1)S(1)}, bf16[3,64,768]{2,1,0:T(8,128)(2,1)S(1)}, u32[]{:S(2)}, u32[]{:S(2)}) collective-permute-start(bf16[3,64,768]{2,1,0:T(8,128)(2,1)S(1)} %slice.68), channel_id=1, source_target_pairs={{0,16},{1,17},{2,18},{3,19},{4,20},{5,21},{6,22},{7,23},{8,24},{9,... | collective-permute-start | bytes 884744 | tf_op jit(solution)/shard_map/ppermute | solution.py:708
  301.5 1.3 copy-start.2
  301.6 243.7 %reduce-scatter.3.cloned.1.call-start = ((), (), s32[]{:S(2)}) async-start(), calls=%async_computation.4 | async-start | bytes 4866048 | tf_op jit(solution)/shard_map/reduce_scatter | solution.py:729
  307.4 352.9 %reduce-scatter.5.cloned.1.call-start = ((), (), s32[]{:S(2)}) async-start(), calls=%async_computation.5 | async-start | bytes 10027008 | tf_op jit(solution)/shard_map/reduce_scatter | solution.py:725
  315.2 0.7 copy-start.10
  315.9 4.6 copy-start.8
  316.0 4.6 copy-start.11
  320.6 45.6 %copy-start.6 = (f32[13,768]{1,0:T(8,128)S(1)}, f32[13,768]{1,0:T(8,128)}, u32[]{:S(2)}) copy-start(f32[13,768]{1,0:T(8,128)} %param.28) | copy-start | bytes 119812
  320.7 46.3 %copy-start.7 = (f32[2,3072]{1,0:T(2,128)S(1)}, f32[2,3072]{1,0:T(2,128)}, u32[]{:S(2)}) copy-start(f32[2,3072]{1,0:T(2,128)} %param.30) | copy-start | bytes 73732
Sparse Core Ops, SparseCore 0:
  11.5 66.1 all-gather.2
  80.6 80.2 all-gather.4
  301.7 132.0 all-reduce.4
  439.1 106.1 reduce-scatter.2
  549.8 110.4 reduce-scatter.4

commit v2 on v1

v2 whole, which is shorter than its diff:
```python
import functools
import math

import jax
import jax.numpy as jnp
from jax import lax
from jax.experimental import pallas as pl
from jax.experimental.pallas import tpu as pltpu
from jax.sharding import PartitionSpec as P

HEADS = 12
TEXT = 64
NEWTON = 6
PAIR_LANES = 128
QUERY_TILE = 256
VMEM_LIMIT = 56 << 20

f32 = jnp.float32
bf16 = jnp.bfloat16
norm_eps = 1e-05
stat_decay = 0.5
matrix_rate = 0.25
moment_keep = 0.9
masked_score = -1e30


def dot_nn(left, right):
    return lax.dot_general(left, right, (((1,), (0,)), ((), ())), preferred_element_type=f32)


def dot_nt(left, right):
    return lax.dot_general(left, right, (((1,), (1,)), ((), ())), preferred_element_type=f32)


def dot_tn(left, right):
    return lax.dot_general(left, right, (((0,), (0,)), ((), ())), preferred_element_type=f32)


def params():
    return pltpu.CompilerParams(vmem_limit_bytes=VMEM_LIMIT)


def cost(microseconds):
    return pl.CostEstimate(flops=int(microseconds * 1e8), bytes_accessed=0, transcendentals=0)


def round_up(value, step):
    return (value + step - 1) // step * step


def whole(shape):
    return pl.BlockSpec(shape, lambda *ids: (0,) * len(shape))


SMEM_SPEC = pl.BlockSpec(memory_space=pltpu.SMEM)


def pack_kernel(up_ref, blocks_ref, out_ref):
    part = pl.program_id(0)
    parts = pl.num_programs(0)
    per_row = blocks_ref.shape[0] // parts
    pieces = []
    for i in range(per_row):
        at = jnp.where(up_ref[0] == 1, i * parts + part, part * per_row + i)
        pieces.append(blocks_ref[at])
    out_ref[0] = jnp.concatenate(pieces, axis=1).astype(bf16)


def pack_rows(is_up, blocks, per_row):
    count, size, _ = blocks.shape
    return pl.pallas_call(
        pack_kernel,
        grid=(count // per_row,),
        in_specs=[SMEM_SPEC, whole(blocks.shape)],
        out_specs=pl.BlockSpec((1, size, per_row * size), lambda i: (i, 0, 0)),
        out_shape=jax.ShapeDtypeStruct((count // per_row, size, per_row * size), bf16),
        compiler_params=params(),
        cost_estimate=cost(3),
        name="pack_rows",
    )(is_up, blocks)


def norm_rows(values):
    centred = values - jnp.mean(values, axis=-1, keepdims=True)
    spread = jnp.mean(centred * centred, axis=-1, keepdims=True)
    inv_std = lax.rsqrt(spread + norm_eps)
    return centred * inv_std, inv_std


def norm_input_grad(grad_out, normal, inv_std, gain):
    grad_norm = grad_out * gain
    mean_grad = jnp.mean(grad_norm, axis=-1, keepdims=True)
    mean_proj = jnp.mean(grad_norm * normal, axis=-1, keepdims=True)
    return inv_std * (grad_norm - mean_grad - normal * mean_proj)


def first_norm_kernel(row_ref, hidden_ref, vec_ref, first_ref):
    rows = hidden_ref.shape[0]
    normal, _ = norm_rows(hidden_ref[...])
    first_ref[...] = jnp.zeros(first_ref.shape, bf16)
    first = normal * vec_ref[0:1, :] + vec_ref[1:2, :]
    first_ref[pl.ds(pl.multiple_of(row_ref[0], 16), rows), :] = first.astype(bf16)


def first_norm(rows_info, hidden, vec, seq):
    return pl.pallas_call(
        first_norm_kernel,
        in_specs=[SMEM_SPEC, whole(hidden.shape), whole(vec.shape)],
        out_specs=whole((seq, hidden.shape[1])),
        out_shape=jax.ShapeDtypeStruct((seq, hidden.shape[1]), bf16),
        compiler_params=params(),
        cost_estimate=cost(4),
        name="first_norm",
    )(rows_info, hidden, vec)


def project_kernel(row_ref, first_ref, vec_ref, *refs):
    weight_refs, (qkv_ref, w_ref) = refs[:-2], refs[-2:]
    step = pl.program_id(0)
    if len(weight_refs) == 1:
        w_ref[...] = weight_refs[0][...]
    else:
        upper, upper_far, lower, lower_far = weight_refs
        half, size = upper.shape[3], 2 * upper.shape[3]
        on_one = row_ref[5] == 1
        for z in range(2):
            for y in range(2):
                for base, near, far in (
                    (0, upper[0, y, z], upper_far[0, y, z]),
                    (half, lower[y, 0, z], lower_far[y, 0, z]),
                ):
                    start = (4 * z + 2 * y) * size + base
                    w_ref[0, start : start + half, :] = jnp.where(on_one, far, near)
                    start += size
                    w_ref[0, start : start + half, :] = jnp.where(on_one, near, far)

    @pl.when(step < 3)
    def _():
        bias = jnp.where(step == 0, vec_ref[5:6, :], jnp.where(step == 2, vec_ref[6:7, :], 0.0))
        qkv_ref[...] = (dot_nn(first_ref[...], w_ref[0]) + bias).astype(bf16)


def project(rows_info, first, vec, attn_parts):
    seq, width = first.shape
    if len(attn_parts) == 1:
        weight_specs = [pl.BlockSpec((1, width, width), lambda i: (i, 0, 0))]
    else:
        half = attn_parts[0].shape[3]
        upper = pl.BlockSpec((1, 2, 2, half, width), lambda i: (i // 2, 0, i % 2, 0, 0))
        lower = pl.BlockSpec((2, 1, 2, half, width), lambda i: (0, i // 2, i % 2, 0, 0))
        weight_specs = [upper, upper, lower, lower]
    return pl.pallas_call(
        project_kernel,
        grid=(4,),
        in_specs=[SMEM_SPEC, whole((seq, width)), whole(vec.shape), *weight_specs],
        out_specs=[
            pl.BlockSpec((seq, width), lambda i: (0, jnp.minimum(i, 2))),
            pl.BlockSpec((1, width, width), lambda i: (i, 0, 0)),
        ],
        out_shape=[
            jax.ShapeDtypeStruct((seq, 3 * width), bf16),
            jax.ShapeDtypeStruct((4, width, width), bf16),
        ],
        compiler_params=params(),
        cost_estimate=cost(8),
        name="project",
    )(rows_info, first, vec, *attn_parts)


def key_bias(row_ref, seq):
    rows = lax.broadcasted_iota(jnp.int32, (seq, 1), 0)
    counts = jnp.logical_and(rows >= row_ref[1], rows < row_ref[2])
    return jnp.where(counts, 0.0, masked_score).astype(f32)


def transposed(values):
    return jnp.transpose(values.astype(f32), (1, 0)).astype(bf16)


def attend_kernel(row_ref, q_ref, k_ref, v_ref, ctx_ref, lse_ref, pair_ref):
    seq = q_ref.shape[0]
    half = PAIR_LANES // 2
    scale = half ** (-0.5)
    bias = key_bias(row_ref, seq)
    keys = k_ref[...]
    values_t = transposed(v_ref[...])
    for start in range(0, seq, QUERY_TILE):
        size = min(QUERY_TILE, seq - start)
        tile = slice(start, start + size)
        queries = q_ref[tile, :]
        lane = lax.broadcasted_iota(jnp.int32, (size, PAIR_LANES), 1)
        parts = []
        for head in range(2):
            own = (lane < half) == (head == 0)
            scores = dot_nt(keys, jnp.where(own, queries, jnp.zeros_like(queries))) * scale + bias
            top = jnp.max(scores, axis=0, keepdims=True)
            raised = jnp.exp(scores - top)
            total = jnp.sum(raised, axis=0, keepdims=True)
            probs = (raised * (1.0 / total)).astype(bf16)
            parts.append(dot_nn(values_t[half * head : half * (head + 1), :], probs))
            lse_ref[0, head : head + 1, tile] = top + jnp.log(total)
        context = jnp.transpose(jnp.concatenate(parts, axis=0), (1, 0)).astype(bf16)
        ctx_ref[tile, :] = context
        if start == 0:
            pair_ref[...] = context[: pair_ref.shape[0]]


def attend(rows_info, qkv):
    seq = qkv.shape[0]
    width = qkv.shape[1] // 3
    pairs = width // PAIR_LANES

    def column(base):
        return pl.BlockSpec((seq, PAIR_LANES), lambda i, base=base: (0, base + i))

    return pl.pallas_call(
        attend_kernel,
        grid=(pairs,),
        in_specs=[SMEM_SPEC, column(0), column(pairs), column(2 * pairs)],
        out_specs=[
            column(0),
            pl.BlockSpec((1, 8, seq), lambda i: (i, 0, 0)),
            pl.BlockSpec((TEXT, PAIR_LANES), lambda i: (0, i)),
        ],
        out_shape=[
            jax.ShapeDtypeStruct((seq, width), bf16),
            jax.ShapeDtypeStruct((pairs, 8, seq), f32),
            jax.ShapeDtypeStruct((TEXT, width), bf16),
        ],
        compiler_params=params(),
        cost_estimate=cost(22),
        name="attend",
    )(rows_info, qkv, qkv, qkv)


def attend_grad_kernel(
    row_ref, q_ref, k_ref, v_ref, g_ref, pair_ref, lse_ref, out_ref, dk_ref, dv_ref
):
    seq = q_ref.shape[0]
    half = PAIR_LANES // 2
    scale = half ** (-0.5)
    bias = key_bias(row_ref, seq)
    keys = k_ref[...]
    values = v_ref[...]
    keys_t = transposed(keys)
    for start in range(0, seq, QUERY_TILE):
        size = min(QUERY_TILE, seq - start)
        tile = slice(start, start + size)
        queries = q_ref[tile, :]
        row = lax.broadcasted_iota(jnp.int32, (size, 1), 0) + start
        counts = jnp.logical_and(row >= row_ref[1], row < row_ref[2])
        grads = g_ref[tile, :]
        if start == 0:
            grads = jnp.concatenate([pair_ref[...], grads[pair_ref.shape[0] :]], axis=0)
        grads = jnp.where(counts, grads, jnp.zeros((size, PAIR_LANES), bf16))
        lane = lax.broadcasted_iota(jnp.int32, (size, PAIR_LANES), 1)
        parts = []
        for head in range(2):
            own = (lane < half) == (head == 0)
            own_q = jnp.where(own, queries, jnp.zeros_like(queries))
            own_g = jnp.where(own, grads, jnp.zeros_like(grads))
            scores = dot_nt(keys, own_q) * scale + bias
            probs = jnp.exp(scores - lse_ref[0, head : head + 1, tile])
            grad_probs = dot_nt(values, own_g)
            row_dot = jnp.sum(probs * grad_probs, axis=0, keepdims=True)
            grad_scores = (probs * (grad_probs - row_dot)).astype(bf16)
            grad_v = dot_nn(probs.astype(bf16), own_g)
            grad_k = dot_nn(grad_scores, own_q)
            if start == 0 and head == 0:
                dv_ref[...] = grad_v
                dk_ref[...] = grad_k
            else:
                dv_ref[...] += grad_v
                dk_ref[...] += grad_k
            parts.append(dot_nn(keys_t[half * head : half * (head + 1), :], grad_scores))
        grad_q = jnp.transpose(jnp.concatenate(parts, axis=0) * scale, (1, 0))
        out_ref[0, tile, :] = grad_q.astype(bf16)
    out_ref[1] = (dk_ref[...] * scale).astype(bf16)
    out_ref[2] = dv_ref[...].astype(bf16)


def attend_grad(rows_info, qkv, grad_ctx, pair_grad, lse):
    seq = qkv.shape[0]
    width = qkv.shape[1] // 3
    pairs = width // PAIR_LANES

    def column(base):
        return pl.BlockSpec((seq, PAIR_LANES), lambda i, base=base: (0, base + i))

    return pl.pallas_call(
        attend_grad_kernel,
        grid=(pairs,),
        in_specs=[
            SMEM_SPEC,
            column(0),
            column(pairs),
            column(2 * pairs),
            column(0),
            pl.BlockSpec((TEXT, PAIR_LANES), lambda i: (0, i)),
            pl.BlockSpec((1, 8, seq), lambda i: (i, 0, 0)),
        ],
        out_specs=pl.BlockSpec((3, seq, PAIR_LANES), lambda i: (0, 0, i)),
        out_shape=jax.ShapeDtypeStruct((3, seq, width), bf16),
        scratch_shapes=[pltpu.VMEM((seq, PAIR_LANES), f32)] * 2,
        compiler_params=params(),
        cost_estimate=cost(25),
        name="attend_grad",
    )(rows_info, qkv, qkv, qkv, grad_ctx, pair_grad, lse)


def gelu_pair(values):
    size = jnp.abs(values)
    tail = 1.0 / (1.0 + (0.3275911 * 0.5**0.5) * size)
    poly = tail * (
        0.254829592
        + tail * (-0.284496736 + tail * (1.421413741 + tail * (-1.453152027 + tail * 1.061405429)))
    )
    bell = jnp.exp(-0.5 * values * values)
    upper = 0.5 * poly * bell
    share = jnp.where(values >= 0.0, 1.0 - upper, upper)
    return values * share, share + values * bell * ((2.0 * math.pi) ** -0.5)


def split_by_core(row_ref, grad, shape):
    size, width = shape[-2:]
    blocks = grad.reshape(-1, 2, size, width)
    near, far = blocks[:, 0], blocks[:, 1]
    on_one = row_ref[5] == 1
    return jnp.where(on_one, far, near).reshape(shape), jnp.where(on_one, near, far).reshape(shape)


def expert_chunk(
    row_ref, second, gbranch, upb, up_ref, down_ref, grad_refs, dupb_ref, branch, gsecond, scratch, begin
):
    pre, gact, act, gpre = scratch
    rows, width = act.shape
    tile = 16
    up = up_ref[...].reshape(width, width)
    down = down_ref[...].reshape(width, width)
    pre[...] = dot_nn(second[...], up)
    gact[...] = dot_nt(gbranch[...], down)

    def body(i, total):
        at = pl.ds(pl.multiple_of(i * tile, tile), tile)
        value, slope = gelu_pair(pre[at, :] + upb[...])
        act[at, :] = value.astype(bf16)
        rounded = (gact[at, :] * slope).astype(bf16)
        gpre[at, :] = rounded
        return total + rounded.astype(f32)

    total = lax.fori_loop(0, rows // tile, body, jnp.zeros((tile, width), f32))
    dupb_ref[...] = jnp.sum(total, axis=0, keepdims=True)
    for which, grad in enumerate(
        (dot_tn(second[...], gpre[...]), dot_tn(act[...], gbranch[...]))
    ):
        grad, shape = grad.astype(bf16), grad_refs[0].shape[1:]
        if len(grad_refs) == 1:
            grad_refs[0][which] = grad.reshape(shape)
        else:
            grad_refs[0][which], grad_refs[1][which] = split_by_core(row_ref, grad, shape)
    own_branch = dot_nn(act[...], down)
    own_gsecond = dot_nt(gpre[...], up)

    @pl.when(begin)
    def _():
        branch[...] = own_branch
        gsecond[...] = own_gsecond

    @pl.when(jnp.logical_not(begin))
    def _():
        branch[...] += own_branch
        gsecond[...] += own_gsecond


def expert_begin_kernel(
    row_ref,
    ctx_ref,
    pair_ref,
    hidden_ref,
    cot_ref,
    vec_ref,
    upb_ref,
    wo_ref,
    up_ref,
    down_ref,
    own_ctx,
    middle,
    second,
    gbranch,
    branch,
    gsecond,
    grad_ref,
    dvec_ref,
    dupb_ref,
    *scratch,
):
    step = pl.program_id(0)
    rows, width = hidden_ref.shape
    tile = 16

    @pl.when(step == 0)
    def _():
        own_ctx[...] = ctx_ref[pl.ds(pl.multiple_of(row_ref[0], 16), rows), :]

        @pl.when(row_ref[3] == 1)
        def _():
            own_ctx[0 : pair_ref.shape[0], :] = pair_ref[...]

        middle[...] = dot_nn(own_ctx[...], wo_ref[0])

        def body(i, total):
            at = pl.ds(pl.multiple_of(i * tile, tile), tile)
            mid = hidden_ref[at, :] + (middle[at, :] + vec_ref[7:8, :])
            middle[at, :] = mid
            normal, _ = norm_rows(mid)
            second[at, :] = (normal * vec_ref[2:3, :] + vec_ref[3:4, :]).astype(bf16)
            row = lax.broadcasted_iota(jnp.int32, (tile, 1), 0) + i * tile
            kept = jnp.where(row < row_ref[4], cot_ref[at, :], 0.0)
            rounded = kept.astype(bf16)
            gbranch[at, :] = rounded
            return total + rounded.astype(f32)

        total = lax.fori_loop(0, rows // tile, body, jnp.zeros((tile, width), f32))
        dvec_ref[...] = jnp.zeros(dvec_ref.shape, f32)
        dvec_ref[2:3, :] = jnp.sum(total, axis=0, keepdims=True)

    expert_chunk(
        row_ref,
        second,
        gbranch,
        upb_ref,
        up_ref,
        down_ref,
        (grad_ref,),
        dupb_ref,
        branch,
        gsecond,
        scratch,
        step == 0,
    )


def expert_end_kernel(
    row_ref,
    own_ctx,
    middle,
    second,
    gbranch,
    branch_in,
    gsecond_in,
    dvec_in,
    cot_ref,
    vec_ref,
    upb_ref,
    wo_ref,
    up_ref,
    down_ref,
    out_ref,
    gmid_ref,
    gctx_ref,
    pair_ref,
    dwo_ref,
    keep_ref,
    send_ref,
    dvec_ref,
    dupb_ref,
    branch,
    gsecond,
    rounded_ref,
    *scratch,
):
    step = pl.program_id(0)
    rows, width = middle.shape
    out_rows = out_ref.shape[0]
    tile = 16

    @pl.when(step == 0)
    def _():
        branch[...] = branch_in[...]
        gsecond[...] = gsecond_in[...]

    expert_chunk(
        row_ref,
        second,
        gbranch,
        upb_ref,
        up_ref,
        down_ref,
        (keep_ref, send_ref),
        dupb_ref,
        branch,
        gsecond,
        scratch,
        step < 0,
    )

    @pl.when(step == pl.num_programs(0) - 1)
    def _():
        def body(i, totals):
            at = pl.ds(pl.multiple_of(i * tile, tile), tile)
            mid = middle[at, :]
            normal, inv_std = norm_rows(mid)
            grad_out = gsecond[at, :]
            row = lax.broadcasted_iota(jnp.int32, (tile, 1), 0) + i * tile
            kept = row < row_ref[4]
            branch[at, :] = jnp.where(kept, mid + (branch[at, :] + vec_ref[4:5, :]), 0.0)
            grad_in = norm_input_grad(grad_out, normal, inv_std, vec_ref[2:3, :])
            grad_mid = jnp.where(kept, cot_ref[at, :], 0.0) + grad_in
            gmid_ref[at, :] = grad_mid
            rounded = grad_mid.astype(bf16)
            rounded_ref[at, :] = rounded
            return (
                totals[0] + grad_out * normal,
                totals[1] + grad_out,
                totals[2] + rounded.astype(f32),
            )

        zero = jnp.zeros((tile, width), f32)
        gains, shifts, biases = lax.fori_loop(0, rows // tile, body, (zero, zero, zero))
        dvec_ref[...] = dvec_in[...]
        dvec_ref[0:1, :] = jnp.sum(gains, axis=0, keepdims=True)
        dvec_ref[1:2, :] = jnp.sum(shifts, axis=0, keepdims=True)
        dvec_ref[3:4, :] = jnp.sum(biases, axis=0, keepdims=True)
        out_ref[...] = branch[0:out_rows, :]
        dwo_ref[...] = dot_tn(own_ctx[...], rounded_ref[...]).astype(bf16)
        grad_ctx = dot_nt(rounded_ref[...], wo_ref[0]).astype(bf16)
        gctx_ref[...] = jnp.zeros(gctx_ref.shape, bf16)
        gctx_ref[pl.ds(pl.multiple_of(row_ref[0], 16), rows), :] = grad_ctx
        pair_ref[...] = grad_ctx[: pair_ref.shape[0]]


def expert_specs(rows, width, ffn_parts, half):
    _, row_blocks, chunks, size, _ = ffn_parts.shape
    base = half * (chunks // 2)

    def weights(which):
        return pl.BlockSpec(
            (1, row_blocks, 1, size, width), lambda i: (which, 0, base + i, 0, 0)
        )

    inputs = [
        pl.BlockSpec((1, width), lambda i: (0, base + i)),
        pl.BlockSpec((1, width, width), lambda i: (3, 0, 0)),
        weights(0),
        weights(1),
    ]
    outs = 1 + half
    per_out = row_blocks // outs
    grad_spec = [pl.BlockSpec((2, per_out, 1, size, width), lambda i: (0, 0, i, 0, 0))] * outs
    grad_shape = [jax.ShapeDtypeStruct((2, per_out, chunks // 2, size, width), bf16)] * outs
    bias_spec = pl.BlockSpec((1, width), lambda i: (0, i))
    bias_shape = jax.ShapeDtypeStruct((1, chunks // 2 * width), f32)
    scratch = [pltpu.VMEM((rows, width), f32)] * 2 + [pltpu.VMEM((rows, width), bf16)] * 2
    return inputs, (grad_spec, grad_shape), (bias_spec, bias_shape), scratch


def expert_begin(rows_info, ctx, pair_ctx, hidden, cot, vec, up_bias, w_attn, ffn_parts):
    rows, width = hidden.shape
    inputs, grads, biases, scratch = expert_specs(rows, width, ffn_parts, 0)
    kept = [bf16, f32, bf16, bf16, f32, f32]
    return pl.pallas_call(
        expert_begin_kernel,
        grid=(ffn_parts.shape[2] // 2,),
        in_specs=[
            SMEM_SPEC,
            whole(ctx.shape),
            whole(pair_ctx.shape),
            whole(hidden.shape),
            whole(cot.shape),
            whole(vec.shape),
            *inputs,
        ],
        out_specs=[whole((rows, width))] * 6 + [*grads[0], whole((8, width)), biases[0]],
        out_shape=[jax.ShapeDtypeStruct((rows, width), kind) for kind in kept]
        + [*grads[1], jax.ShapeDtypeStruct((8, width), f32), biases[1]],
        scratch_shapes=scratch,
        compiler_params=params(),
        cost_estimate=cost(28),
        name="expert_begin",
    )(rows_info, ctx, pair_ctx, hidden, cot, vec, up_bias, w_attn, ffn_parts, ffn_parts)


def expert_end(rows_info, kept, late, cot, vec, up_bias, w_attn, ffn_parts, seq, out_rows):
    rows, width = cot.shape
    inputs, grads, biases, scratch = expert_specs(rows, width, ffn_parts, 1)
    return pl.pallas_call(
        expert_end_kernel,
        grid=(ffn_parts.shape[2] // 2,),
        in_specs=[SMEM_SPEC]
        + [whole((rows, width))] * 6
        + [whole(late.shape), whole(cot.shape), whole(vec.shape), *inputs],
        out_specs=[
            whole((out_rows, width)),
            whole((rows, width)),
            whole((seq, width)),
            whole((TEXT, width)),
            whole((width, width)),
            *grads[0],
            whole((8, width)),
            biases[0],
        ],
        out_shape=[
            jax.ShapeDtypeStruct((out_rows, width), f32),
            jax.ShapeDtypeStruct((rows, width), f32),
            jax.ShapeDtypeStruct((seq, width), bf16),
            jax.ShapeDtypeStruct((TEXT, width), bf16),
            jax.ShapeDtypeStruct((width, width), bf16),
            *grads[1],
            jax.ShapeDtypeStruct((8, width), f32),
            biases[1],
        ],
        scratch_shapes=[
            pltpu.VMEM((rows, width), f32),
            pltpu.VMEM((rows, width), f32),
            pltpu.VMEM((rows, width), bf16),
            *scratch,
        ],
        compiler_params=params(),
        cost_estimate=cost(30),
        name="expert_end",
    )(rows_info, *kept, late, cot, vec, up_bias, w_attn, ffn_parts, ffn_parts)


def project_grad_kernel(
    row_ref, dqkv_ref, first_ref, w_ref, dwo_ref, keep_ref, send_ref, gfirst, pair_ref, sums_ref
):
    step = pl.program_id(0)

    def put(grad):
        keep_ref[0], send_ref[0] = split_by_core(row_ref, grad, keep_ref.shape[1:])

    @pl.when(step < 3)
    def _():
        own = dqkv_ref[0]
        put(dot_tn(first_ref[...], own).astype(bf16))
        share = dot_nt(own, w_ref[0])
        sums = jnp.sum(own.astype(f32), axis=0, keepdims=True)

        @pl.when(step == 0)
        def _():
            gfirst[...] = share
            sums_ref[...] = jnp.zeros(sums_ref.shape, f32)
            sums_ref[0:1, :] = sums

        @pl.when(step > 0)
        def _():
            gfirst[...] += share
            sums_ref[1:2, :] = sums

    @pl.when(step == 3)
    def _():
        put(dwo_ref[...])
        pair_ref[...] = gfirst[0 : pair_ref.shape[0], :]


def project_grad(rows_info, dqkv, first, w_attn, grad_wo, size):
    seq, width = first.shape
    pairs = width // size // 2
    part = pl.BlockSpec((1, pairs, size, width), lambda i: (i, 0, 0, 0))

    def early_index(i):
        return (jnp.minimum(i, 2), 0, 0)

    return pl.pallas_call(
        project_grad_kernel,
        grid=(4,),
        in_specs=[
            SMEM_SPEC,
            pl.BlockSpec((1, seq, width), early_index),
            whole((seq, width)),
            pl.BlockSpec((1, width, width), early_index),
            whole(grad_wo.shape),
        ],
        out_specs=[part, part, whole((seq, width)), whole((TEXT, width)), whole((8, width))],
        out_shape=[
            jax.ShapeDtypeStruct((4, pairs, size, width), bf16),
            jax.ShapeDtypeStruct((4, pairs, size, width), bf16),
            jax.ShapeDtypeStruct((seq, width), f32),
            jax.ShapeDtypeStruct((TEXT, width), f32),
            jax.ShapeDtypeStruct((8, width), f32),
        ],
        compiler_params=params(),
        cost_estimate=cost(15),
        name="project_grad",
    )(rows_info, dqkv, first, w_attn, grad_wo)


def first_grad_kernel(
    row_ref,
    gfirst_ref,
    pair_ref,
    hidden_ref,
    gmid_ref,
    vec_ref,
    sums_ref,
    late_ref,
    upb_ref,
    pos_ref,
    out_ref,
    small_ref,
    own,
):
    rows, width = hidden_ref.shape
    tile = 16
    own[...] = gfirst_ref[pl.ds(pl.multiple_of(row_ref[0], 16), rows), :]

    @pl.when(row_ref[3] == 1)
    def _():
        own[0 : pair_ref.shape[0], :] = pair_ref[...]

    def body(i, totals):
        at = pl.ds(pl.multiple_of(i * tile, tile), tile)
        normal, inv_std = norm_rows(hidden_ref[at, :])
        grad_out = own[at, :]
        grad_in = norm_input_grad(grad_out, normal, inv_std, vec_ref[0:1, :])
        own[at, :] = gmid_ref[at, :] + grad_in
        return totals[0] + grad_out * normal, totals[1] + grad_out

    zero = jnp.zeros((tile, width), f32)
    gains, shifts = lax.fori_loop(0, rows // tile, body, (zero, zero))
    out_ref[...] = own[0 : out_ref.shape[0], :]
    own_rows = (
        jnp.sum(gains, axis=0, keepdims=True),
        jnp.sum(shifts, axis=0, keepdims=True),
        late_ref[0:1, :],
        late_ref[1:2, :],
        late_ref[2:3, :],
    )
    row = lax.broadcasted_iota(jnp.int32, (16, width), 0)
    top = jnp.where(row == 0, sums_ref[0:1, :], 0.0)
    top = jnp.where(row == 1, sums_ref[1:2, :], top)
    top = jnp.where(row == 2, late_ref[3:4, :], top)
    for i, value in enumerate(own_rows):
        top = jnp.where(row == 3 + 5 * row_ref[3] + i, value, top)
    small_ref[0:16, :] = top
    row = lax.broadcasted_iota(jnp.int32, (8, width), 0)
    bias = jnp.zeros((8, width), f32)
    for i in range(upb_ref.shape[0]):
        bias = jnp.where(row == upb_ref.shape[0] * row_ref[3] + i, upb_ref[i : i + 1, :], bias)
    small_ref[16:24, :] = bias
    grads = own[...]
    high = grads.astype(bf16)
    low = (grads - high.astype(f32)).astype(bf16)
    table = lax.broadcasted_iota(jnp.int32, (rows, rows), 0)
    chosen = jnp.where(row_ref[3] == 0, pos_ref[...], -1) == table
    chosen = jnp.where(chosen, 1.0, 0.0).astype(bf16)
    small_ref[24 : 24 + rows, :] = dot_nn(chosen, high) + dot_nn(chosen, low)
    small_ref[24 + rows :, :] = jnp.zeros((small_ref.shape[0] - 24 - rows, width), f32)


def first_grad(
    rows_info, gfirst, pair_grad, hidden, grad_middle, vec, sums, late, up_bias, pos, out_rows
):
    rows, width = hidden.shape
    small = round_up(24 + rows, 128)
    args = (gfirst, pair_grad, hidden, grad_middle, vec, sums, late, up_bias, pos)
    return pl.pallas_call(
        first_grad_kernel,
        in_specs=[SMEM_SPEC] + [whole(arg.shape) for arg in args],
        out_specs=[whole((out_rows, width)), whole((small, width))],
        out_shape=[
            jax.ShapeDtypeStruct((out_rows, width), f32),
            jax.ShapeDtypeStruct((small, width), f32),
        ],
        scratch_shapes=[pltpu.VMEM((rows, width), f32)],
        compiler_params=params(),
        cost_estimate=cost(8),
        name="first_grad",
    )(rows_info, *args)


def widen(values):
    rows, cols = values.shape
    return jnp.concatenate([values, jnp.zeros((rows, PAIR_LANES - cols), f32)], axis=1)


def split_parts(values):
    high = values.astype(bf16)
    return high, (values - high.astype(f32)).astype(bf16)


def left_parts(values):
    return jnp.concatenate(split_parts(values), axis=1)


def right_parts(values):
    high, low = split_parts(values)
    rows, cols = high.shape
    gap = jnp.zeros((cols - rows, cols), bf16)
    near = jnp.concatenate([high, gap, high, gap], axis=0)
    far = jnp.concatenate([low, gap, jnp.zeros((cols, cols), bf16)], axis=0)
    return jnp.concatenate([near, far], axis=1)


def times(left, right):
    both = dot_nn(left, right)
    return both[:, :PAIR_LANES] + both[:, PAIR_LANES:]


def inverse_roots(stats, identity):
    size = stats[0].shape[0]
    mats, factors = [], []
    for stat in stats:
        norm = jnp.sqrt(jnp.sum(stat * stat, keepdims=True))
        mats.append(stat * (1.0 / norm))
        factors.append(lax.rsqrt(jnp.sqrt(norm)))
    for iteration in range(NEWTON):
        steps = [1.25 * identity - 0.25 * mat for mat in mats]
        if iteration == 0:
            factors = [step * factor for step, factor in zip(steps, factors)]
            squares = [times(left_parts(step), right_parts(step)) for step in steps]
        elif iteration < NEWTON - 1:
            both = [
                times(
                    jnp.concatenate([left_parts(step), left_parts(factor)], axis=0),
                    right_parts(step),
                )
                for step, factor in zip(steps, factors)
            ]
            squares = [pair[:size] for pair in both]
            factors = [pair[size:] for pair in both]
        else:
            return [
                times(left_parts(factor), right_parts(step)) for step, factor in zip(steps, factors)
            ]
        fourths = [times(left_parts(square), right_parts(square)) for square in squares]
        mats = [times(left_parts(fourth), right_parts(mat)) for fourth, mat in zip(fourths, mats)]


def shampoo_kernel(group, part, parts, grad_count, earlier, up_ref, *refs):
    grad_refs = refs[:grad_count]
    left_ref, right_ref, w_ref = refs[grad_count : grad_count + 3]
    outs = refs[grad_count + 3 + earlier : grad_count + 7 + earlier]
    results, sems = refs[-2:]
    _, count, size, _ = left_ref.shape
    row = lax.broadcasted_iota(jnp.int32, (size, PAIR_LANES), 0)
    col = lax.broadcasted_iota(jnp.int32, (size, PAIR_LANES), 1)
    identity = (row == col).astype(f32)
    copies = []

    def store(kind, i, at, value):
        results[kind, i] = value
        copy = pltpu.make_async_copy(results.at[kind, i], outs[kind].at[at], sems.at[kind, i])
        copy.start()
        copies.append(copy)

    for base in range(0, count, group):
        places, stats, grads = [], [], []
        for i in range(base, base + group):
            at = jnp.where(up_ref[0] == 1, i * parts + part, part * count + i)
            places.append(at)
            span = slice(i * size, (i + 1) * size)
            grad = grad_refs[0][0, :, span].astype(f32)
            for ref in grad_refs[1:]:
                grad = grad + ref[0, :, span].astype(f32)
            store(0, i, at, grad)
            grad = widen(grad)
            grad_t = widen(jnp.transpose(grad, (1, 0))[:size])
            grads.append(grad)
            outer = times(left_parts(grad), right_parts(grad_t))
            inner = times(left_parts(grad_t), right_parts(grad))
            left_new = stat_decay * left_ref[0, i] + (1.0 - stat_decay) * outer[:, :size]
            right_new = stat_decay * right_ref[0, i] + (1.0 - stat_decay) * inner[:, :size]
            store(1, i, at, left_new)
            store(2, i, at, right_new)
            stats += [widen(left_new), widen(right_new)]
        roots = inverse_roots(stats, identity)
        for i, at in enumerate(places):
            half_way = times(left_parts(roots[2 * i]), right_parts(grads[i]))
            update = times(left_parts(half_way), right_parts(roots[2 * i + 1]))
            store(3, base + i, at, w_ref[0, base + i] - matrix_rate * update[:, :size])
    for copy in copies:
        copy.wait()


def shampoo(is_up, part, at, grad_rows, lefts, rights, weights, earlier=()):
    parts, count, size, _ = lefts.shape
    span = count * size
    blocks = pl.BlockSpec((1, count, size, size), lambda i: (part, 0, 0, 0))
    shape = jax.ShapeDtypeStruct((parts * count, size, size), f32)
    anywhere = pl.BlockSpec(memory_space=pl.ANY)
    first_earlier = 4 + len(grad_rows)
    kernel = functools.partial(
        shampoo_kernel, math.gcd(count, 4), part, parts, len(grad_rows), len(earlier)
    )
    return pl.pallas_call(
        kernel,
        grid=(1,),
        in_specs=[SMEM_SPEC]
        + [pl.BlockSpec((1, size, span), lambda i: (at, 0, 0))] * len(grad_rows)
        + [blocks] * 3
        + [anywhere] * len(earlier),
        out_specs=[anywhere] * 4,
        out_shape=[shape] * 4,
        scratch_shapes=[
            pltpu.VMEM((4, count, size, size), f32),
            pltpu.SemaphoreType.DMA((4, count)),
        ],
        input_output_aliases={first_earlier + i: i for i in range(len(earlier))},
        compiler_params=params(),
        cost_estimate=cost(9),
        name="shampoo",
    )(is_up, *grad_rows, lefts, rights, weights, *earlier)


CORE, Y, Z_LOW, Z_HIGH = 1, 2, 4, 8


def flip(values, bits):
    size = lax.axis_size("dp")
    return lax.ppermute(values, "dp", [(i, i ^ bits) for i in range(size)])


def flip_mod(values):
    return lax.ppermute(values, "mod", [(0, 1), (1, 0)])


def in_order(bit, own, other):
    return jnp.stack([jnp.where(bit == 1, other, own), jnp.where(bit == 1, own, other)])


def place():
    index = lax.axis_index("dp")
    return index % 2, index // 2 % 2, index // 4


def sync(*values):
    return lax.optimization_barrier(values)


def pick(values, index, axis):
    return lax.dynamic_index_in_dim(values, index, axis, keepdims=False)


def plus(left, right):
    return (left.astype(f32) + right.astype(f32)).astype(bf16)


def square_parts(blocks, rows, cols):
    size = blocks.shape[-1]
    shaped = blocks.reshape(rows, cols, size, size)
    return jnp.swapaxes(shaped, 1, 2).reshape(rows, size, cols * size)


def parts_to_blocks(parts):
    rows, size, span = parts.shape
    shaped = parts.reshape(rows, size, span // size, size)
    return jnp.swapaxes(shaped, 1, 2).reshape(-1, size, size)


def local(
    stream_in,
    cotangent,
    patch_count,
    pos_index,
    attn_blocks,
    attn_left,
    attn_right,
    ffn_blocks,
    ffn_left,
    ffn_right,
    vectors,
    vectors_mom,
    ffn_bias,
    ffn_bias_mom,
    pos_table,
    pos_mom,
):
    size = attn_blocks.shape[-1]
    width = vectors.shape[1]
    hidden_units = ffn_bias.shape[1]
    slots = stream_in.shape[2]
    row_blocks = width // size
    chunks = hidden_units // width
    rows = round_up(slots, 16)
    seq = round_up(slots + TEXT, 32)
    by_rows = lax.axis_size("dp") == 16 and attn_blocks.shape[0] == row_blocks
    modality = lax.axis_index("mod")
    is_text = modality == 1
    image_flag = (1 - modality).astype(f32)
    along = lax.axis_index("dp")
    is_up = jnp.where(along < lax.axis_size("dp") // 2, 1, 0).astype(jnp.int32)[None]
    is_not = jnp.zeros((1,), jnp.int32)

    core, y, z = place()
    to_image = [(1, 0)]
    to_text = [(0, 1)]

    if by_rows:
        own_attn = pack_rows(is_not, attn_blocks, row_blocks)[0]
        along_z = [flip(own_attn, bits) for bits in (Z_LOW, Z_HIGH, Z_LOW | Z_HIGH)]
        ffn_rows = pack_rows(is_up, ffn_blocks[0], row_blocks)

    own_vec = lax.dynamic_slice_in_dim(vectors, 3 + 5 * modality, 5, 0)
    vec = jnp.concatenate([own_vec, vectors[0:3]], axis=0)
    up_bias = lax.dynamic_index_in_dim(ffn_bias, modality, 0, keepdims=False)
    up_bias = jnp.swapaxes(up_bias.reshape(row_blocks, chunks, size), 0, 1).reshape(1, hidden_units)
    count = patch_count[0]
    offset = TEXT * (1 - modality)
    first_key = jnp.where(is_text, TEXT, 0)
    end_key = jnp.where(is_text, slots, TEXT + count)
    kept_rows = jnp.where(is_text, slots, count)
    own_core = core if by_rows else 0 * along
    rows_info = jnp.stack([offset, first_key, end_key, modality, kept_rows, own_core])
    rows_info = rows_info.astype(jnp.int32)
    pad = ((0, rows - slots), (0, 0))
    hidden = stream_in[0, 0] + image_flag * jnp.take(pos_table, pos_index[0], axis=0)
    hidden = jnp.pad(hidden, pad)
    pos = jnp.pad(pos_index[0], pad[0], constant_values=-1)[None]
    if by_rows:
        along_z, ffn_rows, hidden, cotangent = sync(along_z, ffn_rows, hidden, cotangent)
        ffn_parts = lax.all_gather(ffn_rows, "dp", axis=0, tiled=True)
        ffn_parts = ffn_parts.reshape(2, row_blocks, chunks, size, width)
        near = in_order(z % 2, own_attn, along_z[0])
        far = in_order(z % 2, along_z[1], along_z[2])
        attn_z = in_order(z // 2, near, far).reshape(4, size, width)
        upper, lower = attn_z[:, : size // 2], attn_z[:, size // 2 :]
        upper_y, lower_x = flip(upper, Y), flip_mod(lower)
    first = first_norm(rows_info, hidden, vec, seq)
    pair_first = lax.ppermute(first[:TEXT], "mod", to_image)
    if by_rows:
        upper_y, lower_x, first, pair_first, cotangent = sync(
            upper_y, lower_x, first, pair_first, cotangent
        )
        upper, lower = in_order(y, upper, upper_y), in_order(modality, lower, lower_x)
        upper_x, lower_y = flip_mod(upper), flip(lower, Y)
    first = lax.dynamic_update_slice(first, jnp.where(is_text, first[:TEXT], pair_first), (0, 0))
    cot = jnp.pad(cotangent[0, 0], pad)

    def by_parts(blocks):
        by_chunk = blocks.reshape(chunks, -1, size, size)
        spread = jnp.swapaxes(blocks.reshape(-1, chunks, size, size), 0, 1)
        return jnp.where(is_up[0] == 1, spread, by_chunk)

    if by_rows:
        ffn_old = [by_parts(part[0]) for part in (ffn_left, ffn_right, ffn_blocks)]
        upper_x, lower_y, first, cot, ffn_old = sync(upper_x, lower_y, first, cot, ffn_old)
        upper, lower = in_order(modality, upper, upper_x), in_order(y, lower, lower_y)
        attn_parts = [upper, flip(upper, CORE), lower, flip(lower, CORE)]
    else:
        attn_all = lax.all_gather(attn_blocks.astype(bf16), ("mod", "dp"), axis=0, tiled=True)
        attn_parts = [square_parts(attn_all, 4 * row_blocks, row_blocks).reshape(4, width, width)]
        ffn_all = lax.all_gather(ffn_blocks[0].astype(bf16), "dp", axis=0, tiled=True)
        shape = (2, row_blocks, row_blocks, chunks, size, size)
        up = ffn_all.reshape(shape)[0].transpose(0, 2, 3, 1, 4)
        down = ffn_all.reshape(2, row_blocks, chunks, row_blocks, size, size)[1]
        down = down.transpose(0, 1, 3, 2, 4)
        ffn_parts = jnp.stack([p.reshape(row_blocks, chunks, size, width) for p in (up, down)])

    qkv, w_attn = project(rows_info, first, vec, attn_parts)
    ctx, lse, pair_ctx = attend(rows_info, qkv)
    pair_ctx = lax.ppermute(pair_ctx, "mod", to_text)
    *kept, grad_1, late_vec, up_bias_grad_1 = expert_begin(
        rows_info, ctx, pair_ctx, hidden, cot, vec, up_bias, w_attn, ffn_parts
    )
    ended = expert_end(rows_info, kept, late_vec, cot, vec, up_bias, w_attn, ffn_parts, seq, slots)
    stream_out, grad_middle, grad_ctx, pair_grad, grad_wo, keep_2, send_2, late_vec, up_bias_grad_2 = ended
    pair_grad = lax.ppermute(pair_grad, "mod", to_image)

    def along_z_of(parts):
        return [flip(part, bits * Z_LOW) for bits, part in enumerate(parts) if bits]

    if by_rows:
        ffn_1 = lax.psum_scatter(
            grad_1.reshape(-1, chunks // 2, size, width), "dp", scatter_dimension=0, tiled=True
        )[0]
        got_2 = flip(send_2, CORE)
        pair_grad, got_2, grad_ctx = sync(pair_grad, got_2, grad_ctx)
        both = plus(keep_2, got_2).reshape((4, 2) + keep_2.shape[2:])
        keep_2, send_2, grad_ctx = sync(pick(both, y, 1), pick(both, 1 - y, 1), grad_ctx)
        got_2 = flip(send_2, Y)
    grad_qkv = attend_grad(rows_info, qkv, grad_ctx, pair_grad, lse)
    if by_rows:
        got_2, grad_qkv = sync(got_2, grad_qkv)
        both = plus(keep_2, got_2)
        ffn_2 = [pick(both, z ^ bits, 0) for bits in range(4)]
        ffn_2, grad_qkv = sync(ffn_2, grad_qkv)
        got_2 = along_z_of(ffn_2)
    projected = project_grad(rows_info, grad_qkv, first, w_attn, grad_wo, size)
    if by_rows:
        projected, ffn_1, got_2 = sync(projected, ffn_1, got_2)
    attn_keep, attn_send, grad_first, pair_first_grad, sums = projected
    pair_first_grad = lax.ppermute(pair_first_grad, "mod", to_text)
    up_bias_grad = jnp.concatenate([up_bias_grad_1, up_bias_grad_2], axis=1)
    up_bias_grad = jnp.swapaxes(up_bias_grad.reshape(chunks, row_blocks, size), 0, 1)
    if by_rows:
        attn_got = flip(attn_send, CORE)
        attn_got, pair_first_grad = sync(attn_got, pair_first_grad)
        both = plus(attn_keep, attn_got).reshape(2, 4, 2, size, width)
        upper, lower = both[..., : size // 2, :], both[..., size // 2 :, :]
        upper_keep, upper_send = pick(upper, modality, 0), pick(upper, 1 - modality, 0)
        lower_keep, lower_send = pick(lower, y, 2), pick(lower, 1 - y, 2)
        upper_keep, upper_send, lower_keep, lower_send, pair_first_grad = sync(
            upper_keep, upper_send, lower_keep, lower_send, pair_first_grad
        )
        upper_got, lower_got = flip_mod(upper_send), flip(lower_send, Y)
    stream_grad, small = first_grad(
        rows_info,
        grad_first,
        pair_first_grad,
        hidden,
        grad_middle,
        vec,
        sums,
        late_vec,
        up_bias_grad.reshape(chunks, width),
        pos,
        slots,
    )
    if by_rows:
        small = small.astype(bf16).reshape(2, 2, 4, -1, width)
        small_keep, small_send = pick(small, core, 0), pick(small, 1 - core, 0)
        small_got = flip(small_send, CORE)
        upper_got, lower_got, small_got = sync(upper_got, lower_got, small_got)
        upper, lower = plus(upper_keep, upper_got), plus(lower_keep, lower_got)
        upper_keep, upper_send = pick(upper, y, 1), pick(upper, 1 - y, 1)
        lower_keep, lower_send = pick(lower, modality, 0), pick(lower, 1 - modality, 0)
        small = plus(small_keep, small_got)
        small_keep, small_send = pick(small, y, 0), pick(small, 1 - y, 0)
        small_keep, small_send, upper_keep, upper_send, lower_keep, lower_send, ffn_1 = sync(
            small_keep, small_send, upper_keep, upper_send, lower_keep, lower_send, ffn_1
        )
        upper_got, lower_got = flip(upper_send, Y), flip_mod(lower_send)
        small_got = flip(small_send, Y)
        ffn_new = shampoo(is_up, 0, 0, [ffn_1], *ffn_old)
        ffn_new, small_got, upper_got, lower_got = sync(ffn_new, small_got, upper_got, lower_got)
        attn = jnp.concatenate([plus(upper_keep, upper_got), plus(lower_keep, lower_got)], axis=1)
        attn_z = [pick(attn, z ^ bits, 0) for bits in range(4)]
        small = plus(small_keep, small_got)
        small_z = [pick(small, z ^ bits, 0) for bits in range(4)]
        small_z, attn_z, ffn_new = sync(small_z, attn_z, ffn_new)
        attn_got = along_z_of(attn_z)
        small_got = along_z_of(small_z)
        ffn_new = shampoo(is_up, 1, 1, [ffn_1], *ffn_old, ffn_new)
        ffn_new, small_got = sync(ffn_new, small_got)
        small = sum(part.astype(f32) for part in (small_z[0], *small_got))
        small, ffn_new = sync(small, ffn_new)
        small_got = flip_mod(small)
        ffn_new = shampoo(is_up, 2, 0, [ffn_2[0], *got_2], *ffn_old, ffn_new)
        ffn_new, small_got = sync(ffn_new, small_got)
        small = (small + small_got).astype(bf16)
        small, ffn_new = sync(small, ffn_new)
        small_got = [flip(small, bits * Z_LOW) for bits in (1, 2, 3)]
        ffn_out = shampoo(is_up, 3, 1, [ffn_2[0], *got_2], *ffn_old, ffn_new)
        small_got, attn_got, ffn_out = sync(small_got, attn_got, ffn_out)
        near = in_order(z % 2, small, small_got[0])
        far = in_order(z % 2, small_got[1], small_got[2])
        small = in_order(z // 2, near, far)
        small, attn_got = sync(small, attn_got)
        small_got = flip(small, Y)
        attn_rows = [part[None] for part in (attn_z[0], *attn_got)]
        attn_old = [part[None] for part in (attn_left, attn_right, attn_blocks)]
        attn_out = shampoo(is_not, 0, 0, attn_rows, *attn_old)
        small_got, attn_out = sync(small_got, attn_out)
        small = in_order(y, small, small_got)
        small_sum = in_order(core, small, flip(small, CORE)).astype(f32).reshape(-1, width)
    else:
        grad_2 = jnp.stack([keep_2, send_2], axis=2).reshape(grad_1.shape)
        grads = jnp.concatenate([grad_1, grad_2], axis=2)
        up = grads[0].reshape(row_blocks, chunks, size, row_blocks, size)
        down = grads[1].reshape(row_blocks, chunks, size, row_blocks, size)
        up = up.transpose(0, 3, 1, 2, 4).reshape(-1, size, size)
        down = down.transpose(0, 1, 3, 2, 4).reshape(-1, size, size)
        ffn_sum = lax.psum_scatter(
            jnp.concatenate([up, down], axis=0), "dp", scatter_dimension=0, tiled=True
        )
        attn_full = jnp.stack([attn_keep, attn_send], axis=2).reshape(-1, size, width)
        attn_sum = lax.psum_scatter(
            parts_to_blocks(attn_full), ("mod", "dp"), scatter_dimension=0, tiled=True
        )
        small_sum = lax.psum(small, ("mod", "dp"))
        ffn_old = [part for part in (ffn_left, ffn_right, ffn_blocks)]
        attn_old = [part[None] for part in (attn_left, attn_right, attn_blocks)]
        ffn_out = shampoo(is_not, 0, 0, [square_parts(ffn_sum, 1, ffn_sum.shape[0])], *ffn_old)
        attn_out = shampoo(is_not, 0, 0, [square_parts(attn_sum, 1, attn_sum.shape[0])], *attn_old)

    items_total = lax.axis_size("dp")
    vector_rate = 0.3 / math.sqrt(items_total * slots)
    pos_rate = 0.5 / math.sqrt(items_total)
    vectors_mom_new = moment_keep * vectors_mom + small_sum[: vectors.shape[0]]
    vectors_new = vectors - vector_rate * vectors_mom_new
    ffn_bias_mom_new = moment_keep * ffn_bias_mom + small_sum[16:24].reshape(ffn_bias.shape)
    ffn_bias_new = ffn_bias - vector_rate * ffn_bias_mom_new
    pos_mom_new = moment_keep * pos_mom + small_sum[24 : 24 + slots]
    pos_new = pos_table - pos_rate * pos_mom_new
    return (
        stream_out[None, None],
        stream_grad[None, None],
        *attn_out,
        *(part[None] for part in ffn_out),
        vectors_mom_new,
        vectors_new,
        ffn_bias_mom_new,
        ffn_bias_new,
        pos_mom_new,
        pos_new,
    )


def solution(mesh):
    items = P("mod", "dp", None, None)
    owned = P(("mod", "dp"), None, None)
    return jax.shard_map(
        local,
        mesh=mesh,
        in_specs=(items, items, P("dp"), P("dp", None), owned, owned, owned, items, items, items)
        + (P(),) * 6,
        out_specs=(items, items, owned, owned, owned, owned, items, items, items, items)
        + (P(),) * 6,
        check_vma=False,
    )
```

time: 707 us -> 393 us (0.56)
  waiting for transfers between devices: 384 us -> 63.6 us
  blocking collectives: 41 us -> 0 us
  starting transfers between devices: 6.07 us -> 45.7 us
  Pallas kernels: 178 us -> 206 us
  other arithmetic: 39.3 us -> 24.3 us
  local copies, waits for them, and re-layouts: 37.4 us -> 29.9 us
    reduce_scatter x2 -> x1, waiting for transfers between devices: 211 us -> 0.02 us  [local(): lax.psum_scatter(grad_1.reshape(-1, chunks // 2, size, width), 'dp', scat...]
    all_gather x2 -> x1, waiting for transfers between devices: 88.1 us -> 9.62 us  [local(): ffn_parts = lax.all_gather(ffn_rows, 'dp', axis=0, tiled=True)]
    psum x1 -> x0, waiting for transfers between devices: 66.2 us -> none  [local(): lax.psum((vector_grad, up_bias_grad, grad_pos), ('mod', 'dp'))]
    psum x1 -> x0, blocking collectives: 41 us -> none  [local(): lax.psum((vector_grad, up_bias_grad, grad_pos), ('mod', 'dp'))]
    ppermute x4 -> x37, starting transfers between devices: 5.86 us -> 45.6 us  [the longest x28 32.7 us: flip(): return lax.ppermute(values, 'dp', [(i, i ^ bits) for i in range(size)])]
    ppermute x4 -> x37, waiting for transfers between devices: 18.1 us -> 53.9 us  [the longest x28 28 us: flip(): return lax.ppermute(values, 'dp', [(i, i ^ bits) for i in range(size)])]
    pallas_call x7 -> x13, Pallas kernels: 131 us -> 159 us  [the longest x5 48.3 us: shampoo(): pl.pallas_call(kernel, grid=(1,), in_specs=[SMEM_SPEC] + [pl.BlockSpec((1...]
    slice x11 -> x6, local copies, waits for them, and re-layouts: 14.2 us -> 1.24 us  [the longest x1 0.91 us: local(): pair_first = lax.ppermute(first[:TEXT], 'mod', to_image)]
  transfers between devices with their start and end apart: 9 -> 39, of which waited for: 8 -> 14; matrix products, arithmetic and copies ran while one was open for 8% -> 9% of each run, Pallas kernels for 6% -> 41%
where the time goes in v2:
time: 393 us; the launch traced here: 385 us
  Pallas kernels  206 us (52%)
  waiting for transfers between devices  63.6 us (16%)
  starting transfers between devices  45.7 us (12%)
  local copies, waits for them, and re-layouts  29.9 us (8%)
  other arithmetic  24.3 us (6%)
  between operations  16 us (4%)
    pallas_call x5, Pallas kernels, shampoo(): pl.pallas_call(kernel, grid=(1,), in_specs=[SMEM_SPEC] + [pl.BlockSpec((1...  48.3 us
    pallas_call x1, Pallas kernels, expert_end(): pl.pallas_call(expert_end_kernel, grid=(ffn_parts.shape[2] // 2,), in_spe...  36.1 us
    ppermute x28, starting transfers between devices, flip(): return lax.ppermute(values, 'dp', [(i, i ^ bits) for i in range(size)])  32.7 us
    pallas_call x1, Pallas kernels, expert_begin(): pl.pallas_call(expert_begin_kernel, grid=(ffn_parts.shape[2] // 2,), in_s...  30.5 us
    ppermute x28, waiting for transfers between devices, flip(): return lax.ppermute(values, 'dp', [(i, i ^ bits) for i in range(size)])  28 us
    pallas_call x1, Pallas kernels, attend_grad(): pl.pallas_call(attend_grad_kernel, grid=(pairs,), in_specs=[SMEM_SPEC, co...  24.9 us
    pallas_call x1, Pallas kernels, attend(): pl.pallas_call(attend_kernel, grid=(pairs,), in_specs=[SMEM_SPEC, column(...  22.3 us
    pallas_call x1, Pallas kernels, first_grad(): pl.pallas_call(first_grad_kernel, in_specs=[SMEM_SPEC] + [whole(arg.shape...  16.7 us
  transfers between devices with their start and end apart: 39, of which 14 were waited for; matrix products, arithmetic and copies ran while one was open for 9% of the time, Pallas kernels for 41%

profile of v2, /device:TPU:0, one launch (start us, length us, event | category | flops | bytes accessed | tf_op | source)
XLA Modules:
  0.0 385.4 jit_solution(5113557749305478367)
XLA Ops:
  16.0 5.0 %gather_fusion = f32[577,768]{1,0:T(8,128)S(1)} fusion(f32[577,768]{1,0:T(8,128)} %param.30, s32[1024]{0:T(1024)S(1)} %pad_clamp_fusion), kind=kCustom, calls=%fused_computation | custom fusion | bytes 3547396 | tf_op jit(solution)/shard_map/jit(_take)/gather | solution.py:1007
  26.9 3.1 pack_rows.3
  41.0 5.2 %collective-permute-done.5 = bf16[64,768]{1,0:T(8,128)(2,1)S(1)} collective-permute-done((bf16[64,768]{1,0:T(8,128)(2,1)S(1)}, bf16[64,768]{1,0:T(8,128)(2,1)S(1)}, u32[]{:S(2)}, u32[]{:S(2)}) %collective-permute-start.5) | collective-permute-done | bytes 98336 | tf_op jit(solution)/shard_map/ppermute | solution.py:1020
  55.5 6.0 %collective-permute-done.7 = bf16[2,4,48,768]{3,2,1,0:T(8,128)(2,1)S(1)} collective-permute-done((bf16[2,4,48,768]{3,2,1,0:T(8,128)(2,1)S(1)}, bf16[2,4,48,768]{3,2,1,0:T(8,128)(2,1)S(1)}, u32[]{:S(2)}, u32[]{:S(2)}) %collective-permute-start.7) | collective-permute-done | bytes 589856 | tf_op jit(solution)/shard_map/ppermute | solution.py:911
  67.3 8.2 %project.1 = (bf16[672,2304]{1,0:T(8,128)(2,1)}, bf16[4,768,768]{2,1,0:T(8,128)(2,1)}) custom-call(s32[6]{0:T(128)} %stack.127.row_ref, bf16[672,768]{1,0:T(8,128)(2,1)} %select_dynamic-update-slice_fusion.first_ref, f32[8,768]{1,0:T(8,128)} %pad_maximum_fusion.12.vec_ref, bf16[2,2,4,48,768]{4,3,2,1,0:T(8,128)(2,1)} %copy-done.5, ...), custom_call_target="tpu_custom_call" | custom-call | flops 800000000 | tf_op jit(solution)/shard_map/project/pallas_call | solution.py:152
  75.5 22.3 %attend.1 = (bf16[672,768]{1,0:T(8,128)(2,1)}, f32[6,8,672]{2,1,0:T(8,128)}, bf16[64,768]{1,0:T(8,128)(2,1)}) custom-call(s32[6]{0:T(128)} %stack.127.row_ref, bf16[672,2304]{1,0:T(8,128)(2,1)} %get-tuple-element.196.q_ref.k_ref.v_ref, bf16[672,2304]{1,0:T(8,128)(2,1)} %get-tuple-element.196.q_ref.k_ref.v_ref, ...), custom_call_target="tpu_custom_call" | custom-call | flops 2200000000 | tf_op jit(solution)/shard_map/attend/pallas_call | solution.py:216
  97.8 3.5 collective-permute-start.10
  103.8 9.6 %all-gather.2.cloned.1.call-done = bf16[64,96,768]{2,1,0:T(8,128)(2,1)} async-done(((bf16[4,96,768]{2,1,0:T(8,128)(2,1)}), bf16[64,96,768]{2,1,0:T(8,128)(2,1)}) %all-gather.2.cloned.1.call-update) | async-done | bytes 9437200 | tf_op jit(solution)/shard_map/all_gather | solution.py:1012
  113.4 30.5 %expert_begin.1 = (bf16[592,768]{1,0:T(8,128)(2,1)}, f32[592,768]{1,0:T(8,128)}, bf16[592,768]{1,0:T(8,128)(2,1)}, bf16[592,768]{1,0:T(8,128)(2,1)}, f32[592,768...) custom-call(s32[6]{0:T(128)} %stack.127.row_ref, ...), custom_call_target="tpu_custom_call" | custom-call | flops 2800000000 | tf_op jit(solution)/shard_map/expert_begin/pallas_call | solution.py:561
  143.9 36.1 %expert_end.1 = (f32[577,768]{1,0:T(8,128)}, f32[592,768]{1,0:T(8,128)}, bf16[672,768]{1,0:T(8,128)(2,1)}, bf16[64,768]{1,0:T(8,128)(2,1)}, bf16[768,768]{1,0:T(...) custom-call(s32[6]{0:T(128)} %stack.127.row_ref, ...), custom_call_target="tpu_custom_call" | custom-call | flops 3000000000 | tf_op jit(solution)/shard_map/expert_end/pallas_call | solution.py:586
  181.9 5.5 %collective-permute-done.11.pair_ref = bf16[64,768]{1,0:T(8,128)(2,1)S(1)} collective-permute-done((bf16[64,768]{1,0:T(8,128)(2,1)}, bf16[64,768]{1,0:T(8,128)(2,1)S(1)}, u32[]{:S(2)}, u32[]{:S(2)}) %collective-permute-start.11) | collective-permute-done | bytes 98336 | tf_op jit(solution)/shard_map/ppermute | solution.py:1058
  190.7 24.9 %attend_grad.1.dqkv_ref = bf16[3,672,768]{2,1,0:T(8,128)(2,1)} custom-call(s32[6]{0:T(128)} %stack.127.row_ref, bf16[672,2304]{1,0:T(8,128)(2,1)} %get-tuple-element.196.q_ref.k_ref.v_ref, bf16[672,2304]{1,0:T(8,128)(2,1)} %get-tuple-element.196.q_ref.k_ref.v_ref, bf16[672,2304]{1,0:T(8,128)(2,1)} %get-tuple-element.196.q_ref.k_ref.v_ref, ...), custom_call_target="tpu_custom_call" | custom-call | flops 2500000000 | tf_op jit(solution)/shard_map/attend_grad/pallas_call | solution.py:290
  215.6 5.1 %collective-permute-done.13 = bf16[4,2,96,768]{3,2,1,0:T(8,128)(2,1)S(1)} collective-permute-done((bf16[4,2,96,768]{3,2,1,0:T(8,128)(2,1)S(1)}, bf16[4,2,96,768]{3,2,1,0:T(8,128)(2,1)S(1)}, u32[]{:S(2)}, u32[]{:S(2)}) %collective-permute-start.13) | collective-permute-done | bytes 1179680 | tf_op jit(solution)/shard_map/ppermute | solution.py:911
  226.2 10.9 %project_grad.1 = (bf16[4,4,96,768]{3,2,1,0:T(8,128)(2,1)}, bf16[4,4,96,768]{3,2,1,0:T(8,128)(2,1)}, f32[672,768]{1,0:T(8,128)}, f32[64,768]{1,0:T(8,128)}, f32[8,768]{1,0:T(8,128)}) custom-call(s32[6]{0:T(128)} %stack.127.row_ref, bf16[3,672,768]{2,1,0:T(8,128)(2,1)} %attend_grad.1.dqkv_ref, bf16[672,768]{1,0:T(8,128)(2,1)} %select_dynamic-update-slice_fusion.first_ref, ...), custom_call_target="tpu_custom_call" | custom-call | flops 1500000000 | tf_op jit(solution)/shard_map/project_grad/pallas_call | solution.py:664
  237.1 8.7 %collective-permute-done.15.refs_2_ = bf16[2,96,768]{2,1,0:T(8,128)(2,1)S(1)} collective-permute-done((bf16[2,96,768]{2,1,0:T(8,128)(2,1)S(1)}, bf16[2,96,768]{2,1,0:T(8,128)(2,1)S(1)}, u32[]{:S(2)}, u32[]{:S(2)}) %collective-permute-start.15) | collective-permute-done | bytes 294944 | tf_op jit(solution)/shard_map/ppermute | solution.py:911
  248.9 3.7 collective-permute-done.18.pair_ref
  257.2 16.7 %first_grad.1 = (f32[577,768]{1,0:T(8,128)}, f32[640,768]{1,0:T(8,128)}) custom-call(s32[6]{0:T(128)} %stack.127.row_ref, f32[672,768]{1,0:T(8,128)} %get-tuple-element.234.gfirst_ref, f32[64,768]{1,0:T(8,128)} %copy-done.15, f32[592,768]{1,0:T(8,128)} %pad.11.hidden_ref, f32[592,768]{1,0:T(8,128)} %get-tuple-element.241.gmid_ref, ...), custom_call_target="tpu_custom_call" | custom-call | flops 800000000 | tf_op jit(solution)/shard_map/first_grad/pallas_call | solution.py:757
  281.5 9.9 %collective-permute-done.19 = bf16[4,2,48,768]{3,2,1,0:T(8,128)(2,1)S(1)} collective-permute-done((bf16[4,2,48,768]{3,2,1,0:T(8,128)(2,1)}, bf16[4,2,48,768]{3,2,1,0:T(8,128)(2,1)S(1)}, u32[]{:S(2)}, u32[]{:S(2)}) %collective-permute-start.19) | collective-permute-done | bytes 589856 | tf_op jit(solution)/shard_map/ppermute | solution.py:915
  296.9 9.4 %shampoo.5 = (f32[32,96,96]{2,1,0:T(8,128)}, f32[32,96,96]{2,1,0:T(8,128)}, f32[32,96,96]{2,1,0:T(8,128)}, f32[32,96,96]{2,1,0:T(8,128)}) custom-call(s32[1]{0:T(128)} %bitcast.8.up_ref, bf16[2,96,768]{2,1,0:T(8,128)(2,1)} %bitcast.178, f32[4,8,96,96]{3,2,1,0:T(8,128)} %bitcast_select_fusion.2.refs_1_.refs_4_, ...), custom_call_target="tpu_custom_call" | custom-call | flops 900000000 | tf_op jit(solution)/shard_map/shampoo/pallas_call | solution.py:886
  308.3 4.5 %collective-permute-start.25 = (bf16[40,768]{1,0:T(8,128)(2,1)S(1)}, bf16[40,768]{1,0:T(8,128)(2,1)S(1)}, u32[]{:S(2)}, u32[]{:S(2)}) collective-permute-start(bf16[40,768]{1,0:T(8,128)(2,1)S(1)} %get-tuple-element.286), channel_id=1, source_target_pairs={{0,4},{1,5},{2,6},{3,7},{4,0},{5,1},{6,2},{7,3},{8,12},{9,13},{10,... | collective-permute-start | bytes 184328 | tf_op jit(solution)/shard_map/ppermute | solution.py:911
  315.1 9.6 %shampoo.6 = (f32[32,96,96]{2,1,0:T(8,128)}, f32[32,96,96]{2,1,0:T(8,128)}, f32[32,96,96]{2,1,0:T(8,128)}, f32[32,96,96]{2,1,0:T(8,128)}) custom-call(s32[1]{0:T(128)} %bitcast.8.up_ref, bf16[2,96,768]{2,1,0:T(8,128)(2,1)} %bitcast.179, ...), custom_call_target="tpu_custom_call", output_to_operand_aliasing={{0}: (5, {}), {1}: (6, {}), {2}: (7, {}), {3}: (8, {})} | custom-call | flops 900000000 | tf_op jit(solution)/shard_map/shampoo/pallas_call | solution.py:886
  329.9 9.6 %shampoo.7 = (f32[32,96,96]{2,1,0:T(8,128)}, f32[32,96,96]{2,1,0:T(8,128)}, f32[32,96,96]{2,1,0:T(8,128)}, f32[32,96,96]{2,1,0:T(8,128)}) custom-call(s32[1]{0:T(128)} %bitcast.8.up_ref, bf16[2,96,768]{2,1,0:T(8,128)(2,1)} %get-tuple-element.297.refs_0_, ...), custom_call_target="tpu_custom_call", output_to_operand_aliasing={{0}: (8, {}), {1}: (9, {}), {2}: (10, {}), {3}: (11, {})} | custom-call | flops 900000000 | tf_op jit(solution)/shard_map/shampoo/pallas_call | solution.py:886
  344.3 9.6 %shampoo.8 = (f32[32,96,96]{2,1,0:T(8,128)}, f32[32,96,96]{2,1,0:T(8,128)}, f32[32,96,96]{2,1,0:T(8,128)}, f32[32,96,96]{2,1,0:T(8,128)}) custom-call(s32[1]{0:T(128)} %bitcast.8.up_ref, bf16[2,96,768]{2,1,0:T(8,128)(2,1)} %get-tuple-element.297.refs_0_, ...), custom_call_target="tpu_custom_call", output_to_operand_aliasing={{0}: (8, {}), {1}: (9, {}), {2}: (10, {}), {3}: (11, {})} | custom-call | flops 900000000 | tf_op jit(solution)/shard_map/shampoo/pallas_call | solution.py:886
  354.8 9.9 %shampoo.9 = (f32[8,96,96]{2,1,0:T(8,128)}, f32[8,96,96]{2,1,0:T(8,128)}, f32[8,96,96]{2,1,0:T(8,128)}, f32[8,96,96]{2,1,0:T(8,128)}) custom-call(s32[1]{0:T(128)} %constant.177.clone.1.up_ref, bf16[1,96,768]{2,1,0:T(8,128)(2,1)} %bitcast.180, bf16[1,96,768]{2,1,0:T(8,128)(2,1)} %bitcast.189, bf16[1,96,768]{2,1,0:T(8,128)(2,1)} %bitcast.190, ...), custom_call_target="tpu_custom_call" | custom-call | flops 900000000 | tf_op jit(solution)/shard_map/shampoo/pallas_call | solution.py:886
  (209 shorter events, 101.7 us)
Async XLA Ops:
  7.2 106.2 %all-gather.2.cloned.1.call-start = ((), (), s32[]{:S(2)}) async-start(), calls=%async_computation.1 | async-start | bytes 10027008 | tf_op jit(solution)/shard_map/all_gather | solution.py:1012
  9.0 21.0 %collective-permute-start = (bf16[96,768]{1,0:T(8,128)(2,1)}, bf16[96,768]{1,0:T(8,128)(2,1)S(1)}, u32[]{:S(2)}, u32[]{:S(2)}) collective-permute-start(bf16[96,768]{1,0:T(8,128)(2,1)} %bitcast.181), channel_id=1, source_target_pairs={{0,4},{1,5},{2,6},{3,7},{4,0},{5,1},{6,2},{7,3},{8,12},{9,13},{10,... | collective-permute-start | bytes 442376 | tf_op jit(solution)/shard_map/ppermute | solution.py:911
  12.0 18.0 %collective-permute-start.1 = (bf16[96,768]{1,0:T(8,128)(2,1)}, bf16[96,768]{1,0:T(8,128)(2,1)S(1)}, u32[]{:S(2)}, u32[]{:S(2)}) collective-permute-start(bf16[96,768]{1,0:T(8,128)(2,1)} %bitcast.182), channel_id=1, source_target_pairs={{0,8},{1,9},{2,10},{3,11},{4,12},{5,13},{6,14},{7,15},{8,0},{9,1},... | collective-permute-start | bytes 442376 | tf_op jit(solution)/shard_map/ppermute | solution.py:911
  14.6 15.4 %collective-permute-start.2 = (bf16[96,768]{1,0:T(8,128)(2,1)}, bf16[96,768]{1,0:T(8,128)(2,1)S(1)}, u32[]{:S(2)}, u32[]{:S(2)}) collective-permute-start(bf16[96,768]{1,0:T(8,128)(2,1)} %bitcast.183), channel_id=1, source_target_pairs={{0,12},{1,13},{2,14},{3,15},{4,8},{5,9},{6,10},{7,11},{8,4},{9,5},... | collective-permute-start | bytes 442376 | tf_op jit(solution)/shard_map/ppermute | solution.py:911
  30.0 215.8 %reduce-scatter.2.cloned.1.call-start = ((), (), s32[]{:S(2)}) async-start(), calls=%async_computation.2 | async-start | bytes 5013504 | tf_op jit(solution)/shard_map/reduce_scatter | solution.py:1064
  30.4 15.8 %collective-permute-start.3 = (bf16[4,48,768]{2,1,0:T(8,128)(2,1)S(1)}, bf16[4,48,768]{2,1,0:T(8,128)(2,1)S(1)}, u32[]{:S(2)}, u32[]{:S(2)}) collective-permute-start(bf16[4,48,768]{2,1,0:T(8,128)(2,1)S(1)} %get-tuple-element.437), channel_id=1, source_target_pairs={{0,2},{1,3},{2,0},{3,1},{4,6},{5,7},{6,4},{7,5},{8,10},{9,11},{10,... | collective-permute-start | bytes 884744 | tf_op jit(solution)/shard_map/ppermute | solution.py:911
  32.2 14.0 %collective-permute-start.4 = (bf16[4,48,768]{2,1,0:T(8,128)(2,1)S(1)}, bf16[4,48,768]{2,1,0:T(8,128)(2,1)S(1)}, u32[]{:S(2)}, u32[]{:S(2)}) collective-permute-start(bf16[4,48,768]{2,1,0:T(8,128)(2,1)S(1)} %get-tuple-element.436), channel_id=1, source_target_pairs={{0,16},{16,0},{1,17},{17,1},{2,18},{18,2},{3,19},{19,3},{4,20},{20... | collective-permute-start | bytes 884744 | tf_op jit(solution)/shard_map/ppermute | solution.py:915
  46.4 15.1 %collective-permute-start.7 = (bf16[2,4,48,768]{3,2,1,0:T(8,128)(2,1)S(1)}, bf16[2,4,48,768]{3,2,1,0:T(8,128)(2,1)S(1)}, u32[]{:S(2)}, u32[]{:S(2)}) collective-permute-start(bf16[2,4,48,768]{3,2,1,0:T(8,128)(2,1)S(1)} %pad_maximum_fusion.5), channel_id=1, source_target_pairs={{0,2},{1,3},{2,0},{3,1},{4,6},{5,7},{6,4},{7,5},{8,10},{9,11},{10,... | collective-permute-start | bytes 1769480 | tf_op jit(solution)/shard_map/ppermute | solution.py:911
  47.0 14.5 %collective-permute-start.6 = (bf16[2,4,48,768]{3,2,1,0:T(8,128)(2,1)S(1)}, bf16[2,4,48,768]{3,2,1,0:T(8,128)(2,1)S(1)}, u32[]{:S(2)}, u32[]{:S(2)}) collective-permute-start(bf16[2,4,48,768]{3,2,1,0:T(8,128)(2,1)S(1)} %pad_maximum_fusion.4), channel_id=1, source_target_pairs={{0,16},{16,0},{1,17},{17,1},{2,18},{18,2},{3,19},{19,3},{4,20},{20... | collective-permute-start | bytes 1769480 | tf_op jit(solution)/shard_map/ppermute | solution.py:915
  190.1 30.6 %collective-permute-start.13 = (bf16[4,2,96,768]{3,2,1,0:T(8,128)(2,1)S(1)}, bf16[4,2,96,768]{3,2,1,0:T(8,128)(2,1)S(1)}, u32[]{:S(2)}, u32[]{:S(2)}) collective-permute-start(bf16[4,2,96,768]{3,2,1,0:T(8,128)(2,1)S(1)} %get-tuple-element.217), channel_id=1, source_target_pairs={{0,2},{1,3},{2,0},{3,1},{4,6},{5,7},{6,4},{7,5},{8,10},{9,11},{10,... | collective-permute-start | bytes 3538952 | tf_op jit(solution)/shard_map/ppermute | solution.py:911
  221.8 15.3 %collective-permute-start.14 = (bf16[2,96,768]{2,1,0:T(8,128)(2,1)S(1)}, bf16[2,96,768]{2,1,0:T(8,128)(2,1)S(1)}, u32[]{:S(2)}, u32[]{:S(2)}) collective-permute-start(bf16[2,96,768]{2,1,0:T(8,128)(2,1)S(1)} %get-tuple-element.231), channel_id=1, source_target_pairs={{0,4},{1,5},{2,6},{3,7},{4,0},{5,1},{6,2},{7,3},{8,12},{9,13},{10,... | collective-permute-start | bytes 884744 | tf_op jit(solution)/shard_map/ppermute | solution.py:911
  222.3 23.5 %collective-permute-start.15 = (bf16[2,96,768]{2,1,0:T(8,128)(2,1)S(1)}, bf16[2,96,768]{2,1,0:T(8,128)(2,1)S(1)}, u32[]{:S(2)}, u32[]{:S(2)}) collective-permute-start(bf16[2,96,768]{2,1,0:T(8,128)(2,1)S(1)} %get-tuple-element.232), channel_id=1, source_target_pairs={{0,8},{1,9},{2,10},{3,11},{4,12},{5,13},{6,14},{7,15},{8,0},{9,1},... | collective-permute-start | bytes 884744 | tf_op jit(solution)/shard_map/ppermute | solution.py:911
  223.7 22.1 %collective-permute-start.16 = (bf16[2,96,768]{2,1,0:T(8,128)(2,1)S(1)}, bf16[2,96,768]{2,1,0:T(8,128)(2,1)S(1)}, u32[]{:S(2)}, u32[]{:S(2)}) collective-permute-start(bf16[2,96,768]{2,1,0:T(8,128)(2,1)S(1)} %get-tuple-element.233), channel_id=1, source_target_pairs={{0,12},{1,13},{2,14},{3,15},{4,8},{5,9},{6,10},{7,11},{8,4},{9,5},... | collective-permute-start | bytes 884744 | tf_op jit(solution)/shard_map/ppermute | solution.py:911
  275.5 15.9 %collective-permute-start.19 = (bf16[4,2,48,768]{3,2,1,0:T(8,128)(2,1)}, bf16[4,2,48,768]{3,2,1,0:T(8,128)(2,1)S(1)}, u32[]{:S(2)}, u32[]{:S(2)}) collective-permute-start(bf16[4,2,48,768]{3,2,1,0:T(8,128)(2,1)} %get-tuple-element.248), channel_id=1, source_target_pairs={{0,16},{16,0},{1,17},{17,1},{2,18},{18,2},{3,19},{19,3},{4,20},{20... | collective-permute-start | bytes 1769480 | tf_op jit(solution)/shard_map/ppermute | solution.py:915
  277.9 14.9 %collective-permute-start.20 = (bf16[2,4,48,768]{3,2,1,0:T(8,128)(2,1)}, bf16[2,4,48,768]{3,2,1,0:T(8,128)(2,1)S(1)}, u32[]{:S(2)}, u32[]{:S(2)}) collective-permute-start(bf16[2,4,48,768]{3,2,1,0:T(8,128)(2,1)} %get-tuple-element.249), channel_id=1, source_target_pairs={{0,2},{1,3},{2,0},{3,1},{4,6},{5,7},{6,4},{7,5},{8,10},{9,11},{10,... | collective-permute-start | bytes 1769480 | tf_op jit(solution)/shard_map/ppermute | solution.py:911
  294.5 12.8 %collective-permute-start.23 = (bf16[4,48,768]{2,1,0:T(8,128)(2,1)S(1)}, bf16[4,48,768]{2,1,0:T(8,128)(2,1)S(1)}, u32[]{:S(2)}, u32[]{:S(2)}) collective-permute-start(bf16[4,48,768]{2,1,0:T(8,128)(2,1)S(1)} %get-tuple-element.266), channel_id=1, source_target_pairs={{0,2},{1,3},{2,0},{3,1},{4,6},{5,7},{6,4},{7,5},{8,10},{9,11},{10,... | collective-permute-start | bytes 884744 | tf_op jit(solution)/shard_map/ppermute | solution.py:911
  295.1 12.2 %collective-permute-start.24 = (bf16[4,48,768]{2,1,0:T(8,128)(2,1)S(1)}, bf16[4,48,768]{2,1,0:T(8,128)(2,1)S(1)}, u32[]{:S(2)}, u32[]{:S(2)}) collective-permute-start(bf16[4,48,768]{2,1,0:T(8,128)(2,1)S(1)} %get-tuple-element.267), channel_id=1, source_target_pairs={{0,16},{16,0},{1,17},{17,1},{2,18},{18,2},{3,19},{19,3},{4,20},{20... | collective-permute-start | bytes 884744 | tf_op jit(solution)/shard_map/ppermute | solution.py:915
  308.3 16.5 %collective-permute-start.25 = (bf16[40,768]{1,0:T(8,128)(2,1)S(1)}, bf16[40,768]{1,0:T(8,128)(2,1)S(1)}, u32[]{:S(2)}, u32[]{:S(2)}) collective-permute-start(bf16[40,768]{1,0:T(8,128)(2,1)S(1)} %get-tuple-element.286), channel_id=1, source_target_pairs={{0,4},{1,5},{2,6},{3,7},{4,0},{5,1},{6,2},{7,3},{8,12},{9,13},{10,... | collective-permute-start | bytes 184328 | tf_op jit(solution)/shard_map/ppermute | solution.py:911
  324.8 14.8 %collective-permute-start.28 = (f32[40,768]{1,0:T(8,128)S(1)}, f32[40,768]{1,0:T(8,128)S(1)}, u32[]{:S(2)}, u32[]{:S(2)}) collective-permute-start(f32[40,768]{1,0:T(8,128)S(1)} %convert_add_fusion.1), channel_id=1, source_target_pairs={{0,16},{16,0},{1,17},{17,1},{2,18},{18,2},{3,19},{19,3},{4,20},{20... | collective-permute-start | bytes 368648 | tf_op jit(solution)/shard_map/ppermute | solution.py:915
  325.6 17.0 %collective-permute-start.32 = (bf16[96,768]{1,0:T(8,128)(2,1)S(1)}, bf16[96,768]{1,0:T(8,128)(2,1)S(1)}, u32[]{:S(2)}, u32[]{:S(2)}) collective-permute-start(bf16[96,768]{1,0:T(8,128)(2,1)S(1)} %get-tuple-element.315), channel_id=1, source_target_pairs={{0,4},{1,5},{2,6},{3,7},{4,0},{5,1},{6,2},{7,3},{8,12},{9,13},{10,... | collective-permute-start | bytes 442376 | tf_op jit(solution)/shard_map/ppermute | solution.py:911
  326.7 27.3 %collective-permute-start.33 = (bf16[96,768]{1,0:T(8,128)(2,1)S(1)}, bf16[96,768]{1,0:T(8,128)(2,1)S(1)}, u32[]{:S(2)}, u32[]{:S(2)}) collective-permute-start(bf16[96,768]{1,0:T(8,128)(2,1)S(1)} %get-tuple-element.316), channel_id=1, source_target_pairs={{0,8},{1,9},{2,10},{3,11},{4,12},{5,13},{6,14},{7,15},{8,0},{9,1},... | collective-permute-start | bytes 442376 | tf_op jit(solution)/shard_map/ppermute | solution.py:911
  328.4 25.6 %collective-permute-start.34 = (bf16[96,768]{1,0:T(8,128)(2,1)S(1)}, bf16[96,768]{1,0:T(8,128)(2,1)S(1)}, u32[]{:S(2)}, u32[]{:S(2)}) collective-permute-start(bf16[96,768]{1,0:T(8,128)(2,1)S(1)} %get-tuple-element.317), channel_id=1, source_target_pairs={{0,12},{1,13},{2,14},{3,15},{4,8},{5,9},{6,10},{7,11},{8,4},{9,5},... | collective-permute-start | bytes 442376 | tf_op jit(solution)/shard_map/ppermute | solution.py:911
  339.6 14.4 %collective-permute-start.29 = (bf16[40,768]{1,0:T(8,128)(2,1)S(1)}, bf16[40,768]{1,0:T(8,128)(2,1)S(1)}, u32[]{:S(2)}, u32[]{:S(2)}) collective-permute-start(bf16[40,768]{1,0:T(8,128)(2,1)S(1)} %add_convert_fusion.8), channel_id=1, source_target_pairs={{0,4},{1,5},{2,6},{3,7},{4,0},{5,1},{6,2},{7,3},{8,12},{9,13},{10,... | collective-permute-start | bytes 184328 | tf_op jit(solution)/shard_map/ppermute | solution.py:911
  339.9 14.1 %collective-permute-start.30 = (bf16[40,768]{1,0:T(8,128)(2,1)S(1)}, bf16[40,768]{1,0:T(8,128)(2,1)S(1)}, u32[]{:S(2)}, u32[]{:S(2)}) collective-permute-start(bf16[40,768]{1,0:T(8,128)(2,1)S(1)} %add_convert_fusion.8), channel_id=1, source_target_pairs={{0,8},{1,9},{2,10},{3,11},{4,12},{5,13},{6,14},{7,15},{8,0},{9,1},... | collective-permute-start | bytes 184328 | tf_op jit(solution)/shard_map/ppermute | solution.py:911
  (46 other events, 292.5 us)
Sparse Core Ops, SparseCore 0:
  30.2 83.1 all-gather.1
  144.0 76.9 reduce-scatter.1

commit v3 on v2

--- a/solution.py
+++ b/solution.py
@@ -12,8 +12,8 @@
 TEXT = 64
 NEWTON = 6
 PAIR_LANES = 128
-QUERY_TILE = 256
-VMEM_LIMIT = 56 << 20
+QUERY_TILE = 336
+GRAD_TILE = 256
 
 f32 = jnp.float32
 bf16 = jnp.bfloat16
@@ -36,12 +36,12 @@
     return lax.dot_general(left, right, (((0,), (0,)), ((), ())), preferred_element_type=f32)
 
 
-def params():
-    return pltpu.CompilerParams(vmem_limit_bytes=VMEM_LIMIT)
+def params(mebibytes=56):
+    return pltpu.CompilerParams(vmem_limit_bytes=mebibytes << 20)
 
 
 def cost(microseconds):
-    return pl.CostEstimate(flops=int(microseconds * 1e8), bytes_accessed=0, transcendentals=0)
+    return pl.CostEstimate(flops=int(microseconds), bytes_accessed=0, transcendentals=0)
 
 
 def round_up(value, step):
@@ -181,28 +181,40 @@
     seq = q_ref.shape[0]
     half = PAIR_LANES // 2
     scale = half ** (-0.5)
-    bias = key_bias(row_ref, seq)
+    lane = lax.broadcasted_iota(jnp.int32, (seq, PAIR_LANES), 1)
+    bias = key_bias(row_ref, seq).astype(bf16)
+    queries = q_ref[...] * jnp.asarray(scale, bf16)
     keys = k_ref[...]
-    values_t = transposed(v_ref[...])
+    values = v_ref[...]
+    one = jnp.ones((seq, PAIR_LANES), bf16)
+    heads = []
+    for head in range(2):
+        own = (lane < half) == (head == 0)
+        spare = lane == half * (1 - head)
+        head_q = jnp.where(own, queries, jnp.where(spare, one, jnp.zeros_like(one)))
+        head_k = jnp.where(own, keys, jnp.where(spare, bias, jnp.zeros_like(one)))
+        head_v = jnp.where(own, values, one)
+        heads.append((head_q, head_k, head_v))
     for start in range(0, seq, QUERY_TILE):
         size = min(QUERY_TILE, seq - start)
         tile = slice(start, start + size)
-        queries = q_ref[tile, :]
-        lane = lax.broadcasted_iota(jnp.int32, (size, PAIR_LANES), 1)
-        parts = []
-        for head in range(2):
-            own = (lane < half) == (head == 0)
-            scores = dot_nt(keys, jnp.where(own, queries, jnp.zeros_like(queries))) * scale + bias
-            top = jnp.max(scores, axis=0, keepdims=True)
-            raised = jnp.exp(scores - top)
-            total = jnp.sum(raised, axis=0, keepdims=True)
-            probs = (raised * (1.0 / total)).astype(bf16)
-            parts.append(dot_nn(values_t[half * head : half * (head + 1), :], probs))
-            lse_ref[0, head : head + 1, tile] = top + jnp.log(total)
-        context = jnp.transpose(jnp.concatenate(parts, axis=0), (1, 0)).astype(bf16)
+        parts, lses = [], []
+        for head, (head_q, head_k, head_v) in enumerate(heads):
+            scores = dot_nt(head_q[tile], head_k)
+            top = jnp.max(scores, axis=1, keepdims=True)
+            raised = jnp.exp(scores - top).astype(bf16)
+            summed = dot_nn(raised, head_v)
+            at = half * (1 - head)
+            total = summed[:, at : at + 1]
+            parts.append(summed * (1.0 / total))
+            lses.append(top + jnp.log(total))
+        low = lax.broadcasted_iota(jnp.int32, (size, PAIR_LANES), 1) < half
+        context = jnp.where(low, parts[0], parts[1]).astype(bf16)
         ctx_ref[tile, :] = context
         if start == 0:
             pair_ref[...] = context[: pair_ref.shape[0]]
+        lane8 = lax.broadcasted_iota(jnp.int32, (size, 8), 1)
+        lse_ref[0, tile, :] = jnp.where(lane8 == 0, lses[0], lses[1])
 
 
 def attend(rows_info, qkv):
@@ -214,58 +226,66 @@
         return pl.BlockSpec((seq, PAIR_LANES), lambda i, base=base: (0, base + i))
 
     return pl.pallas_call(
-        attend_kernel,
-        grid=(pairs,),
+        attend_kernel, grid=(pairs,),
         in_specs=[SMEM_SPEC, column(0), column(pairs), column(2 * pairs)],
-        out_specs=[
-            column(0),
-            pl.BlockSpec((1, 8, seq), lambda i: (i, 0, 0)),
-            pl.BlockSpec((TEXT, PAIR_LANES), lambda i: (0, i)),
-        ],
-        out_shape=[
-            jax.ShapeDtypeStruct((seq, width), bf16),
-            jax.ShapeDtypeStruct((pairs, 8, seq), f32),
-            jax.ShapeDtypeStruct((TEXT, width), bf16),
-        ],
-        compiler_params=params(),
-        cost_estimate=cost(22),
-        name="attend",
+        out_specs=[column(0), pl.BlockSpec((1, seq, 8), lambda i: (i, 0, 0)), pl.BlockSpec((TEXT, PAIR_LANES), lambda i: (0, i))],
+        out_shape=[jax.ShapeDtypeStruct((seq, width), bf16), jax.ShapeDtypeStruct((pairs, seq, 8), f32), jax.ShapeDtypeStruct((TEXT, width), bf16)],
+        compiler_params=params(), cost_estimate=cost(12), name="attend",
     )(rows_info, qkv, qkv, qkv)
 
 
+def three_parts(values):
+    high = values.astype(bf16)
+    rest = values - high.astype(f32)
+    middle = rest.astype(bf16)
+    return high, middle, (rest - middle.astype(f32)).astype(bf16)
+
+
 def attend_grad_kernel(
-    row_ref, q_ref, k_ref, v_ref, g_ref, pair_ref, lse_ref, out_ref, dk_ref, dv_ref
+    row_ref, q_ref, k_ref, v_ref, g_ref, pair_ref, ctx_ref, lse_ref, out_ref, dk_ref, dv_ref
 ):
     seq = q_ref.shape[0]
     half = PAIR_LANES // 2
     scale = half ** (-0.5)
-    bias = key_bias(row_ref, seq)
+    lane = lax.broadcasted_iota(jnp.int32, (seq, PAIR_LANES), 1)
+    bias = key_bias(row_ref, seq).astype(bf16)
+    queries = q_ref[...]
+    scaled = queries * jnp.asarray(scale, bf16)
     keys = k_ref[...]
     values = v_ref[...]
     keys_t = transposed(keys)
-    for start in range(0, seq, QUERY_TILE):
-        size = min(QUERY_TILE, seq - start)
+    row = lax.broadcasted_iota(jnp.int32, (seq, 1), 0)
+    counts = jnp.logical_and(row >= row_ref[1], row < row_ref[2])
+    grads = jnp.concatenate([pair_ref[...], g_ref[pair_ref.shape[0] :, :]], axis=0)
+    grads = jnp.where(counts, grads, jnp.zeros((seq, PAIR_LANES), bf16))
+    products = grads.astype(f32) * ctx_ref[...].astype(f32)
+    one = jnp.ones((seq, PAIR_LANES), bf16)
+    zero = jnp.zeros((seq, PAIR_LANES), bf16)
+    heads = []
+    for head in range(2):
+        own = (lane < half) == (head == 0)
+        spare = lane - half * (1 - head)
+        lse = three_parts(-lse_ref[0, :, head : head + 1])
+        dots = three_parts(-jnp.sum(jnp.where(own, products, 0.0), axis=1, keepdims=True))
+        own_q = jnp.where(own, queries, zero)
+        own_g = jnp.where(own, grads, zero)
+        head_q = jnp.where(own, scaled, jnp.where(spare == 3, one, zero))
+        head_g = own_g
+        for i in range(3):
+            head_q = jnp.where(spare == i, lse[i], head_q)
+            head_g = jnp.where(spare == i, dots[i], head_g)
+        head_k = jnp.where(own, keys, jnp.where(spare == 3, bias, one))
+        head_v = jnp.where(own, values, one)
+        heads.append((head_q, head_g, head_k, head_v, own_q, own_g))
+    for start in range(0, seq, GRAD_TILE):
+        size = min(GRAD_TILE, seq - start)
         tile = slice(start, start + size)
-        queries = q_ref[tile, :]
-        row = lax.broadcasted_iota(jnp.int32, (size, 1), 0) + start
-        counts = jnp.logical_and(row >= row_ref[1], row < row_ref[2])
-        grads = g_ref[tile, :]
-        if start == 0:
-            grads = jnp.concatenate([pair_ref[...], grads[pair_ref.shape[0] :]], axis=0)
-        grads = jnp.where(counts, grads, jnp.zeros((size, PAIR_LANES), bf16))
-        lane = lax.broadcasted_iota(jnp.int32, (size, PAIR_LANES), 1)
         parts = []
-        for head in range(2):
-            own = (lane < half) == (head == 0)
-            own_q = jnp.where(own, queries, jnp.zeros_like(queries))
-            own_g = jnp.where(own, grads, jnp.zeros_like(grads))
-            scores = dot_nt(keys, own_q) * scale + bias
-            probs = jnp.exp(scores - lse_ref[0, head : head + 1, tile])
-            grad_probs = dot_nt(values, own_g)
-            row_dot = jnp.sum(probs * grad_probs, axis=0, keepdims=True)
-            grad_scores = (probs * (grad_probs - row_dot)).astype(bf16)
-            grad_v = dot_nn(probs.astype(bf16), own_g)
-            grad_k = dot_nn(grad_scores, own_q)
+        for head, (head_q, head_g, head_k, head_v, own_q, own_g) in enumerate(heads):
+            probs = jnp.exp(dot_nt(head_k, head_q[tile]))
+            grad_scores = (probs * dot_nt(head_v, head_g[tile])).astype(bf16)
+            grad_v = dot_nn(probs.astype(bf16), own_g[tile])
+            grad_k = dot_nn(grad_scores, own_q[tile])
             if start == 0 and head == 0:
                 dv_ref[...] = grad_v
                 dk_ref[...] = grad_k
@@ -279,7 +299,7 @@
     out_ref[2] = dv_ref[...].astype(bf16)
 
 
-def attend_grad(rows_info, qkv, grad_ctx, pair_grad, lse):
+def attend_grad(rows_info, qkv, grad_ctx, pair_grad, ctx, lse):
     seq = qkv.shape[0]
     width = qkv.shape[1] // 3
     pairs = width // PAIR_LANES
@@ -297,15 +317,16 @@
             column(2 * pairs),
             column(0),
             pl.BlockSpec((TEXT, PAIR_LANES), lambda i: (0, i)),
-            pl.BlockSpec((1, 8, seq), lambda i: (i, 0, 0)),
+            column(0),
+            pl.BlockSpec((1, seq, 8), lambda i: (i, 0, 0)),
         ],
         out_specs=pl.BlockSpec((3, seq, PAIR_LANES), lambda i: (0, 0, i)),
         out_shape=jax.ShapeDtypeStruct((3, seq, width), bf16),
         scratch_shapes=[pltpu.VMEM((seq, PAIR_LANES), f32)] * 2,
         compiler_params=params(),
-        cost_estimate=cost(25),
+        cost_estimate=cost(15),
         name="attend_grad",
-    )(rows_info, qkv, qkv, qkv, grad_ctx, pair_grad, lse)
+    )(rows_info, qkv, qkv, qkv, grad_ctx, pair_grad, ctx, lse)
 
 
 def gelu_pair(values):
@@ -330,7 +351,7 @@
 
 
 def expert_chunk(
-    row_ref, second, gbranch, upb, up_ref, down_ref, grad_refs, dupb_ref, branch, gsecond, scratch, begin
+    second, gbranch, upb, up_ref, down_ref, grad_ref, dupb_ref, branch, gsecond, scratch, begin
 ):
     pre, gact, act, gpre = scratch
     rows, width = act.shape
@@ -348,16 +369,12 @@
         gpre[at, :] = rounded
         return total + rounded.astype(f32)
 
-    total = lax.fori_loop(0, rows // tile, body, jnp.zeros((tile, width), f32))
+    total = lax.fori_loop(0, rows // tile, body, jnp.zeros((tile, width), f32), unroll=True)
     dupb_ref[...] = jnp.sum(total, axis=0, keepdims=True)
     for which, grad in enumerate(
         (dot_tn(second[...], gpre[...]), dot_tn(act[...], gbranch[...]))
     ):
-        grad, shape = grad.astype(bf16), grad_refs[0].shape[1:]
-        if len(grad_refs) == 1:
-            grad_refs[0][which] = grad.reshape(shape)
-        else:
-            grad_refs[0][which], grad_refs[1][which] = split_by_core(row_ref, grad, shape)
+        grad_ref[which] = grad.astype(bf16).reshape(grad_ref.shape[1:])
     own_branch = dot_nn(act[...], down)
     own_gsecond = dot_nt(gpre[...], up)
 
@@ -372,7 +389,7 @@
         gsecond[...] += own_gsecond
 
 
-def expert_begin_kernel(
+def expert_kernel(
     row_ref,
     ctx_ref,
     pair_ref,
@@ -383,19 +400,25 @@
     wo_ref,
     up_ref,
     down_ref,
+    out_ref,
+    gmid_ref,
+    gctx_ref,
+    pair_grad_ref,
+    dwo_ref,
+    grad_ref,
+    dvec_ref,
+    dupb_ref,
     own_ctx,
     middle,
     second,
     gbranch,
     branch,
     gsecond,
-    grad_ref,
-    dvec_ref,
-    dupb_ref,
     *scratch,
 ):
     step = pl.program_id(0)
     rows, width = hidden_ref.shape
+    out_rows = out_ref.shape[0]
     tile = 16
 
     @pl.when(step == 0)
@@ -420,78 +443,24 @@
             gbranch[at, :] = rounded
             return total + rounded.astype(f32)
 
-        total = lax.fori_loop(0, rows // tile, body, jnp.zeros((tile, width), f32))
+        total = lax.fori_loop(
+            0, rows // tile, body, jnp.zeros((tile, width), f32), unroll=True
+        )
         dvec_ref[...] = jnp.zeros(dvec_ref.shape, f32)
         dvec_ref[2:3, :] = jnp.sum(total, axis=0, keepdims=True)
 
     expert_chunk(
-        row_ref,
         second,
         gbranch,
         upb_ref,
         up_ref,
         down_ref,
-        (grad_ref,),
+        grad_ref,
         dupb_ref,
         branch,
         gsecond,
         scratch,
         step == 0,
-    )
-
-
-def expert_end_kernel(
-    row_ref,
-    own_ctx,
-    middle,
-    second,
-    gbranch,
-    branch_in,
-    gsecond_in,
-    dvec_in,
-    cot_ref,
-    vec_ref,
-    upb_ref,
-    wo_ref,
-    up_ref,
-    down_ref,
-    out_ref,
-    gmid_ref,
-    gctx_ref,
-    pair_ref,
-    dwo_ref,
-    keep_ref,
-    send_ref,
-    dvec_ref,
-    dupb_ref,
-    branch,
-    gsecond,
-    rounded_ref,
-    *scratch,
-):
-    step = pl.program_id(0)
-    rows, width = middle.shape
-    out_rows = out_ref.shape[0]
-    tile = 16
-
-    @pl.when(step == 0)
-    def _():
-        branch[...] = branch_in[...]
-        gsecond[...] = gsecond_in[...]
-
-    expert_chunk(
-        row_ref,
-        second,
-        gbranch,
-        upb_ref,
-        up_ref,
-        down_ref,
-        (keep_ref, send_ref),
-        dupb_ref,
-        branch,
-        gsecond,
-        scratch,
-        step < 0,
     )
 
     @pl.when(step == pl.num_programs(0) - 1)
@@ -508,7 +477,7 @@
             grad_mid = jnp.where(kept, cot_ref[at, :], 0.0) + grad_in
             gmid_ref[at, :] = grad_mid
             rounded = grad_mid.astype(bf16)
-            rounded_ref[at, :] = rounded
+            gbranch[at, :] = rounded
             return (
                 totals[0] + grad_out * normal,
                 totals[1] + grad_out,
@@ -516,51 +485,31 @@
             )
 
         zero = jnp.zeros((tile, width), f32)
-        gains, shifts, biases = lax.fori_loop(0, rows // tile, body, (zero, zero, zero))
-        dvec_ref[...] = dvec_in[...]
+        gains, shifts, biases = lax.fori_loop(
+            0, rows // tile, body, (zero, zero, zero), unroll=True
+        )
         dvec_ref[0:1, :] = jnp.sum(gains, axis=0, keepdims=True)
         dvec_ref[1:2, :] = jnp.sum(shifts, axis=0, keepdims=True)
         dvec_ref[3:4, :] = jnp.sum(biases, axis=0, keepdims=True)
-        out_ref[...] = branch[0:out_rows, :]
-        dwo_ref[...] = dot_tn(own_ctx[...], rounded_ref[...]).astype(bf16)
-        grad_ctx = dot_nt(rounded_ref[...], wo_ref[0]).astype(bf16)
+        out_ref[...] = branch[0:out_rows, :].reshape(out_ref.shape)
+        dwo_ref[...] = dot_tn(own_ctx[...], gbranch[...]).astype(bf16)
+        grad_ctx = dot_nt(gbranch[...], wo_ref[0]).astype(bf16)
         gctx_ref[...] = jnp.zeros(gctx_ref.shape, bf16)
         gctx_ref[pl.ds(pl.multiple_of(row_ref[0], 16), rows), :] = grad_ctx
-        pair_ref[...] = grad_ctx[: pair_ref.shape[0]]
-
-
-def expert_specs(rows, width, ffn_parts, half):
+        pair_grad_ref[...] = grad_ctx[: pair_grad_ref.shape[0]]
+
+
+def expert(rows_info, ctx, pair_ctx, hidden, cot, vec, up_bias, w_attn, ffn_parts, out_rows):
+    rows, width = hidden.shape
+    seq = ctx.shape[0]
     _, row_blocks, chunks, size, _ = ffn_parts.shape
-    base = half * (chunks // 2)
 
     def weights(which):
-        return pl.BlockSpec(
-            (1, row_blocks, 1, size, width), lambda i: (which, 0, base + i, 0, 0)
-        )
-
-    inputs = [
-        pl.BlockSpec((1, width), lambda i: (0, base + i)),
-        pl.BlockSpec((1, width, width), lambda i: (3, 0, 0)),
-        weights(0),
-        weights(1),
-    ]
-    outs = 1 + half
-    per_out = row_blocks // outs
-    grad_spec = [pl.BlockSpec((2, per_out, 1, size, width), lambda i: (0, 0, i, 0, 0))] * outs
-    grad_shape = [jax.ShapeDtypeStruct((2, per_out, chunks // 2, size, width), bf16)] * outs
-    bias_spec = pl.BlockSpec((1, width), lambda i: (0, i))
-    bias_shape = jax.ShapeDtypeStruct((1, chunks // 2 * width), f32)
-    scratch = [pltpu.VMEM((rows, width), f32)] * 2 + [pltpu.VMEM((rows, width), bf16)] * 2
-    return inputs, (grad_spec, grad_shape), (bias_spec, bias_shape), scratch
-
-
-def expert_begin(rows_info, ctx, pair_ctx, hidden, cot, vec, up_bias, w_attn, ffn_parts):
-    rows, width = hidden.shape
-    inputs, grads, biases, scratch = expert_specs(rows, width, ffn_parts, 0)
-    kept = [bf16, f32, bf16, bf16, f32, f32]
+        return pl.BlockSpec((1, row_blocks, 1, size, width), lambda i: (which, 0, i, 0, 0))
+
     return pl.pallas_call(
-        expert_begin_kernel,
-        grid=(ffn_parts.shape[2] // 2,),
+        expert_kernel,
+        grid=(chunks,),
         in_specs=[
             SMEM_SPEC,
             whole(ctx.shape),
@@ -568,57 +517,47 @@
             whole(hidden.shape),
             whole(cot.shape),
             whole(vec.shape),
-            *inputs,
+            pl.BlockSpec((1, width), lambda i: (0, i)),
+            pl.BlockSpec((1, width, width), lambda i: (3, 0, 0)),
+            weights(0),
+            weights(1),
         ],
-        out_specs=[whole((rows, width))] * 6 + [*grads[0], whole((8, width)), biases[0]],
-        out_shape=[jax.ShapeDtypeStruct((rows, width), kind) for kind in kept]
-        + [*grads[1], jax.ShapeDtypeStruct((8, width), f32), biases[1]],
-        scratch_shapes=scratch,
-        compiler_params=params(),
-        cost_estimate=cost(28),
-        name="expert_begin",
-    )(rows_info, ctx, pair_ctx, hidden, cot, vec, up_bias, w_attn, ffn_parts, ffn_parts)
-
-
-def expert_end(rows_info, kept, late, cot, vec, up_bias, w_attn, ffn_parts, seq, out_rows):
-    rows, width = cot.shape
-    inputs, grads, biases, scratch = expert_specs(rows, width, ffn_parts, 1)
-    return pl.pallas_call(
-        expert_end_kernel,
-        grid=(ffn_parts.shape[2] // 2,),
-        in_specs=[SMEM_SPEC]
-        + [whole((rows, width))] * 6
-        + [whole(late.shape), whole(cot.shape), whole(vec.shape), *inputs],
         out_specs=[
-            whole((out_rows, width)),
+            whole((out_rows, 1, width)),
             whole((rows, width)),
             whole((seq, width)),
             whole((TEXT, width)),
             whole((width, width)),
-            *grads[0],
+            pl.BlockSpec((2, row_blocks, 1, size, width), lambda i: (0, 0, i, 0, 0)),
             whole((8, width)),
-            biases[0],
+            pl.BlockSpec((1, width), lambda i: (0, i)),
         ],
         out_shape=[
-            jax.ShapeDtypeStruct((out_rows, width), f32),
+            jax.ShapeDtypeStruct((out_rows, 1, width), f32),
             jax.ShapeDtypeStruct((rows, width), f32),
             jax.ShapeDtypeStruct((seq, width), bf16),
             jax.ShapeDtypeStruct((TEXT, width), bf16),
             jax.ShapeDtypeStruct((width, width), bf16),
-            *grads[1],
+            jax.ShapeDtypeStruct(ffn_parts.shape, bf16),
             jax.ShapeDtypeStruct((8, width), f32),
-            biases[1],
+            jax.ShapeDtypeStruct((1, chunks * width), f32),
         ],
         scratch_shapes=[
+            pltpu.VMEM((rows, width), bf16),
+            pltpu.VMEM((rows, width), f32),
+            pltpu.VMEM((rows, width), bf16),
+            pltpu.VMEM((rows, width), bf16),
+            pltpu.VMEM((rows, width), f32),
+            pltpu.VMEM((rows, width), f32),
             pltpu.VMEM((rows, width), f32),
             pltpu.VMEM((rows, width), f32),
             pltpu.VMEM((rows, width), bf16),
-            *scratch,
+            pltpu.VMEM((rows, width), bf16),
         ],
         compiler_params=params(),
-        cost_estimate=cost(30),
-        name="expert_end",
-    )(rows_info, *kept, late, cot, vec, up_bias, w_attn, ffn_parts, ffn_parts)
+        cost_estimate=cost(43),
+        name="expert",
+    )(rows_info, ctx, pair_ctx, hidden, cot, vec, up_bias, w_attn, ffn_parts, ffn_parts)
 
 
 def project_grad_kernel(
@@ -717,8 +656,8 @@
         return totals[0] + grad_out * normal, totals[1] + grad_out
 
     zero = jnp.zeros((tile, width), f32)
-    gains, shifts = lax.fori_loop(0, rows // tile, body, (zero, zero))
-    out_ref[...] = own[0 : out_ref.shape[0], :]
+    gains, shifts = lax.fori_loop(0, rows // tile, body, (zero, zero), unroll=True)
+    out_ref[...] = own[0 : out_ref.shape[0], :].reshape(out_ref.shape)
     own_rows = (
         jnp.sum(gains, axis=0, keepdims=True),
         jnp.sum(shifts, axis=0, keepdims=True),
@@ -732,38 +671,41 @@
     top = jnp.where(row == 2, late_ref[3:4, :], top)
     for i, value in enumerate(own_rows):
         top = jnp.where(row == 3 + 5 * row_ref[3] + i, value, top)
-    small_ref[0:16, :] = top
+    small_ref[0:16, :] = top.astype(small_ref.dtype)
     row = lax.broadcasted_iota(jnp.int32, (8, width), 0)
     bias = jnp.zeros((8, width), f32)
     for i in range(upb_ref.shape[0]):
         bias = jnp.where(row == upb_ref.shape[0] * row_ref[3] + i, upb_ref[i : i + 1, :], bias)
-    small_ref[16:24, :] = bias
+    small_ref[16:32, :] = jnp.concatenate([bias, jnp.zeros_like(bias)], axis=0).astype(small_ref.dtype)
     grads = own[...]
     high = grads.astype(bf16)
     low = (grads - high.astype(f32)).astype(bf16)
     table = lax.broadcasted_iota(jnp.int32, (rows, rows), 0)
     chosen = jnp.where(row_ref[3] == 0, pos_ref[...], -1) == table
     chosen = jnp.where(chosen, 1.0, 0.0).astype(bf16)
-    small_ref[24 : 24 + rows, :] = dot_nn(chosen, high) + dot_nn(chosen, low)
-    small_ref[24 + rows :, :] = jnp.zeros((small_ref.shape[0] - 24 - rows, width), f32)
+    sums = dot_nn(chosen, high) + dot_nn(chosen, low)
+    small_ref[32 : 32 + rows, :] = sums.astype(small_ref.dtype)
+    spare = small_ref.shape[0] - 32 - rows
+    if spare:
+        small_ref[32 + rows :, :] = jnp.zeros((spare, width), small_ref.dtype)
 
 
 def first_grad(
     rows_info, gfirst, pair_grad, hidden, grad_middle, vec, sums, late, up_bias, pos, out_rows
 ):
     rows, width = hidden.shape
-    small = round_up(24 + rows, 128)
+    small = round_up(32 + rows, 128)
     args = (gfirst, pair_grad, hidden, grad_middle, vec, sums, late, up_bias, pos)
     return pl.pallas_call(
         first_grad_kernel,
         in_specs=[SMEM_SPEC] + [whole(arg.shape) for arg in args],
-        out_specs=[whole((out_rows, width)), whole((small, width))],
+        out_specs=[whole((out_rows, 1, width)), whole((small, width))],
         out_shape=[
-            jax.ShapeDtypeStruct((out_rows, width), f32),
-            jax.ShapeDtypeStruct((small, width), f32),
+            jax.ShapeDtypeStruct((out_rows, 1, width), f32),
+            jax.ShapeDtypeStruct((small, width), bf16),
         ],
         scratch_shapes=[pltpu.VMEM((rows, width), f32)],
-        compiler_params=params(),
+        compiler_params=params(24),
         cost_estimate=cost(8),
         name="first_grad",
     )(rows_info, *args)
@@ -827,7 +769,8 @@
         mats = [times(left_parts(fourth), right_parts(mat)) for fourth, mat in zip(fourths, mats)]
 
 
-def shampoo_kernel(group, part, parts, grad_count, earlier, up_ref, *refs):
+def shampoo_kernel(group, begin, parts, grad_count, earlier, up_ref, *refs):
+    part = begin + pl.program_id(0)
     grad_refs = refs[:grad_count]
     left_ref, right_ref, w_ref = refs[grad_count : grad_count + 3]
     outs = refs[grad_count + 3 + earlier : grad_count + 7 + earlier]
@@ -873,21 +816,21 @@
         copy.wait()
 
 
-def shampoo(is_up, part, at, grad_rows, lefts, rights, weights, earlier=()):
+def shampoo(is_up, begin, end, grad_rows, lefts, rights, weights, earlier=(), mebibytes=24):
     parts, count, size, _ = lefts.shape
     span = count * size
-    blocks = pl.BlockSpec((1, count, size, size), lambda i: (part, 0, 0, 0))
+    blocks = pl.BlockSpec((1, count, size, size), lambda i: (begin + i, 0, 0, 0))
     shape = jax.ShapeDtypeStruct((parts * count, size, size), f32)
     anywhere = pl.BlockSpec(memory_space=pl.ANY)
     first_earlier = 4 + len(grad_rows)
     kernel = functools.partial(
-        shampoo_kernel, math.gcd(count, 4), part, parts, len(grad_rows), len(earlier)
+        shampoo_kernel, math.gcd(count, 8), begin, parts, len(grad_rows), len(earlier)
     )
     return pl.pallas_call(
         kernel,
-        grid=(1,),
+        grid=(end - begin,),
         in_specs=[SMEM_SPEC]
-        + [pl.BlockSpec((1, size, span), lambda i: (at, 0, 0))] * len(grad_rows)
+        + [pl.BlockSpec((1, size, span), lambda i: (begin + i, 0, 0))] * len(grad_rows)
         + [blocks] * 3
         + [anywhere] * len(earlier),
         out_specs=[anywhere] * 4,
@@ -897,10 +840,45 @@
             pltpu.SemaphoreType.DMA((4, count)),
         ],
         input_output_aliases={first_earlier + i: i for i in range(len(earlier))},
-        compiler_params=params(),
+        compiler_params=params(mebibytes),
         cost_estimate=cost(9),
         name="shampoo",
     )(is_up, *grad_rows, lefts, rights, weights, *earlier)
+
+
+def momentum_kernel(
+    vector_rate, pos_rate, sum_ref, v_ref, vm_ref, b_ref, bm_ref, p_ref, pm_ref, vm_out, v_out, bm_out, b_out, pm_out, p_out
+):
+    width = v_ref.shape[1]
+    new = moment_keep * vm_ref[...] + sum_ref[0 : v_ref.shape[0], :].astype(f32)
+    vm_out[...] = new
+    v_out[...] = v_ref[...] - vector_rate * new
+    per_row = b_ref.shape[1] // width
+    rows = sum_ref[16:32, :].astype(f32)
+    for i in range(b_ref.shape[0]):
+        for j in range(per_row):
+            at = (slice(i, i + 1), slice(j * width, (j + 1) * width))
+            row = i * per_row + j
+            new = moment_keep * bm_ref[at] + rows[row : row + 1, :]
+            bm_out[at] = new
+            b_out[at] = b_ref[at] - vector_rate * new
+    new = moment_keep * pm_ref[...] + sum_ref[32 : 32 + p_ref.shape[0], :].astype(f32)
+    pm_out[...] = new
+    p_out[...] = p_ref[...] - pos_rate * new
+
+
+def momentum_step(sums, vectors, vectors_mom, bias, bias_mom, table, table_mom, vector_rate, pos_rate):
+    args = (sums, vectors, vectors_mom, bias, bias_mom, table, table_mom)
+    outs = (vectors, vectors, bias, bias, table, table)
+    return pl.pallas_call(
+        functools.partial(momentum_kernel, vector_rate, pos_rate),
+        in_specs=[whole(arg.shape) for arg in args],
+        out_specs=[whole(out.shape) for out in outs],
+        out_shape=[jax.ShapeDtypeStruct(out.shape, f32) for out in outs],
+        compiler_params=params(),
+        cost_estimate=cost(3),
+        name="momentum",
+    )(*args)
 
 
 CORE, Y, Z_LOW, Z_HIGH = 1, 2, 4, 8
@@ -1007,8 +985,11 @@
     hidden = stream_in[0, 0] + image_flag * jnp.take(pos_table, pos_index[0], axis=0)
     hidden = jnp.pad(hidden, pad)
     pos = jnp.pad(pos_index[0], pad[0], constant_values=-1)[None]
+    first = first_norm(rows_info, hidden, vec, seq)
     if by_rows:
-        along_z, ffn_rows, hidden, cotangent = sync(along_z, ffn_rows, hidden, cotangent)
+        along_z, hidden, first, cotangent, up_bias, pos = sync(
+            along_z, hidden, first, cotangent, up_bias, pos
+        )
         ffn_parts = lax.all_gather(ffn_rows, "dp", axis=0, tiled=True)
         ffn_parts = ffn_parts.reshape(2, row_blocks, chunks, size, width)
         near = in_order(z % 2, own_attn, along_z[0])
@@ -1016,7 +997,6 @@
         attn_z = in_order(z // 2, near, far).reshape(4, size, width)
         upper, lower = attn_z[:, : size // 2], attn_z[:, size // 2 :]
         upper_y, lower_x = flip(upper, Y), flip_mod(lower)
-    first = first_norm(rows_info, hidden, vec, seq)
     pair_first = lax.ppermute(first[:TEXT], "mod", to_image)
     if by_rows:
         upper_y, lower_x, first, pair_first, cotangent = sync(
@@ -1050,38 +1030,23 @@
     qkv, w_attn = project(rows_info, first, vec, attn_parts)
     ctx, lse, pair_ctx = attend(rows_info, qkv)
     pair_ctx = lax.ppermute(pair_ctx, "mod", to_text)
-    *kept, grad_1, late_vec, up_bias_grad_1 = expert_begin(
-        rows_info, ctx, pair_ctx, hidden, cot, vec, up_bias, w_attn, ffn_parts
+    stream_out, grad_middle, grad_ctx, pair_grad, grad_wo, grad_ffn, late_vec, up_bias_grad = expert(
+        rows_info, ctx, pair_ctx, hidden, cot, vec, up_bias, w_attn, ffn_parts, slots
     )
-    ended = expert_end(rows_info, kept, late_vec, cot, vec, up_bias, w_attn, ffn_parts, seq, slots)
-    stream_out, grad_middle, grad_ctx, pair_grad, grad_wo, keep_2, send_2, late_vec, up_bias_grad_2 = ended
     pair_grad = lax.ppermute(pair_grad, "mod", to_image)
 
     def along_z_of(parts):
         return [flip(part, bits * Z_LOW) for bits, part in enumerate(parts) if bits]
 
     if by_rows:
-        ffn_1 = lax.psum_scatter(
-            grad_1.reshape(-1, chunks // 2, size, width), "dp", scatter_dimension=0, tiled=True
+        ffn_sum = lax.psum_scatter(
+            grad_ffn.reshape(-1, chunks, size, width), "dp", scatter_dimension=0, tiled=True
         )[0]
-        got_2 = flip(send_2, CORE)
-        pair_grad, got_2, grad_ctx = sync(pair_grad, got_2, grad_ctx)
-        both = plus(keep_2, got_2).reshape((4, 2) + keep_2.shape[2:])
-        keep_2, send_2, grad_ctx = sync(pick(both, y, 1), pick(both, 1 - y, 1), grad_ctx)
-        got_2 = flip(send_2, Y)
-    grad_qkv = attend_grad(rows_info, qkv, grad_ctx, pair_grad, lse)
-    if by_rows:
-        got_2, grad_qkv = sync(got_2, grad_qkv)
-        both = plus(keep_2, got_2)
-        ffn_2 = [pick(both, z ^ bits, 0) for bits in range(4)]
-        ffn_2, grad_qkv = sync(ffn_2, grad_qkv)
-        got_2 = along_z_of(ffn_2)
-    projected = project_grad(rows_info, grad_qkv, first, w_attn, grad_wo, size)
-    if by_rows:
-        projected, ffn_1, got_2 = sync(projected, ffn_1, got_2)
-    attn_keep, attn_send, grad_first, pair_first_grad, sums = projected
+    grad_qkv = attend_grad(rows_info, qkv, grad_ctx, pair_grad, ctx, lse)
+    attn_keep, attn_send, grad_first, pair_first_grad, sums = project_grad(
+        rows_info, grad_qkv, first, w_attn, grad_wo, size
+    )
     pair_first_grad = lax.ppermute(pair_first_grad, "mod", to_text)
-    up_bias_grad = jnp.concatenate([up_bias_grad_1, up_bias_grad_2], axis=1)
     up_bias_grad = jnp.swapaxes(up_bias_grad.reshape(chunks, row_blocks, size), 0, 1)
     if by_rows:
         attn_got = flip(attn_send, CORE)
@@ -1107,58 +1072,58 @@
         pos,
         slots,
     )
+    stream_out = stream_out.reshape(stream_in.shape)
+    stream_grad = stream_grad.reshape(stream_in.shape)
     if by_rows:
-        small = small.astype(bf16).reshape(2, 2, 4, -1, width)
+        small = small.reshape(2, 2, 4, -1, width)
         small_keep, small_send = pick(small, core, 0), pick(small, 1 - core, 0)
         small_got = flip(small_send, CORE)
         upper_got, lower_got, small_got = sync(upper_got, lower_got, small_got)
         upper, lower = plus(upper_keep, upper_got), plus(lower_keep, lower_got)
+        small = plus(small_keep, small_got)
+        upper = jnp.concatenate([upper, jnp.swapaxes(small, 0, 1)], axis=2)
         upper_keep, upper_send = pick(upper, y, 1), pick(upper, 1 - y, 1)
         lower_keep, lower_send = pick(lower, modality, 0), pick(lower, 1 - modality, 0)
-        small = plus(small_keep, small_got)
-        small_keep, small_send = pick(small, y, 0), pick(small, 1 - y, 0)
-        small_keep, small_send, upper_keep, upper_send, lower_keep, lower_send, ffn_1 = sync(
-            small_keep, small_send, upper_keep, upper_send, lower_keep, lower_send, ffn_1
+        upper_keep, upper_send, lower_keep, lower_send = sync(
+            upper_keep, upper_send, lower_keep, lower_send
         )
         upper_got, lower_got = flip(upper_send, Y), flip_mod(lower_send)
-        small_got = flip(small_send, Y)
-        ffn_new = shampoo(is_up, 0, 0, [ffn_1], *ffn_old)
-        ffn_new, small_got, upper_got, lower_got = sync(ffn_new, small_got, upper_got, lower_got)
-        attn = jnp.concatenate([plus(upper_keep, upper_got), plus(lower_keep, lower_got)], axis=1)
+        attn = jnp.concatenate([plus(lower_keep, lower_got), plus(upper_keep, upper_got)], axis=1)
         attn_z = [pick(attn, z ^ bits, 0) for bits in range(4)]
-        small = plus(small_keep, small_got)
-        small_z = [pick(small, z ^ bits, 0) for bits in range(4)]
-        small_z, attn_z, ffn_new = sync(small_z, attn_z, ffn_new)
         attn_got = along_z_of(attn_z)
-        small_got = along_z_of(small_z)
-        ffn_new = shampoo(is_up, 1, 1, [ffn_1], *ffn_old, ffn_new)
-        ffn_new, small_got = sync(ffn_new, small_got)
-        small = sum(part.astype(f32) for part in (small_z[0], *small_got))
-        small, ffn_new = sync(small, ffn_new)
+        attn_got = sync(*attn_got)
+        small = sum(part[size:].astype(f32) for part in (attn_z[0], *attn_got))
+        half = size // 2
+        attn_rows = [
+            jnp.concatenate([part[half:size], part[:half]], axis=0)[None]
+            for part in (attn_z[0], *attn_got)
+        ]
+        small, attn_rows = sync(small, attn_rows)
         small_got = flip_mod(small)
-        ffn_new = shampoo(is_up, 2, 0, [ffn_2[0], *got_2], *ffn_old, ffn_new)
-        ffn_new, small_got = sync(ffn_new, small_got)
+        attn_old = [part[None] for part in (attn_left, attn_right, attn_blocks)]
+        attn_out = shampoo(is_not, 0, 1, attn_rows, *attn_old, mebibytes=56)
+        attn_out, small_got = sync(attn_out, small_got)
         small = (small + small_got).astype(bf16)
-        small, ffn_new = sync(small, ffn_new)
-        small_got = [flip(small, bits * Z_LOW) for bits in (1, 2, 3)]
-        ffn_out = shampoo(is_up, 3, 1, [ffn_2[0], *got_2], *ffn_old, ffn_new)
-        small_got, attn_got, ffn_out = sync(small_got, attn_got, ffn_out)
-        near = in_order(z % 2, small, small_got[0])
-        far = in_order(z % 2, small_got[1], small_got[2])
-        small = in_order(z // 2, near, far)
-        small, attn_got = sync(small, attn_got)
+        small, ffn_sum = sync(small, ffn_sum)
+        small_got = flip(small, Z_LOW)
+        ffn_new = shampoo(is_up, 0, 1, [ffn_sum], *ffn_old)
+        small_got, ffn_new = sync(small_got, ffn_new)
+        small, ffn_new = sync(in_order(z % 2, small, small_got), ffn_new)
+        small_got = flip(small, Z_HIGH)
+        ffn_new = shampoo(is_up, 1, 2, [ffn_sum], *ffn_old, ffn_new)
+        small_got, ffn_new = sync(small_got, ffn_new)
+        small, ffn_new = sync(in_order(z // 2, small, small_got), ffn_new)
         small_got = flip(small, Y)
-        attn_rows = [part[None] for part in (attn_z[0], *attn_got)]
-        attn_old = [part[None] for part in (attn_left, attn_right, attn_blocks)]
-        attn_out = shampoo(is_not, 0, 0, attn_rows, *attn_old)
-        small_got, attn_out = sync(small_got, attn_out)
-        small = in_order(y, small, small_got)
-        small_sum = in_order(core, small, flip(small, CORE)).astype(f32).reshape(-1, width)
+        ffn_new = shampoo(is_up, 2, 3, [ffn_sum], *ffn_old, ffn_new)
+        small_got, ffn_new = sync(small_got, ffn_new)
+        small, ffn_new = sync(in_order(y, small, small_got), ffn_new)
+        small_got = flip(small, CORE)
+        ffn_out = shampoo(is_up, 3, 4, [ffn_sum], *ffn_old, ffn_new)
+        small_got, ffn_out = sync(small_got, ffn_out)
+        small_sum = in_order(core, small, small_got).reshape(-1, width)
     else:
-        grad_2 = jnp.stack([keep_2, send_2], axis=2).reshape(grad_1.shape)
-        grads = jnp.concatenate([grad_1, grad_2], axis=2)
-        up = grads[0].reshape(row_blocks, chunks, size, row_blocks, size)
-        down = grads[1].reshape(row_blocks, chunks, size, row_blocks, size)
+        up = grad_ffn[0].reshape(row_blocks, chunks, size, row_blocks, size)
+        down = grad_ffn[1].reshape(row_blocks, chunks, size, row_blocks, size)
         up = up.transpose(0, 3, 1, 2, 4).reshape(-1, size, size)
         down = down.transpose(0, 1, 3, 2, 4).reshape(-1, size, size)
         ffn_sum = lax.psum_scatter(
@@ -1168,32 +1133,24 @@
         attn_sum = lax.psum_scatter(
             parts_to_blocks(attn_full), ("mod", "dp"), scatter_dimension=0, tiled=True
         )
-        small_sum = lax.psum(small, ("mod", "dp"))
+        small_sum = lax.psum(small.astype(f32), ("mod", "dp")).astype(bf16)
         ffn_old = [part for part in (ffn_left, ffn_right, ffn_blocks)]
         attn_old = [part[None] for part in (attn_left, attn_right, attn_blocks)]
-        ffn_out = shampoo(is_not, 0, 0, [square_parts(ffn_sum, 1, ffn_sum.shape[0])], *ffn_old)
-        attn_out = shampoo(is_not, 0, 0, [square_parts(attn_sum, 1, attn_sum.shape[0])], *attn_old)
+        ffn_out = shampoo(is_not, 0, 1, [square_parts(ffn_sum, 1, ffn_sum.shape[0])], *ffn_old)
+        attn_out = shampoo(is_not, 0, 1, [square_parts(attn_sum, 1, attn_sum.shape[0])], *attn_old)
 
     items_total = lax.axis_size("dp")
     vector_rate = 0.3 / math.sqrt(items_total * slots)
     pos_rate = 0.5 / math.sqrt(items_total)
-    vectors_mom_new = moment_keep * vectors_mom + small_sum[: vectors.shape[0]]
-    vectors_new = vectors - vector_rate * vectors_mom_new
-    ffn_bias_mom_new = moment_keep * ffn_bias_mom + small_sum[16:24].reshape(ffn_bias.shape)
-    ffn_bias_new = ffn_bias - vector_rate * ffn_bias_mom_new
-    pos_mom_new = moment_keep * pos_mom + small_sum[24 : 24 + slots]
-    pos_new = pos_table - pos_rate * pos_mom_new
+    vector_news = momentum_step(
+        small_sum, vectors, vectors_mom, ffn_bias, ffn_bias_mom, pos_table, pos_mom, vector_rate, pos_rate
+    )
     return (
-        stream_out[None, None],
-        stream_grad[None, None],
+        stream_out,
+        stream_grad,
         *attn_out,
         *(part[None] for part in ffn_out),
-        vectors_mom_new,
-        vectors_new,
-        ffn_bias_mom_new,
-        ffn_bias_new,
-        pos_mom_new,
-        pos_new,
+        *vector_news,
     )
 
 

time: 393 us -> 350 us (0.89)
  the two profiles are of different devices: /device:TPU:0 before, /device:TPU:11 now
where the time goes in v3:
time: 350 us; the launch traced here: 343 us
  Pallas kernels  143 us (41%)
  waiting for transfers between devices  86.2 us (25%)
  starting transfers between devices  49.4 us (14%)
  local copies, waits for them, and re-layouts  24.9 us (7%)
  other arithmetic  24.4 us (7%)
  between operations  15.5 us (4%)
    ppermute x18, waiting for transfers between devices, flip(): return lax.ppermute(values, 'dp', [(i, i ^ bits) for i in range(size)])  58.6 us
    pallas_call x1, Pallas kernels, expert(): pl.pallas_call(expert_kernel, grid=(chunks,), in_specs=[SMEM_SPEC, whole(...  37.1 us
    pallas_call x5, Pallas kernels, shampoo(): pl.pallas_call(kernel, grid=(end - begin,), in_specs=[SMEM_SPEC] + [pl.Bl...  36.3 us
    ppermute x18, starting transfers between devices, flip(): return lax.ppermute(values, 'dp', [(i, i ^ bits) for i in range(size)])  31.6 us
    pallas_call x1, Pallas kernels, attend_grad(): pl.pallas_call(attend_grad_kernel, grid=(pairs,), in_specs=[SMEM_SPEC, co...  20.4 us
    pallas_call x1, Pallas kernels, attend(): pl.pallas_call(attend_kernel, grid=(pairs,), in_specs=[SMEM_SPEC, column(...  13.2 us
    ppermute x5, waiting for transfers between devices, flip_mod(): return lax.ppermute(values, 'mod', [(0, 1), (1, 0)])  12.9 us
    pallas_call x1, Pallas kernels, project_grad(): pl.pallas_call(project_grad_kernel, grid=(4,), in_specs=[SMEM_SPEC, pl.Bl...  11.5 us
  transfers between devices with their start and end apart: 29, of which 17 were waited for; matrix products, arithmetic and copies ran while one was open for 10% of the time, Pallas kernels for 29%

profile of v3, /device:TPU:11, one launch (start us, length us, event | category | flops | bytes accessed | tf_op | source)
XLA Modules:
  0.0 343.0 jit_solution(15886395980049448922)
XLA Ops:
  15.0 3.3 gather_fusion
  28.0 7.0 %collective-permute-done.2 = bf16[96,768]{1,0:T(8,128)(2,1)S(1)} collective-permute-done((bf16[96,768]{1,0:T(8,128)(2,1)}, bf16[96,768]{1,0:T(8,128)(2,1)S(1)}, u32[]{:S(2)}, u32[]{:S(2)}) %collective-permute-start.2) | collective-permute-done | bytes 147488 | tf_op jit(solution)/shard_map/ppermute | solution.py:889
  55.3 15.2 %collective-permute-start.9 = (bf16[2,2,4,48,768]{4,3,2,1,0:T(8,128)(2,1)S(1)}, bf16[2,2,4,48,768]{4,3,2,1,0:T(8,128)(2,1)S(1)}, u32[]{:S(2)}, u32[]{:S(2)}) collective-permute-start(bf16[2,2,4,48,768]{4,3,2,1,0:T(8,128)(2,1)S(1)} %pad_maximum_fusion.1.refs_2_), channel_id=1, source_target_pairs={{0,1},{1,0},{2,3},{3,2},{4,5},{5,4},{6,7},{7,6},{8,9},{9,8},{10,11... | collective-permute-start | bytes 3538952 | tf_op jit(solution)/shard_map/ppermute | solution.py:889
  75.7 7.6 %project.1 = (bf16[672,2304]{1,0:T(8,128)(2,1)}, bf16[4,768,768]{2,1,0:T(8,128)(2,1)}) custom-call(s32[6]{0:T(128)} %stack.122.row_ref, bf16[672,768]{1,0:T(8,128)(2,1)} %select_dynamic-update-slice_fusion.first_ref, f32[8,768]{1,0:T(8,128)} %pad_maximum_fusion.11.vec_ref, bf16[2,2,4,48,768]{4,3,2,1,0:T(8,128)(2,1)} %copy-done.18, ...), custom_call_target="tpu_custom_call" | custom-call | flops 8 | tf_op jit(solution)/shard_map/project/pallas_call | solution.py:152
  83.3 13.2 %attend.1 = (bf16[672,768]{1,0:T(8,128)(2,1)}, f32[6,672,8]{2,1,0:T(8,128)}, bf16[64,768]{1,0:T(8,128)(2,1)}) custom-call(s32[6]{0:T(128)} %stack.122.row_ref, bf16[672,2304]{1,0:T(8,128)(2,1)} %get-tuple-element.159.q_ref.k_ref.v_ref, bf16[672,2304]{1,0:T(8,128)(2,1)} %get-tuple-element.159.q_ref.k_ref.v_ref, ...), custom_call_target="tpu_custom_call" | custom-call | flops 12 | tf_op jit(solution)/shard_map/attend/pallas_call | solution.py:228
  98.0 5.9 %collective-permute-done.10.pair_ref = bf16[64,768]{1,0:T(8,128)(2,1)S(1)} collective-permute-done((bf16[64,768]{1,0:T(8,128)(2,1)}, bf16[64,768]{1,0:T(8,128)(2,1)S(1)}, u32[]{:S(2)}, u32[]{:S(2)}) %collective-permute-start.10) | collective-permute-done | bytes 98336 | tf_op jit(solution)/shard_map/ppermute | solution.py:1032
  104.6 37.1 %expert.1 = (f32[577,1,768]{2,1,0:T(1,128)}, f32[592,768]{1,0:T(8,128)}, bf16[672,768]{1,0:T(8,128)(2,1)}, bf16[64,768]{1,0:T(8,128)(2,1)}, bf16[768,768]{1,0:T(...) custom-call(s32[6]{0:T(128)} %stack.122.row_ref, ...), custom_call_target="tpu_custom_call" | custom-call | flops 43 | tf_op jit(solution)/shard_map/expert/pallas_call | solution.py:510
  146.1 20.4 %attend_grad.1.dqkv_ref = bf16[3,672,768]{2,1,0:T(8,128)(2,1)} custom-call(s32[6]{0:T(128)} %stack.122.row_ref, bf16[672,2304]{1,0:T(8,128)(2,1)} %get-tuple-element.159.q_ref.k_ref.v_ref, bf16[672,2304]{1,0:T(8,128)(2,1)} %get-tuple-element.159.q_ref.k_ref.v_ref, bf16[672,2304]{1,0:T(8,128)(2,1)} %get-tuple-element.159.q_ref.k_ref.v_ref, ...), custom_call_target="tpu_custom_call" | custom-call | flops 15 | tf_op jit(solution)/shard_map/attend_grad/pallas_call | solution.py:310
  166.5 11.5 %project_grad.1 = (bf16[4,4,96,768]{3,2,1,0:T(8,128)(2,1)}, bf16[4,4,96,768]{3,2,1,0:T(8,128)(2,1)}, f32[672,768]{1,0:T(8,128)}, f32[64,768]{1,0:T(8,128)}, f32[8,768]{1,0:T(8,128)}) custom-call(s32[6]{0:T(128)} %stack.122.row_ref, bf16[3,672,768]{2,1,0:T(8,128)(2,1)} %attend_grad.1.dqkv_ref, bf16[672,768]{1,0:T(8,128)(2,1)} %select_dynamic-update-slice_fusion.first_ref, ...), custom_call_target="tpu_custom_call" | custom-call | flops 15 | tf_op jit(solution)/shard_map/project_grad/pallas_call | solution.py:603
  182.3 6.0 %collective-permute-done.13.pair_ref = f32[64,768]{1,0:T(8,128)S(1)} collective-permute-done((f32[64,768]{1,0:T(8,128)}, f32[64,768]{1,0:T(8,128)S(1)}, u32[]{:S(2)}, u32[]{:S(2)}) %collective-permute-start.13) | collective-permute-done | bytes 196640 | tf_op jit(solution)/shard_map/ppermute | solution.py:1049
  195.4 4.1 %first_grad.1 = (f32[577,1,768]{2,1,0:T(1,128)}, bf16[640,768]{1,0:T(8,128)(2,1)S(1)}) custom-call(s32[6]{0:T(128)S(1)} %copy-done.10, f32[672,768]{1,0:T(8,128)S(1)} %copy-done.5, f32[64,768]{1,0:T(8,128)S(1)} %collective-permute-done.13.pair_ref, f32[592,768]{1,0:T(8,128)S(1)} %copy-done.2, f32[592,768]{1,0:T(8,128)S(1)} %copy-done.6, ...), custom_call_target="tpu_custom_call" | custom-call | flops 8 | tf_op jit(solution)/shard_map/first_grad/pallas_call | solution.py:699
  203.8 5.3 %collective-permute-done.14 = bf16[4,2,48,768]{3,2,0,1:T(8,128)(2,1)} collective-permute-done((bf16[4,2,48,768]{3,2,0,1:T(8,128)(2,1)}, bf16[4,2,48,768]{3,2,0,1:T(8,128)(2,1)}, u32[]{:S(2)}, u32[]{:S(2)}) %collective-permute-start.14) | collective-permute-done | bytes 589856 | tf_op jit(solution)/shard_map/ppermute | solution.py:893
  216.1 5.7 %collective-permute-done.17 = bf16[4,48,768]{2,1,0:T(8,128)(2,1)} collective-permute-done((bf16[4,48,768]{2,1,0:T(8,128)(2,1)}, bf16[4,48,768]{2,1,0:T(8,128)(2,1)}, u32[]{:S(2)}, u32[]{:S(2)}) %collective-permute-start.17) | collective-permute-done | bytes 294944 | tf_op jit(solution)/shard_map/ppermute | solution.py:893
  222.8 13.0 %collective-permute-done.18 = bf16[4,88,768]{2,1,0:T(8,128)(2,1)} collective-permute-done((bf16[4,88,768]{2,1,0:T(8,128)(2,1)}, bf16[4,88,768]{2,1,0:T(8,128)(2,1)}, u32[]{:S(2)}, u32[]{:S(2)}) %collective-permute-start.18) | collective-permute-done | bytes 540704 | tf_op jit(solution)/shard_map/ppermute | solution.py:889
  241.1 8.1 %collective-permute-done.19 = bf16[136,768]{1,0:T(8,128)(2,1)S(1)} collective-permute-done((bf16[136,768]{1,0:T(8,128)(2,1)S(1)}, bf16[136,768]{1,0:T(8,128)(2,1)S(1)}, u32[]{:S(2)}, u32[]{:S(2)}) %collective-permute-start.19) | collective-permute-done | bytes 208928 | tf_op jit(solution)/shard_map/ppermute | solution.py:889
  249.1 4.5 %collective-permute-done.20 = bf16[136,768]{1,0:T(8,128)(2,1)S(1)} collective-permute-done((bf16[136,768]{1,0:T(8,128)(2,1)S(1)}, bf16[136,768]{1,0:T(8,128)(2,1)S(1)}, u32[]{:S(2)}, u32[]{:S(2)}) %collective-permute-start.20) | collective-permute-done | bytes 208928 | tf_op jit(solution)/shard_map/ppermute | solution.py:889
  253.6 19.5 %collective-permute-done.21 = bf16[136,768]{1,0:T(8,128)(2,1)S(1)} collective-permute-done((bf16[136,768]{1,0:T(8,128)(2,1)S(1)}, bf16[136,768]{1,0:T(8,128)(2,1)S(1)}, u32[]{:S(2)}, u32[]{:S(2)}) %collective-permute-start.21) | collective-permute-done | bytes 208928 | tf_op jit(solution)/shard_map/ppermute | solution.py:889
  275.1 6.3 %collective-permute-start.22 = (f32[40,768]{1,0:T(8,128)S(1)}, f32[40,768]{1,0:T(8,128)S(1)}, u32[]{:S(2)}, u32[]{:S(2)}) collective-permute-start(f32[40,768]{1,0:T(8,128)S(1)} %fusion.14), channel_id=1, source_target_pairs={{0,16},{16,0},{1,17},{17,1},{2,18},{18,2},{3,19},{19,3},{4,20},{20... | collective-permute-start | bytes 368648 | tf_op jit(solution)/shard_map/ppermute | solution.py:893
  281.4 8.2 %shampoo.5 = (f32[8,96,96]{2,1,0:T(8,128)}, f32[8,96,96]{2,1,0:T(8,128)}, f32[8,96,96]{2,1,0:T(8,128)}, f32[8,96,96]{2,1,0:T(8,128)}) custom-call(s32[1]{0:T(128)} %constant.137.clone.1.up_ref, bf16[1,96,768]{2,1,0:T(8,128)(2,1)} %maximum_bitcast_fusion.refs_0_, bf16[1,96,768]{2,1,0:T(8,128)(2,1)} %maximum_bitcast_fusion.1.refs_1_, ...), custom_call_target="tpu_custom_call" | custom-call | flops 9 | tf_op jit(solution)/shard_map/shampoo/pallas_call | solution.py:829
  292.3 7.1 %shampoo.6 = (f32[32,96,96]{2,1,0:T(8,128)}, f32[32,96,96]{2,1,0:T(8,128)}, f32[32,96,96]{2,1,0:T(8,128)}, f32[32,96,96]{2,1,0:T(8,128)}) custom-call(s32[1]{0:T(128)} %bitcast.32.up_ref, bf16[4,96,768]{2,1,0:T(8,128)(2,1)S(1)} %bitcast.145, f32[4,8,96,96]{3,2,1,0:T(8,128)S(1)} %copy-done, f32[4,8,96,96]{3,2,1,0:T(8,128)S(1)} %get-tuple-element.217.refs_2_, ...), custom_call_target="tpu_custom_call" | custom-call | flops 9 | tf_op jit(solution)/shard_map/shampoo/pallas_call | solution.py:829
  301.5 6.8 %shampoo.7 = (f32[32,96,96]{2,1,0:T(8,128)}, f32[32,96,96]{2,1,0:T(8,128)}, f32[32,96,96]{2,1,0:T(8,128)}, f32[32,96,96]{2,1,0:T(8,128)}) custom-call(s32[1]{0:T(128)} %bitcast.32.up_ref, bf16[4,96,768]{2,1,0:T(8,128)(2,1)S(1)} %bitcast.146, f32[4,8,96,96]{3,2,1,0:T(8,128)S(1)} %copy-done, ...), custom_call_target="tpu_custom_call", output_to_operand_aliasing={{0}: (5, {}), {1}: (6, {}), {2}: (7, {}), {3}: (8, {})} | custom-call | flops 9 | tf_op jit(solution)/shard_map/shampoo/pallas_call | solution.py:829
  309.5 7.3 %shampoo.8 = (f32[32,96,96]{2,1,0:T(8,128)}, f32[32,96,96]{2,1,0:T(8,128)}, f32[32,96,96]{2,1,0:T(8,128)}, f32[32,96,96]{2,1,0:T(8,128)}) custom-call(s32[1]{0:T(128)} %bitcast.32.up_ref, bf16[4,96,768]{2,1,0:T(8,128)(2,1)S(1)} %bitcast.147, f32[4,8,96,96]{3,2,1,0:T(8,128)S(1)} %copy-done, ...), custom_call_target="tpu_custom_call", output_to_operand_aliasing={{0}: (5, {}), {1}: (6, {}), {2}: (7, {}), {3}: (8, {})} | custom-call | flops 9 | tf_op jit(solution)/shard_map/shampoo/pallas_call | solution.py:829
  322.4 6.9 %shampoo.9 = (f32[32,96,96]{2,1,0:T(8,128)}, f32[32,96,96]{2,1,0:T(8,128)}, f32[32,96,96]{2,1,0:T(8,128)}, f32[32,96,96]{2,1,0:T(8,128)}) custom-call(s32[1]{0:T(128)} %bitcast.32.up_ref, bf16[4,96,768]{2,1,0:T(8,128)(2,1)S(1)} %bitcast.148, f32[4,8,96,96]{3,2,1,0:T(8,128)S(1)} %copy-done.1, ...), custom_call_target="tpu_custom_call", output_to_operand_aliasing={{0}: (5, {}), {1}: (6, {}), {2}: (7, {}), {3}: (8, {})} | custom-call | flops 9 | tf_op jit(solution)/shard_map/shampoo/pallas_call | solution.py:829
  331.6 4.5 %momentum.1 = (f32[13,768]{1,0:T(8,128)}, f32[13,768]{1,0:T(8,128)}, f32[2,3072]{1,0:T(2,128)}, f32[2,3072]{1,0:T(2,128)}, f32[577,768]{1,0:T(8,128)}, /*index=5*/f32[577,768]{1,0:T(8,128)}) custom-call(bf16[640,768]{1,0:T(8,128)(2,1)} %bitcast.169, f32[13,768]{1,0:T(8,128)} %v_ref.1, f32[13,768]{1,0:T(8,128)} %vm_ref.1, f32[2,3072]{1,0:T(2,128)} %b_ref.1, ...), custom_call_target="tpu_custom_call" | custom-call | flops 3 | tf_op jit(solution)/shard_map/momentum/pallas_call | solution.py:873
  (186 shorter events, 93.4 us)
Async XLA Ops:
  7.2 96.8 %all-gather.2.cloned.1.call-start = ((), (), s32[]{:S(2)}) async-start(), calls=%async_computation.1 | async-start | bytes 10027008 | tf_op jit(solution)/shard_map/all_gather | solution.py:993
  10.5 279.2 %reduce-scatter.2.cloned.1.call-start = ((), (), s32[]{:S(2)}) async-start(), calls=%async_computation.2 | async-start | bytes 10027008 | tf_op jit(solution)/shard_map/reduce_scatter | solution.py:1042
  12.3 15.7 %collective-permute-start = (bf16[96,768]{1,0:T(8,128)(2,1)}, bf16[96,768]{1,0:T(8,128)(2,1)S(1)}, u32[]{:S(2)}, u32[]{:S(2)}) collective-permute-start(bf16[96,768]{1,0:T(8,128)(2,1)} %bitcast.172), channel_id=1, source_target_pairs={{0,4},{1,5},{2,6},{3,7},{4,0},{5,1},{6,2},{7,3},{8,12},{9,13},{10,... | collective-permute-start | bytes 442376 | tf_op jit(solution)/shard_map/ppermute | solution.py:889
  12.5 15.5 %collective-permute-start.1 = (bf16[96,768]{1,0:T(8,128)(2,1)}, bf16[96,768]{1,0:T(8,128)(2,1)S(1)}, u32[]{:S(2)}, u32[]{:S(2)}) collective-permute-start(bf16[96,768]{1,0:T(8,128)(2,1)} %bitcast.173), channel_id=1, source_target_pairs={{0,8},{1,9},{2,10},{3,11},{4,12},{5,13},{6,14},{7,15},{8,0},{9,1},... | collective-permute-start | bytes 442376 | tf_op jit(solution)/shard_map/ppermute | solution.py:889
  14.8 20.2 %collective-permute-start.2 = (bf16[96,768]{1,0:T(8,128)(2,1)}, bf16[96,768]{1,0:T(8,128)(2,1)S(1)}, u32[]{:S(2)}, u32[]{:S(2)}) collective-permute-start(bf16[96,768]{1,0:T(8,128)(2,1)} %bitcast.174), channel_id=1, source_target_pairs={{0,12},{1,13},{2,14},{3,15},{4,8},{5,9},{6,10},{7,11},{8,4},{9,5},... | collective-permute-start | bytes 442376 | tf_op jit(solution)/shard_map/ppermute | solution.py:889
  35.2 7.2 %collective-permute-start.3 = (bf16[4,48,768]{2,1,0:T(8,128)(2,1)S(1)}, bf16[4,48,768]{2,1,0:T(8,128)(2,1)S(1)}, u32[]{:S(2)}, u32[]{:S(2)}) collective-permute-start(bf16[4,48,768]{2,1,0:T(8,128)(2,1)S(1)} %get-tuple-element.351), channel_id=1, source_target_pairs={{0,2},{1,3},{2,0},{3,1},{4,6},{5,7},{6,4},{7,5},{8,10},{9,11},{10,... | collective-permute-start | bytes 884744 | tf_op jit(solution)/shard_map/ppermute | solution.py:889
  42.7 10.6 %collective-permute-start.7 = (bf16[2,4,48,768]{3,2,1,0:T(8,128)(2,1)S(1)}, bf16[2,4,48,768]{3,2,1,0:T(8,128)(2,1)S(1)}, u32[]{:S(2)}, u32[]{:S(2)}) collective-permute-start(bf16[2,4,48,768]{3,2,1,0:T(8,128)(2,1)S(1)} %pad_maximum_fusion.5), channel_id=1, source_target_pairs={{0,2},{1,3},{2,0},{3,1},{4,6},{5,7},{6,4},{7,5},{8,10},{9,11},{10,... | collective-permute-start | bytes 1769480 | tf_op jit(solution)/shard_map/ppermute | solution.py:889
  42.9 12.2 %collective-permute-start.6 = (bf16[2,4,48,768]{3,2,1,0:T(8,128)(2,1)S(1)}, bf16[2,4,48,768]{3,2,1,0:T(8,128)(2,1)S(1)}, u32[]{:S(2)}, u32[]{:S(2)}) collective-permute-start(bf16[2,4,48,768]{3,2,1,0:T(8,128)(2,1)S(1)} %pad_maximum_fusion.4), channel_id=1, source_target_pairs={{0,16},{16,0},{1,17},{17,1},{2,18},{18,2},{3,19},{19,3},{4,20},{20... | collective-permute-start | bytes 1769480 | tf_op jit(solution)/shard_map/ppermute | solution.py:893
  55.3 17.7 %collective-permute-start.9 = (bf16[2,2,4,48,768]{4,3,2,1,0:T(8,128)(2,1)S(1)}, bf16[2,2,4,48,768]{4,3,2,1,0:T(8,128)(2,1)S(1)}, u32[]{:S(2)}, u32[]{:S(2)}) collective-permute-start(bf16[2,2,4,48,768]{4,3,2,1,0:T(8,128)(2,1)S(1)} %pad_maximum_fusion.1.refs_2_), channel_id=1, source_target_pairs={{0,1},{1,0},{2,3},{3,2},{4,5},{5,4},{6,7},{7,6},{8,9},{9,8},{10,11... | collective-permute-start | bytes 3538952 | tf_op jit(solution)/shard_map/ppermute | solution.py:889
  96.5 7.5 %collective-permute-start.10 = (bf16[64,768]{1,0:T(8,128)(2,1)}, bf16[64,768]{1,0:T(8,128)(2,1)S(1)}, u32[]{:S(2)}, u32[]{:S(2)}) collective-permute-start(bf16[64,768]{1,0:T(8,128)(2,1)} %get-tuple-element.161), channel_id=1, source_target_pairs={{0,16},{1,17},{2,18},{3,19},{4,20},{5,21},{6,22},{7,23},{8,24},{9,... | collective-permute-start | bytes 294920 | tf_op jit(solution)/shard_map/ppermute | solution.py:1032
  178.0 10.4 %collective-permute-start.12 = (bf16[4,4,96,768]{3,2,1,0:T(8,128)(2,1)}, bf16[4,4,96,768]{3,2,1,0:T(8,128)(2,1)}, u32[]{:S(2)}, u32[]{:S(2)}) collective-permute-start(bf16[4,4,96,768]{3,2,1,0:T(8,128)(2,1)} %get-tuple-element.173), channel_id=1, source_target_pairs={{0,1},{1,0},{2,3},{3,2},{4,5},{5,4},{6,7},{7,6},{8,9},{9,8},{10,11... | collective-permute-start | bytes 7077896 | tf_op jit(solution)/shard_map/ppermute | solution.py:889
  179.7 8.7 %collective-permute-start.13 = (f32[64,768]{1,0:T(8,128)}, f32[64,768]{1,0:T(8,128)S(1)}, u32[]{:S(2)}, u32[]{:S(2)}) collective-permute-start(f32[64,768]{1,0:T(8,128)} %get-tuple-element.174), channel_id=1, source_target_pairs={{0,16},{1,17},{2,18},{3,19},{4,20},{5,21},{6,22},{7,23},{8,24},{9,... | collective-permute-start | bytes 589832 | tf_op jit(solution)/shard_map/ppermute | solution.py:1049
  194.6 14.5 %collective-permute-start.14 = (bf16[4,2,48,768]{3,2,0,1:T(8,128)(2,1)}, bf16[4,2,48,768]{3,2,0,1:T(8,128)(2,1)}, u32[]{:S(2)}, u32[]{:S(2)}) collective-permute-start(bf16[4,2,48,768]{3,2,0,1:T(8,128)(2,1)} %bitcast.140), channel_id=1, source_target_pairs={{0,16},{16,0},{1,17},{17,1},{2,18},{18,2},{3,19},{19,3},{4,20},{20... | collective-permute-start | bytes 1769480 | tf_op jit(solution)/shard_map/ppermute | solution.py:893
  194.6 14.5 %collective-permute-start.15 = (bf16[2,4,48,768]{3,2,1,0:T(8,128)(2,1)}, bf16[2,4,48,768]{3,2,1,0:T(8,128)(2,1)}, u32[]{:S(2)}, u32[]{:S(2)}) collective-permute-start(bf16[2,4,48,768]{3,2,1,0:T(8,128)(2,1)} %get-tuple-element.186), channel_id=1, source_target_pairs={{0,2},{1,3},{2,0},{3,1},{4,6},{5,7},{6,4},{7,5},{8,10},{9,11},{10,... | collective-permute-start | bytes 1769480 | tf_op jit(solution)/shard_map/ppermute | solution.py:889
  214.6 7.1 %collective-permute-start.17 = (bf16[4,48,768]{2,1,0:T(8,128)(2,1)}, bf16[4,48,768]{2,1,0:T(8,128)(2,1)}, u32[]{:S(2)}, u32[]{:S(2)}) collective-permute-start(bf16[4,48,768]{2,1,0:T(8,128)(2,1)} %get-tuple-element.193), channel_id=1, source_target_pairs={{0,16},{16,0},{1,17},{17,1},{2,18},{18,2},{3,19},{19,3},{4,20},{20... | collective-permute-start | bytes 884744 | tf_op jit(solution)/shard_map/ppermute | solution.py:893
  215.9 19.9 %collective-permute-start.18 = (bf16[4,88,768]{2,1,0:T(8,128)(2,1)}, bf16[4,88,768]{2,1,0:T(8,128)(2,1)}, u32[]{:S(2)}, u32[]{:S(2)}) collective-permute-start(bf16[4,88,768]{2,1,0:T(8,128)(2,1)} %get-tuple-element.195), channel_id=1, source_target_pairs={{0,2},{1,3},{2,0},{3,1},{4,6},{5,7},{6,4},{7,5},{8,10},{9,11},{10,... | collective-permute-start | bytes 1622024 | tf_op jit(solution)/shard_map/ppermute | solution.py:889
  237.2 11.9 %collective-permute-start.19 = (bf16[136,768]{1,0:T(8,128)(2,1)S(1)}, bf16[136,768]{1,0:T(8,128)(2,1)S(1)}, u32[]{:S(2)}, u32[]{:S(2)}) collective-permute-start(bf16[136,768]{1,0:T(8,128)(2,1)S(1)} %get-tuple-element.344), channel_id=1, source_target_pairs={{0,4},{1,5},{2,6},{3,7},{4,0},{5,1},{6,2},{7,3},{8,12},{9,13},{10,... | collective-permute-start | bytes 626696 | tf_op jit(solution)/shard_map/ppermute | solution.py:889
  239.1 14.5 %collective-permute-start.20 = (bf16[136,768]{1,0:T(8,128)(2,1)S(1)}, bf16[136,768]{1,0:T(8,128)(2,1)S(1)}, u32[]{:S(2)}, u32[]{:S(2)}) collective-permute-start(bf16[136,768]{1,0:T(8,128)(2,1)S(1)} %get-tuple-element.345), channel_id=1, source_target_pairs={{0,8},{1,9},{2,10},{3,11},{4,12},{5,13},{6,14},{7,15},{8,0},{9,1},... | collective-permute-start | bytes 626696 | tf_op jit(solution)/shard_map/ppermute | solution.py:889
  240.2 32.8 %collective-permute-start.21 = (bf16[136,768]{1,0:T(8,128)(2,1)S(1)}, bf16[136,768]{1,0:T(8,128)(2,1)S(1)}, u32[]{:S(2)}, u32[]{:S(2)}) collective-permute-start(bf16[136,768]{1,0:T(8,128)(2,1)S(1)} %get-tuple-element.342), channel_id=1, source_target_pairs={{0,12},{1,13},{2,14},{3,15},{4,8},{5,9},{6,10},{7,11},{8,4},{9,5},... | collective-permute-start | bytes 626696 | tf_op jit(solution)/shard_map/ppermute | solution.py:889
  275.1 14.5 %collective-permute-start.22 = (f32[40,768]{1,0:T(8,128)S(1)}, f32[40,768]{1,0:T(8,128)S(1)}, u32[]{:S(2)}, u32[]{:S(2)}) collective-permute-start(f32[40,768]{1,0:T(8,128)S(1)} %fusion.14), channel_id=1, source_target_pairs={{0,16},{16,0},{1,17},{17,1},{2,18},{18,2},{3,19},{19,3},{4,20},{20... | collective-permute-start | bytes 368648 | tf_op jit(solution)/shard_map/ppermute | solution.py:893
  289.7 9.7 %collective-permute-start.23 = (bf16[40,768]{1,0:T(8,128)(2,1)S(1)}, bf16[40,768]{1,0:T(8,128)(2,1)S(1)}, u32[]{:S(2)}, u32[]{:S(2)}) collective-permute-start(bf16[40,768]{1,0:T(8,128)(2,1)S(1)} %add_convert_fusion.5), channel_id=1, source_target_pairs={{0,4},{1,5},{2,6},{3,7},{4,0},{5,1},{6,2},{7,3},{8,12},{9,13},{10,... | collective-permute-start | bytes 184328 | tf_op jit(solution)/shard_map/ppermute | solution.py:889
  299.4 8.9 %collective-permute-start.24 = (bf16[2,40,768]{2,1,0:T(8,128)(2,1)S(1)}, bf16[2,40,768]{2,1,0:T(8,128)(2,1)S(1)}, u32[]{:S(2)}, u32[]{:S(2)}) collective-permute-start(bf16[2,40,768]{2,1,0:T(8,128)(2,1)S(1)} %pad_maximum_fusion.10), channel_id=1, source_target_pairs={{0,8},{1,9},{2,10},{3,11},{4,12},{5,13},{6,14},{7,15},{8,0},{9,1},... | collective-permute-start | bytes 368648 | tf_op jit(solution)/shard_map/ppermute | solution.py:889
  308.4 8.4 %collective-permute-start.25 = (bf16[2,2,40,768]{3,2,1,0:T(8,128)(2,1)S(1)}, bf16[2,2,40,768]{3,2,1,0:T(8,128)(2,1)S(1)}, u32[]{:S(2)}, u32[]{:S(2)}) collective-permute-start(bf16[2,2,40,768]{3,2,1,0:T(8,128)(2,1)S(1)} %pad_maximum_fusion.9), channel_id=1, source_target_pairs={{0,2},{1,3},{2,0},{3,1},{4,6},{5,7},{6,4},{7,5},{8,10},{9,11},{10,... | collective-permute-start | bytes 737288 | tf_op jit(solution)/shard_map/ppermute | solution.py:889
  317.6 11.6 %collective-permute-start.26 = (bf16[2,2,2,40,768]{4,3,2,1,0:T(8,128)(2,1)}, bf16[2,2,2,40,768]{4,3,2,1,0:T(8,128)(2,1)}, u32[]{:S(2)}, u32[]{:S(2)}) collective-permute-start(bf16[2,2,2,40,768]{4,3,2,1,0:T(8,128)(2,1)} %pad_maximum_fusion.6), channel_id=1, source_target_pairs={{0,1},{1,0},{2,3},{3,2},{4,5},{5,4},{6,7},{7,6},{8,9},{9,8},{10,11... | collective-permute-start | bytes 1474568 | tf_op jit(solution)/shard_map/ppermute | solution.py:889
  (37 other events, 141.0 us)
Sparse Core Ops, SparseCore 0:
  10.9 88.7 all-gather.1
  141.8 136.5 reduce-scatter.1
